TPU v7x, 256 devices: a whole 4x4x8 slice. The times are simulated.
256 devices in a mesh: atom: 32 (over y, z_lo, core), refl: 8 (over z_hi, x).
Axes of the slice: x: 4, y: 4, z: 8 (z_hi: 2, z_lo: 4; z = z_hi * 4 + z_lo), core: 2. Of those that a mesh axis runs over, the one named last changes fastest.
Arguments:
- coords: float32 [3, 8192], P(None, 'atom'), may hold values from -0.5 to 0.5
- weights: float32 [8192], P('atom'), may hold values from 0.5 to 2
- thermal: float32 [8192], P('atom'), may hold values from 0.5 to 8
- angles: float32 [3, 4], replicated, may hold values from -3.140625 to 3.140625
- miller: int32 [3, 8, 4096], P(None, 'refl'), may hold values from -128 to 127, as said below
- observed: float32 [2, 8, 4096], P(None, 'refl', 'atom'), may hold values from -6 to 6
Outputs:
- tfun: float32 [4, 256, 256, 256], P(None, 'refl', 'atom')
Inputs may be any that keep to these rules, and one draw needn't show every extreme that they name: `miller`: reflection i of group g has h mod 256 in g * 32 to (g + 1) * 32 - 1 and k mod 256 in j * 8 to (j + 1) * 8 - 1 with j = i // 128; no two reflections have the same (h, k, l) mod 256.
All inputs are finite; a program needn't handle non-finite values.
Results may differ from a plain program's by a relative error of at most 0.0003.
Values sent between devices are 32-bit elements; how exact they have to be, the bound alone decides.
No kernel may reach another device: no remote copies, remote signals or barrier semaphores. Data moves between devices by JAX's collectives and lax.ppermute only.
A program may use at most 320 MiB of HBM per device.

v0:
```python
import math

import jax
import jax.numpy as jnp
from jax import lax
from jax.sharding import PartitionSpec as P

G = 256


TWO_PI = 2.0 * math.pi


def rotations(angle_batch):
    cos_first = jnp.cos(angle_batch[0])
    sin_first = jnp.sin(angle_batch[0])
    cos_tilt = jnp.cos(angle_batch[1])
    sin_tilt = jnp.sin(angle_batch[1])
    cos_last = jnp.cos(angle_batch[2])
    sin_last = jnp.sin(angle_batch[2])
    top_row = [
        cos_first * cos_tilt * cos_last - sin_first * sin_last,
        -cos_first * cos_tilt * sin_last - sin_first * cos_last,
        cos_first * sin_tilt,
    ]
    mid_row = [
        sin_first * cos_tilt * cos_last + cos_first * sin_last,
        -sin_first * cos_tilt * sin_last + cos_first * cos_last,
        sin_first * sin_tilt,
    ]
    low_row = [-sin_tilt * cos_last, sin_tilt * sin_last, cos_tilt]
    return jnp.stack([jnp.stack(top_row), jnp.stack(mid_row), jnp.stack(low_row)])


def structure_terms(matrices, coords, weights, thermal, indices, atom_scale):
    placed = jnp.einsum("ijb,ja->bia", matrices, coords, precision=lax.Precision.HIGHEST)
    index_float = indices.astype(jnp.float32)
    turns = jnp.einsum("bia,in->ban", placed, index_float, precision=lax.Precision.HIGHEST)
    resolution = jnp.sum(index_float * index_float, axis=0) / float(G * G)
    amplitude = weights[:, None] * jnp.exp(-thermal[:, None] * resolution[None, :])
    phase_angle = TWO_PI * turns
    real_part = jnp.sum(amplitude * jnp.cos(phase_angle), axis=1) * atom_scale
    imag_part = jnp.sum(amplitude * jnp.sin(phase_angle), axis=1) * atom_scale
    return jnp.stack([real_part, imag_part], axis=1)


def products(obs_part, fcalc, refl_scale):
    real_part = (obs_part[0] * fcalc[:, 0] + obs_part[1] * fcalc[:, 1]) * refl_scale
    imag_part = (obs_part[1] * fcalc[:, 0] - obs_part[0] * fcalc[:, 1]) * refl_scale
    return jnp.stack([real_part, imag_part], axis=1)


def phase_tables(length):
    positions = jnp.arange(length, dtype=jnp.int32)
    product = jnp.mod(positions[:, None] * positions[None, :], length)
    phase_angle = TWO_PI * product.astype(jnp.float32) / length
    return (jnp.cos(phase_angle), jnp.sin(phase_angle))


def spread_rows(coefficients, third_cells, row_index, columns, row_total):
    product = jnp.mod(third_cells[:, None] * columns[None, :], G)
    phase_angle = TWO_PI * product.astype(jnp.float32) / G
    cosine = jnp.cos(phase_angle)
    sine_part = jnp.sin(phase_angle)
    real_part = coefficients[:, 0, :, None]
    imag_part = coefficients[:, 1, :, None]
    spread = jnp.stack(
        [real_part * cosine - imag_part * sine_part, real_part * sine_part + imag_part * cosine],
        axis=1,
    )
    empty = jnp.zeros((coefficients.shape[0], 2, row_total, columns.shape[0]), jnp.float32)
    return empty.at[:, :, row_index].add(spread)


def direct_lines(coefficients, indices, first_planes, second_planes, group_index, member):
    cell_index = jnp.mod(indices, G)
    row_index = (cell_index[0] - group_index * first_planes) * second_planes + (
        cell_index[1] - member * second_planes
    )
    columns = jnp.arange(G, dtype=jnp.int32)
    filled = spread_rows(
        coefficients, cell_index[2], row_index, columns, first_planes * second_planes
    )
    return filled.reshape(coefficients.shape[0], 2, first_planes, second_planes, G)


def shards(coords, weights, thermal, angles, miller, observed):
    atom_count = lax.axis_size("atom")
    refl_count = lax.axis_size("refl")
    first_planes = G // refl_count
    second_planes = G // atom_count
    group_index = lax.axis_index("refl")
    member = lax.axis_index("atom")
    own_count = observed.shape[2]
    atom_scale = 1.0 / math.sqrt(coords.shape[1] * atom_count)
    refl_scale = 1.0 / math.sqrt(own_count * atom_count * refl_count)
    group_indices = miller[:, 0, :]
    own_indices = lax.dynamic_slice_in_dim(group_indices, member * own_count, own_count, 1)
    own_observed = observed[:, 0, :]
    cos_table, sin_table = phase_tables(G)

    def turn_second(pencils):
        real_part = pencils[:, 0]
        imag_part = pencils[:, 1]
        out_real = jnp.einsum(
            "kuvw,vx->kuxw", real_part, cos_table, precision=lax.Precision.HIGHEST
        ) - jnp.einsum("kuvw,vx->kuxw", imag_part, sin_table, precision=lax.Precision.HIGHEST)
        out_imag = jnp.einsum(
            "kuvw,vx->kuxw", real_part, sin_table, precision=lax.Precision.HIGHEST
        ) + jnp.einsum("kuvw,vx->kuxw", imag_part, cos_table, precision=lax.Precision.HIGHEST)
        return jnp.stack([out_real, out_imag], axis=1)

    def turn_first(pencils):
        real_part = pencils[:, 0]
        imag_part = pencils[:, 1]
        return jnp.einsum(
            "kuvw,ux->kvwx", real_part, cos_table, precision=lax.Precision.HIGHEST
        ) - jnp.einsum("kuvw,ux->kvwx", imag_part, sin_table, precision=lax.Precision.HIGHEST)

    def process(angle_batch):
        matrices = rotations(angle_batch)
        partial_value = structure_terms(
            matrices, coords, weights, thermal, group_indices, atom_scale
        )
        fcalc = lax.psum_scatter(partial_value, "atom", scatter_dimension=2, tiled=True)
        coefficients = products(own_observed, fcalc, refl_scale)
        grid_block = direct_lines(
            coefficients, own_indices, first_planes, second_planes, group_index, member
        )
        pencils = turn_second(
            lax.all_to_all(grid_block, "atom", split_axis=4, concat_axis=3, tiled=True)
        )
        return turn_first(lax.all_to_all(pencils, "refl", split_axis=3, concat_axis=2, tiled=True))

    results = lax.map(lambda single: process(single[:, None]), jnp.transpose(angles))
    return results[:, 0]


def solution(mesh):
    placed = (
        P(None, "atom"),
        P("atom"),
        P("atom"),
        P(),
        P(None, "refl", None),
        P(None, "refl", "atom"),
    )
    return jax.shard_map(
        shards, mesh=mesh, in_specs=placed, out_specs=P(None, "refl", "atom", None), check_vma=False
    )
```

profile of v0, /device:TPU:1, one launch (start us, length us, event | category | flops | bytes accessed | tf_op | source)
XLA Modules:
  0.0 1038.1 jit_solution(14397122609076840169)
XLA Ops:
  9.6 1022.0 %while.15 = (s32[]{:T(128)}, f32[4,1,32,8,256]{4,3,2,1,0:T(8,128)}, s32[3,128]{1,0:T(4,128)S(1)}, s32[3,128]{1,0:T(4,128)S(1)}, s32[]{:T(128)}, /*index=5*/s32[]...) while((s32[]{:T(128)}, f32[4,1,32,8,256]{4,3,2,1,0:T(8,128)}, ...), condition=%wide.region_6.7_spmd.clone.clone, body=%wide.region_1.6_spmd.clone.clone.sunk | while | flops 1259713280 | bytes 27494224 | solution.py:135
  16.3 21.1 %multiply_reduce_fusion.4 = (f32[4096]{0:T(1024)S(1)}, f32[4096]{0:T(1024)S(1)}) fusion(f32[4096]{0:T(1024)S(1)} %broadcast_multiply_fusion.6, f32[256]{0:T(256)S(1)} %bitcast.285, f32[256]{0:T(256)} %get-tuple-element.515, f32[3,256]{1,0:T(4,128)S(1)} %fusion.128, f32[3,4096]{1,0:T(4,128)S(1)} %get-tuple-element.520), kind=kOutput, calls=%fused_computation.5.clone.1 | convolution fusion | flops 45080576 | bytes 103424 | tf_op jit(solution)/shard_map/while/body/eval_jaxpr/bia,in->ban/dot_general | solution.py:38
  41.2 145.6 %reduce-scatter.6.cloned.1.call-done = f32[128,2]{1,0:T(8,128)} async-done(((f32[4096,2]{1,0:T(8,128)}), f32[128,2]{1,0:T(8,128)}) %reduce-scatter.6.cloned.1.call-update) | async-done | bytes 1040 | tf_op jit(solution)/shard_map/while
  189.1 5.2 scatter_fusion
  196.4 25.6 %all_to_all.82 = f32[32,1,4096]{2,1,0:T(1,128)S(1)} all-to-all(f32[32,1,4096]{2,1,0:T(1,128)S(1)} %reshape.504), channel_id=1, replica_groups=mesh['atom'=32,'refl'=8] {'atom'}, dimensions={0} | all-to-all | bytes 1048576 | tf_op jit(solution)/shard_map/while/body/eval_jaxpr/all_to_all | solution.py:131
  235.8 8.1 all-to-all-start.1
  244.0 15.0 %all-to-all-done.1 = f32[8,1,16384]{2,1,0:T(1,128)S(1)} async-done(((f32[8,1,16384]{2,1,0:T(1,128)}), f32[8,1,16384]{2,1,0:T(1,128)S(1)}, u32[]{:S(2)}, u32[]{:S(2)}) %all-to-all-start.1) | async-done | bytes 524320 | tf_op jit(solution)/shard_map/while/body/eval_jaxpr/all_to_all | solution.py:133
  277.0 21.1 %multiply_reduce_fusion.4 = (f32[4096]{0:T(1024)S(1)}, f32[4096]{0:T(1024)S(1)}) fusion(f32[4096]{0:T(1024)S(1)} %broadcast_multiply_fusion.6, f32[256]{0:T(256)S(1)} %bitcast.285, f32[256]{0:T(256)} %get-tuple-element.515, f32[3,256]{1,0:T(4,128)S(1)} %fusion.128, f32[3,4096]{1,0:T(4,128)S(1)} %get-tuple-element.520), kind=kOutput, calls=%fused_computation.5.clone.1 | convolution fusion | flops 45080576 | bytes 103424 | tf_op jit(solution)/shard_map/while/body/eval_jaxpr/bia,in->ban/dot_general | solution.py:38
  301.8 139.0 %reduce-scatter.6.cloned.1.call-done = f32[128,2]{1,0:T(8,128)} async-done(((f32[4096,2]{1,0:T(8,128)}), f32[128,2]{1,0:T(8,128)}) %reduce-scatter.6.cloned.1.call-update) | async-done | bytes 1040 | tf_op jit(solution)/shard_map/while
  443.1 5.2 scatter_fusion
  450.5 25.3 %all_to_all.82 = f32[32,1,4096]{2,1,0:T(1,128)S(1)} all-to-all(f32[32,1,4096]{2,1,0:T(1,128)S(1)} %reshape.504), channel_id=1, replica_groups=mesh['atom'=32,'refl'=8] {'atom'}, dimensions={0} | all-to-all | bytes 1048576 | tf_op jit(solution)/shard_map/while/body/eval_jaxpr/all_to_all | solution.py:131
  489.5 8.3 all-to-all-start.1
  497.9 15.0 %all-to-all-done.1 = f32[8,1,16384]{2,1,0:T(1,128)S(1)} async-done(((f32[8,1,16384]{2,1,0:T(1,128)}), f32[8,1,16384]{2,1,0:T(1,128)S(1)}, u32[]{:S(2)}, u32[]{:S(2)}) %all-to-all-start.1) | async-done | bytes 524320 | tf_op jit(solution)/shard_map/while/body/eval_jaxpr/all_to_all | solution.py:133
  530.9 21.1 %multiply_reduce_fusion.4 = (f32[4096]{0:T(1024)S(1)}, f32[4096]{0:T(1024)S(1)}) fusion(f32[4096]{0:T(1024)S(1)} %broadcast_multiply_fusion.6, f32[256]{0:T(256)S(1)} %bitcast.285, f32[256]{0:T(256)} %get-tuple-element.515, f32[3,256]{1,0:T(4,128)S(1)} %fusion.128, f32[3,4096]{1,0:T(4,128)S(1)} %get-tuple-element.520), kind=kOutput, calls=%fused_computation.5.clone.1 | convolution fusion | flops 45080576 | bytes 103424 | tf_op jit(solution)/shard_map/while/body/eval_jaxpr/bia,in->ban/dot_general | solution.py:38
  555.7 138.7 %reduce-scatter.6.cloned.1.call-done = f32[128,2]{1,0:T(8,128)} async-done(((f32[4096,2]{1,0:T(8,128)}), f32[128,2]{1,0:T(8,128)}) %reduce-scatter.6.cloned.1.call-update) | async-done | bytes 1040 | tf_op jit(solution)/shard_map/while
  704.1 25.5 %all_to_all.82 = f32[32,1,4096]{2,1,0:T(1,128)S(1)} all-to-all(f32[32,1,4096]{2,1,0:T(1,128)S(1)} %reshape.504), channel_id=1, replica_groups=mesh['atom'=32,'refl'=8] {'atom'}, dimensions={0} | all-to-all | bytes 1048576 | tf_op jit(solution)/shard_map/while/body/eval_jaxpr/all_to_all | solution.py:131
  743.4 8.5 all-to-all-start.1
  751.9 15.0 %all-to-all-done.1 = f32[8,1,16384]{2,1,0:T(1,128)S(1)} async-done(((f32[8,1,16384]{2,1,0:T(1,128)}), f32[8,1,16384]{2,1,0:T(1,128)S(1)}, u32[]{:S(2)}, u32[]{:S(2)}) %all-to-all-start.1) | async-done | bytes 524320 | tf_op jit(solution)/shard_map/while/body/eval_jaxpr/all_to_all | solution.py:133
  784.9 21.1 %multiply_reduce_fusion.4 = (f32[4096]{0:T(1024)S(1)}, f32[4096]{0:T(1024)S(1)}) fusion(f32[4096]{0:T(1024)S(1)} %broadcast_multiply_fusion.6, f32[256]{0:T(256)S(1)} %bitcast.285, f32[256]{0:T(256)} %get-tuple-element.515, f32[3,256]{1,0:T(4,128)S(1)} %fusion.128, f32[3,4096]{1,0:T(4,128)S(1)} %get-tuple-element.520), kind=kOutput, calls=%fused_computation.5.clone.1 | convolution fusion | flops 45080576 | bytes 103424 | tf_op jit(solution)/shard_map/while/body/eval_jaxpr/bia,in->ban/dot_general | solution.py:38
  809.8 138.8 %reduce-scatter.6.cloned.1.call-done = f32[128,2]{1,0:T(8,128)} async-done(((f32[4096,2]{1,0:T(8,128)}), f32[128,2]{1,0:T(8,128)}) %reduce-scatter.6.cloned.1.call-update) | async-done | bytes 1040 | tf_op jit(solution)/shard_map/while
  950.8 5.2 scatter_fusion
  958.2 25.3 %all_to_all.82 = f32[32,1,4096]{2,1,0:T(1,128)S(1)} all-to-all(f32[32,1,4096]{2,1,0:T(1,128)S(1)} %reshape.504), channel_id=1, replica_groups=mesh['atom'=32,'refl'=8] {'atom'}, dimensions={0} | all-to-all | bytes 1048576 | tf_op jit(solution)/shard_map/while/body/eval_jaxpr/all_to_all | solution.py:131
  997.3 8.0 all-to-all-start.1
  1005.3 15.0 %all-to-all-done.1 = f32[8,1,16384]{2,1,0:T(1,128)S(1)} async-done(((f32[8,1,16384]{2,1,0:T(1,128)}), f32[8,1,16384]{2,1,0:T(1,128)S(1)}, u32[]{:S(2)}, u32[]{:S(2)}) %all-to-all-start.1) | async-done | bytes 524320 | tf_op jit(solution)/shard_map/while/body/eval_jaxpr/all_to_all | solution.py:133
  (208 shorter events, 150.0 us)
Async XLA Ops:
  9.6 177.1 %reduce-scatter.6.cloned.1.call-start = ((), (), s32[]{:S(2)}) async-start(), calls=%async_computation.3 | async-start | bytes 2162688 | tf_op jit(solution)/shard_map/while
  37.5 150.6 %copy-start = (f32[2,128]{1,0:T(2,128)S(1)}, f32[2,128]{1,0:T(2,128)}, u32[]{:S(2)}) copy-start(f32[2,128]{1,0:T(2,128)} %get-tuple-element.514) | copy-start | bytes 3076 | tf_op jit(solution)/shard_map/while
  235.8 23.2 %all-to-all-start.1 = ((f32[8,1,16384]{2,1,0:T(1,128)}), f32[8,1,16384]{2,1,0:T(1,128)S(1)}, u32[]{:S(2)}, u32[]{:S(2)}) async-start(f32[8,1,16384]{2,1,0:T(1,128)} %reshape.506), calls=%async_computation.2 | async-start | bytes 1048576 | tf_op jit(solution)/shard_map/while/body/eval_jaxpr/all_to_all | solution.py:133
  270.3 170.5 %reduce-scatter.6.cloned.1.call-start = ((), (), s32[]{:S(2)}) async-start(), calls=%async_computation.3 | async-start | bytes 2162688 | tf_op jit(solution)/shard_map/while
  298.1 144.0 %copy-start = (f32[2,128]{1,0:T(2,128)S(1)}, f32[2,128]{1,0:T(2,128)}, u32[]{:S(2)}) copy-start(f32[2,128]{1,0:T(2,128)} %get-tuple-element.514) | copy-start | bytes 3076 | tf_op jit(solution)/shard_map/while
  489.5 23.3 %all-to-all-start.1 = ((f32[8,1,16384]{2,1,0:T(1,128)}), f32[8,1,16384]{2,1,0:T(1,128)S(1)}, u32[]{:S(2)}, u32[]{:S(2)}) async-start(f32[8,1,16384]{2,1,0:T(1,128)} %reshape.506), calls=%async_computation.2 | async-start | bytes 1048576 | tf_op jit(solution)/shard_map/while/body/eval_jaxpr/all_to_all | solution.py:133
  524.2 170.3 %reduce-scatter.6.cloned.1.call-start = ((), (), s32[]{:S(2)}) async-start(), calls=%async_computation.3 | async-start | bytes 2162688 | tf_op jit(solution)/shard_map/while
  552.0 143.7 %copy-start = (f32[2,128]{1,0:T(2,128)S(1)}, f32[2,128]{1,0:T(2,128)}, u32[]{:S(2)}) copy-start(f32[2,128]{1,0:T(2,128)} %get-tuple-element.514) | copy-start | bytes 3076 | tf_op jit(solution)/shard_map/while
  743.4 23.5 %all-to-all-start.1 = ((f32[8,1,16384]{2,1,0:T(1,128)}), f32[8,1,16384]{2,1,0:T(1,128)S(1)}, u32[]{:S(2)}, u32[]{:S(2)}) async-start(f32[8,1,16384]{2,1,0:T(1,128)} %reshape.506), calls=%async_computation.2 | async-start | bytes 1048576 | tf_op jit(solution)/shard_map/while/body/eval_jaxpr/all_to_all | solution.py:133
  778.2 170.3 %reduce-scatter.6.cloned.1.call-start = ((), (), s32[]{:S(2)}) async-start(), calls=%async_computation.3 | async-start | bytes 2162688 | tf_op jit(solution)/shard_map/while
  806.1 143.7 %copy-start = (f32[2,128]{1,0:T(2,128)S(1)}, f32[2,128]{1,0:T(2,128)}, u32[]{:S(2)}) copy-start(f32[2,128]{1,0:T(2,128)} %get-tuple-element.514) | copy-start | bytes 3076 | tf_op jit(solution)/shard_map/while
  997.3 23.1 %all-to-all-start.1 = ((f32[8,1,16384]{2,1,0:T(1,128)}), f32[8,1,16384]{2,1,0:T(1,128)S(1)}, u32[]{:S(2)}, u32[]{:S(2)}) async-start(f32[8,1,16384]{2,1,0:T(1,128)} %reshape.506), calls=%async_computation.2 | async-start | bytes 1048576 | tf_op jit(solution)/shard_map/while/body/eval_jaxpr/all_to_all | solution.py:133
Sparse Core Ops, SparseCore 0:
  41.3 145.4 reduce-scatter.5
  301.9 138.8 reduce-scatter.5
  555.8 138.5 reduce-scatter.5
  809.9 138.6 reduce-scatter.5
where the time goes:
time: 1040 us
  waiting for transfers between devices  622 us (60%)
  matrix products  123 us (12%)
  blocking collectives  102 us (10%)
  local copies, waits for them, and re-layouts  84.5 us (8%)
  other arithmetic  42.2 us (4%)
  starting transfers between devices  33 us (3%)
  loops' own time  18.5 us (2%)
  between operations  13.1 us (1%)
    while x8, waiting for transfers between devices  562 us
    all_to_all x4, blocking collectives, process(): lax.all_to_all(grid_block, 'atom', split_axis=4, concat_axis=3, tiled=True)  102 us
    dot_general x4, matrix products, structure_terms(): jnp.einsum('bia,in->ban', placed, index_float, precision=lax.Precision.HI...  84.3 us
    all_to_all x4, waiting for transfers between devices, process(): lax.all_to_all(pencils, 'refl', split_axis=3, concat_axis=2, tiled=True)  60.1 us
    while x44, local copies, waits for them, and re-layouts  34.2 us
    all_to_all x4, starting transfers between devices, process(): lax.all_to_all(pencils, 'refl', split_axis=3, concat_axis=2, tiled=True)  33 us
    all_to_all x12, local copies, waits for them, and re-layouts, process(): lax.all_to_all(pencils, 'refl', split_axis=3, concat_axis=2, tiled=True)  21 us
  transfers between devices with their start and end apart: 8, of which 8 were waited for; matrix products, arithmetic and copies ran while one was open for 0% of the time, Pallas kernels for 0%

commit v1 on v0

v1 whole, which is shorter than its diff:
```python
import functools
import math

import jax
import jax.numpy as jnp
import numpy as np
from jax import lax
from jax.experimental import pallas as pl
from jax.experimental.pallas import tpu as pltpu
from jax.sharding import PartitionSpec as P

G = 256
TILE = 256
LOG2E = math.log2(math.e)

SIN_C = (3.141592640183972, -5.167710090328514, 2.550077659663962, -0.5982921590533228, 0.07765940739590604)
COS_C = (0.9999999534665512, -4.934792858660287, 4.058411913867176, -1.3318801593277205, 0.21969679475921783)


def rotations(angle_batch):
    cos_first = jnp.cos(angle_batch[0])
    sin_first = jnp.sin(angle_batch[0])
    cos_tilt = jnp.cos(angle_batch[1])
    sin_tilt = jnp.sin(angle_batch[1])
    cos_last = jnp.cos(angle_batch[2])
    sin_last = jnp.sin(angle_batch[2])
    top_row = [
        cos_first * cos_tilt * cos_last - sin_first * sin_last,
        -cos_first * cos_tilt * sin_last - sin_first * cos_last,
        cos_first * sin_tilt,
    ]
    mid_row = [
        sin_first * cos_tilt * cos_last + cos_first * sin_last,
        -sin_first * cos_tilt * sin_last + cos_first * cos_last,
        sin_first * sin_tilt,
    ]
    low_row = [-sin_tilt * cos_last, sin_tilt * sin_last, cos_tilt]
    return jnp.stack([jnp.stack(top_row), jnp.stack(mid_row), jnp.stack(low_row)])


def monic(coefs):
    lead = coefs[-1]
    return lead, [c / lead for c in coefs[:-1]]


def horner_monic(u, rest):
    total = u + rest[-1]
    for c in rest[-2::-1]:
        total = total * u + c
    return total


def half_angle(t):
    t = t - jnp.round(t)
    u = t * t
    return t * horner_monic(u, SIN_M), horner_monic(u, COS_M)


SIN_K, SIN_M = monic(SIN_C)
COS_K, COS_M = monic(COS_C)


def sincos_turns(t):
    s, c = half_angle(t)
    return (2.0 * SIN_K * COS_K) * (s * c), 1.0 - (2.0 * SIN_K * SIN_K) * (s * s)


def split2(x):
    hi = x.astype(jnp.bfloat16)
    lo = (x - hi.astype(jnp.float32)).astype(jnp.bfloat16)
    return hi, lo


def phase_kernel(n_in, first, last, scales, *refs):
    lhs_ref, s2_ref, rc_ref = refs[:3]
    atom_refs = refs[3 : 3 + n_in]
    pos = 3 + n_in
    if not first:
        acc_in = refs[pos]
        pos += 1
    if last:
        obs_ref = refs[pos]
        pos += 1
    out_ref = refs[pos]
    pos += 1
    if last:
        acc_ref = refs[pos]
        pos += 1
    else:
        acc_ref = out_ref
    turns_ref = refs[pos]

    if first:
        acc_ref[...] = jnp.zeros_like(acc_ref)
    else:
        acc_ref[...] = acc_in[...]

    rc0, rc1, rc2 = rc_ref[:, 0:1], rc_ref[:, 1:2], rc_ref[:, 2:3]
    lhs = lhs_ref[...]

    for a_ref in atom_refs:

        @pl.loop(0, a_ref.shape[1] // TILE)
        def _(i):
            a = a_ref[:, pl.ds(pl.multiple_of(i * TILE, TILE), TILE)]
            placed = rc0 * a[0:1] + rc1 * a[1:2] + rc2 * a[2:3]
            p1 = placed.astype(jnp.bfloat16)
            rest = placed - p1.astype(jnp.float32)
            p2 = rest.astype(jnp.bfloat16)
            p3 = (rest - p2.astype(jnp.float32)).astype(jnp.bfloat16)
            rhs = jnp.concatenate([p1, p2, p3], axis=0)
            turns_ref[...] = jnp.dot(lhs, rhs, preferred_element_type=jnp.float32)
            for nb in range(16):
                rows = slice(nb * 8, nb * 8 + 8)
                s2 = s2_ref[rows, :]
                amps = []
                for half in range(2):
                    lanes = slice(half * 128, half * 128 + 128)
                    amps.append(a[3:4, lanes] * jnp.exp2(a[4:5, lanes] * s2))
                acc_ref[8, rows, :] += amps[0] + amps[1]
                for r in range(4):
                    ms = mc = None
                    for half in range(2):
                        lanes = slice(half * 128, half * 128 + 128)
                        s, c = half_angle(turns_ref[r * 128 + nb * 8 : r * 128 + nb * 8 + 8, lanes])
                        m = amps[half] * s
                        ms = m * s if ms is None else ms + m * s
                        mc = m * c if mc is None else mc + m * c
                    acc_ref[r, rows, :] += ms
                    acc_ref[4 + r, rows, :] += mc

    if last:
        atom_scale, refl_scale = scales
        sums = [jnp.sum(acc_ref[q].T, axis=0, keepdims=True) for q in range(9)]
        obs0, obs1 = obs_ref[0:1, :], obs_ref[1:2, :]
        reals, imags = [], []
        for r in range(4):
            f_re = (sums[8] - (2.0 * SIN_K * SIN_K) * sums[r]) * atom_scale
            f_im = ((2.0 * SIN_K * COS_K) * sums[4 + r]) * atom_scale
            reals.append((obs0 * f_re + obs1 * f_im) * refl_scale)
            imags.append((obs1 * f_re - obs0 * f_im) * refl_scale)
        out_ref[...] = jnp.concatenate(reals + imags, axis=0)


def phase_call(lhs, s2, rc, atoms, acc, obs, scales):
    first, last = acc is None, obs is not None
    operands = [lhs, s2, rc, *atoms] + ([] if first else [acc]) + ([obs] if last else [])
    acc_shape = (9, 128, 128)
    scratch = [pltpu.VMEM((512, TILE), jnp.float32)]
    if last:
        scratch = [pltpu.VMEM(acc_shape, jnp.float32)] + scratch
    out = jax.ShapeDtypeStruct((8, 128) if last else acc_shape, jnp.float32)
    count = sum(a.shape[1] for a in atoms)
    return pl.pallas_call(
        functools.partial(phase_kernel, len(atoms), first, last, scales),
        out_shape=out,
        in_specs=[pl.BlockSpec(memory_space=pltpu.VMEM)] * len(operands),
        out_specs=pl.BlockSpec(memory_space=pltpu.VMEM),
        scratch_shapes=scratch,
        compiler_params=pltpu.CompilerParams(vmem_limit_bytes=16 << 20),
        cost_estimate=pl.CostEstimate(
            flops=count * 512 * 22, bytes_accessed=1 << 20, transcendentals=count * 128
        ),
        name="phases",
    )(*operands)


def block_id(core, y, x, z_lo, z_hi):
    return (((core * 4 + y) * 4 + x) * 4 + z_lo) * 2 + z_hi


def transform_kernel(own_ref, c_ref, m_ref, tt_ref, d_ref, out_ref, x_ref, z_ref):
    own = own_ref[0]
    own_j = own_ref[1]
    own_g = own_ref[2]
    cells = lax.broadcasted_iota(jnp.int32, (128, 128), 0)
    w_index = lax.broadcasted_iota(jnp.int32, (8, 128), 0) + own_j * 8

    def scatter(b):
        where = own ^ b
        z_hi = where & 1
        z_lo = (where >> 1) & 3
        x = (where >> 3) & 3
        y = (where >> 5) & 3
        core = (where >> 7) & 1
        g = z_hi * 4 + x
        j = (y * 4 + z_lo) * 2 + core
        m = m_ref[b]
        h = (m[0:1] & 255) - g * 32
        k = (m[1:2] & 255) - j * 8
        row = (h >> 1) * 8 + k
        odd = (h & 1).astype(jnp.float32)
        one_hot = jnp.where(cells == row, 1.0, 0.0).astype(jnp.bfloat16)
        product = (m[2:3] * w_index) & 255
        sine, cosine = sincos_turns(product.astype(jnp.float32) * (1.0 / G))
        c = c_ref[b]
        reals, imags = [], []
        for r in range(4):
            re, im = c[r : r + 1], c[4 + r : 5 + r]
            reals.append(re * cosine - im * sine)
            imags.append(re * sine + im * cosine)
        real, imag = jnp.concatenate(reals, axis=0), jnp.concatenate(imags, axis=0)
        value = jnp.concatenate(
            [real * (1.0 - odd), real * odd, imag * (1.0 - odd), imag * odd], axis=0
        )
        rows = jnp.concatenate(split2(value), axis=0)
        both = lax.dot_general(
            one_hot, rows, (((1,), (1,)), ((), ())), preferred_element_type=jnp.float32
        )
        total = both[:, :128] + both[:, 128:]
        x_ref[pl.ds(g * 16, 16), pl.ds(pl.multiple_of(j * 8, 8), 8), :] = total.reshape(16, 8, 128)

    @pl.loop(0, c_ref.shape[0] // 2)
    def _(i):
        scatter(2 * i)
        scatter(2 * i + 1)

    table = jnp.concatenate(
        [tt_ref[q, pl.ds(pl.multiple_of(own_g * 32, 32), 32), :] for q in range(4)], axis=0
    )
    lane = lax.broadcasted_iota(jnp.int32, (32, 128), 1)
    sign = jnp.where(lane < 64, -1.0, 1.0)

    @pl.loop(0, 64)
    def _(i):
        block = jnp.concatenate([x_ref[2 * i], x_ref[2 * i + 1]], axis=1)
        hi, lo = split2(block)
        o1 = jnp.dot(table, hi, preferred_element_type=jnp.float32)
        o2 = jnp.dot(table[:64], lo, preferred_element_type=jnp.float32)
        z = o1[:64] + o1[64:] + o2
        for half in range(2):
            lanes = slice(half * 128, half * 128 + 128)
            combined = z[:32, lanes] + sign * pltpu.roll(z[32:, lanes], 64, 1)
            z_ref[pl.ds(2 * i + half, 32, stride=128), :] = combined

    @pl.loop(0, 4)
    def _(i):
        parts = []
        for q in range(8):
            zv = z_ref[pl.ds(pl.multiple_of((i * 8 + q) * 128, 128), 128), :].T
            parts.append(
                jnp.concatenate([zv[0:32], zv[32:64], zv[64:96], zv[96:128]], axis=1)
            )
        hi, lo = split2(jnp.concatenate(parts, axis=0))
        d_hi, d_lo = d_ref[0], d_ref[1]
        field = (
            jnp.dot(hi, d_hi, preferred_element_type=jnp.float32)
            + jnp.dot(lo, d_hi, preferred_element_type=jnp.float32)
            + jnp.dot(hi, d_lo, preferred_element_type=jnp.float32)
        )
        for q in range(8):
            for r in range(4):
                out_ref[r, i * 8 + q] = field[q * 32 + r * 8 : q * 32 + r * 8 + 8, :]


def split_np(x):
    hi = x.astype(np.float32).astype(jnp.bfloat16)
    lo = (x - hi.astype(np.float64)).astype(np.float32).astype(jnp.bfloat16)
    return hi, lo


def tables():
    index = np.arange(G)
    angle = 2.0 * np.pi * ((index[:, None] * index[None, :]) % G) / G
    cos_hi, cos_lo = split_np(np.cos(angle))
    sin_hi, sin_lo = split_np(np.sin(angle))
    second = np.stack([cos_hi, sin_hi, cos_lo, sin_lo])
    order = np.concatenate([np.arange(0, G, 2), np.arange(1, G, 2)])
    first = np.stack(
        [
            np.concatenate([cos_hi[order], -sin_hi[order]]),
            np.concatenate([cos_lo[order], -sin_lo[order]]),
        ]
    )
    return second, first


def transform_call(own, coefs, miller, second, first):
    vmem = pl.BlockSpec(memory_space=pltpu.VMEM)
    return pl.pallas_call(
        transform_kernel,
        out_shape=jax.ShapeDtypeStruct((4, 32, 8, G), jnp.float32),
        in_specs=[pl.BlockSpec(memory_space=pltpu.SMEM)] + [vmem] * 4,
        out_specs=vmem,
        scratch_shapes=[
            pltpu.VMEM((128, G, 128), jnp.float32),
            pltpu.VMEM((32 * 128, 128), jnp.float32),
        ],
        compiler_params=pltpu.CompilerParams(vmem_limit_bytes=40 << 20),
        name="transform",
    )(own, coefs, miller, second, first)


def swap(x, axis, mask):
    count = lax.axis_size(axis)
    return lax.ppermute(x, axis, [(i, i ^ mask) for i in range(count)])


def spread(x, axis, masks, dim=0):
    return jnp.concatenate([x] + [swap(x, axis, mask) for mask in masks], axis=dim)


def spread_all(x):
    x = spread(x, "refl", (4,))
    x = spread(x, "atom", (2, 4, 6))
    x = spread(x, "refl", (1, 2, 3))
    x = spread(x, "atom", (8, 16, 24))
    return spread(x, "atom", (1,))


def shards(coords, weights, thermal, angles, miller, observed):
    atom_count = lax.axis_size("atom")
    refl_count = lax.axis_size("refl")
    g = lax.axis_index("refl")
    j = lax.axis_index("atom")
    own_count = observed.shape[2]
    scales = (
        1.0 / math.sqrt(coords.shape[1] * atom_count),
        1.0 / math.sqrt(own_count * atom_count * refl_count),
    )
    atoms = jnp.concatenate([coords, weights[None], thermal[None], jnp.zeros_like(coords)], axis=0)
    atoms = spread(atoms, "atom", (1,), 1)
    atoms = spread(atoms, "atom", (2, 4, 6), 1)
    others = [swap(atoms, "atom", mask) for mask in (8, 16, 24)]

    own_miller = lax.dynamic_slice_in_dim(miller[:, 0, :], j * own_count, own_count, 1)
    indices = own_miller.astype(jnp.float32)
    resolution = jnp.sum(indices * indices, axis=0) * (-LOG2E / (G * G))
    s2 = jnp.broadcast_to(resolution[:, None], (own_count, 128))
    lhs = indices.T[None, :, :, None] * jnp.eye(4, dtype=jnp.float32)[:, None, None, :]
    lhs = jnp.pad(lhs.reshape(4 * own_count, 12), ((0, 0), (0, 4)))
    lhs = jnp.concatenate([lhs, lhs, lhs], axis=1).astype(jnp.bfloat16)
    matrices = rotations(angles)
    rc = jnp.transpose(matrices, (0, 2, 1)).reshape(12, 3)
    rc = jnp.pad(rc, ((0, 4), (0, 125)))

    all_miller = spread_all(own_miller[None])
    acc = phase_call(lhs, s2, rc, [atoms], None, None, scales)
    coefs = phase_call(lhs, s2, rc, others, acc, observed[:, 0, :], scales)
    coefs = spread_all(coefs[None])

    z_hi, x = g // 4, g % 4
    y, z_lo, core = j // 8, (j // 2) % 4, j % 2
    own = jnp.stack([block_id(core, y, x, z_lo, z_hi), j, g]).astype(jnp.int32)
    second, first = tables()
    return transform_call(own, coefs, all_miller, second, first)


def solution(mesh):
    placed = (
        P(None, "atom"),
        P("atom"),
        P("atom"),
        P(),
        P(None, "refl", None),
        P(None, "refl", "atom"),
    )
    return jax.shard_map(
        shards, mesh=mesh, in_specs=placed, out_specs=P(None, "refl", "atom", None), check_vma=False
    )
```

time: 1040 us -> 153 us (0.15)
  waiting for transfers between devices: 622 us -> 20 us
  matrix products: 123 us -> 0 us
  blocking collectives: 102 us -> 0 us
  local copies, waits for them, and re-layouts: 84.5 us -> 3.86 us
  Pallas kernels: 0 us -> 70 us
  other arithmetic: 42.2 us -> 1.03 us
  starting transfers between devices: 33 us -> 57.2 us
  loops' own time: 18.5 us -> 0 us
  between operations: 13.1 us -> 0.34 us
    while x8 -> x0, waiting for transfers between devices: 562 us -> none
    dot_general x32 -> x0, matrix products: 123 us -> none  [the longest x4 84.3 us: structure_terms(): jnp.einsum('bia,in->ban', placed, index_float, precision=lax.Precision.HI...]
    all_to_all x4 -> x0, blocking collectives: 102 us -> none  [process(): lax.all_to_all(grid_block, 'atom', split_axis=4, concat_axis=3, tiled=True)]
    pallas_call x0 -> x3, Pallas kernels: none -> 70 us  [the longest x1 50.1 us: transform_call(): pl.pallas_call(transform_kernel, out_shape=jax.ShapeDtypeStruct((4, 32, 8...]
    all_to_all x4 -> x0, waiting for transfers between devices: 60.1 us -> none  [process(): lax.all_to_all(pencils, 'refl', split_axis=3, concat_axis=2, tiled=True)]
    ppermute x0 -> x29, starting transfers between devices: none -> 57.2 us  [swap(): return lax.ppermute(x, axis, [(i, i ^ mask) for i in range(count)])]
    while x44 -> x0, local copies, waits for them, and re-layouts: 34.2 us -> none
    all_to_all x4 -> x0, starting transfers between devices: 33 us -> none  [process(): lax.all_to_all(pencils, 'refl', split_axis=3, concat_axis=2, tiled=True)]
  transfers between devices with their start and end apart: 8 -> 29, of which waited for: 8 -> 12; matrix products, arithmetic and copies ran while one was open for 0% -> 1% of each run, Pallas kernels for 0% -> 13%
where the time goes in v1:
time: 153 us; the launch traced here: 152 us
  Pallas kernels  70 us (46%)
  starting transfers between devices  57.2 us (37%)
  waiting for transfers between devices  20 us (13%)
  local copies, waits for them, and re-layouts  3.86 us (3%)
    ppermute x29, starting transfers between devices, swap(): return lax.ppermute(x, axis, [(i, i ^ mask) for i in range(count)])  57.2 us
    pallas_call x1, Pallas kernels, transform_call(): pl.pallas_call(transform_kernel, out_shape=jax.ShapeDtypeStruct((4, 32, 8...  50.1 us
    ppermute x29, waiting for transfers between devices, swap(): return lax.ppermute(x, axis, [(i, i ^ mask) for i in range(count)])  20 us
    pallas_call x2, Pallas kernels, phase_call(): pl.pallas_call(functools.partial(phase_kernel, len(atoms), first, last, s...  19.9 us
    unnamed x40, local copies, waits for them, and re-layouts  3.39 us
  transfers between devices with their start and end apart: 29, of which 12 were waited for; matrix products, arithmetic and copies ran while one was open for 1% of the time, Pallas kernels for 13%

profile of v1, /device:TPU:1, one launch (start us, length us, event | category | flops | bytes accessed | tf_op | source)
XLA Modules:
  0.0 152.5 jit_solution(4746907853252420683)
XLA Ops:
  0.7 3.3 %collective-permute-start = (f32[8,256]{1,0:T(8,128)S(1)}, f32[8,256]{1,0:T(8,128)S(1)}, u32[]{:S(2)}, u32[]{:S(2)}) collective-permute-start(f32[8,256]{1,0:T(8,128)S(1)} %get-tuple-element.37), channel_id=1, source_target_pairs={{0,8},{8,0},{16,24},{24,16},{32,40},{40,32},{48,56},{56,48},{64,72... | collective-permute-start | bytes 24584 | tf_op jit(solution)/shard_map/ppermute | solution.py:296
  4.7 5.2 %collective-permute-start.18 = (s32[1,3,128]{2,1,0:T(4,128)S(1)}, s32[1,3,128]{2,1,0:T(4,128)S(1)}, u32[]{:S(2)}, u32[]{:S(2)}) collective-permute-start(s32[1,3,128]{2,1,0:T(4,128)S(1)} %get-tuple-element.89), channel_id=1, source_target_pairs={{0,4},{1,5},{2,6},{3,7},{4,0},{5,1},{6,2},{7,3},{8,12},{9,13},{10,... | collective-permute-start | bytes 4616 | tf_op jit(solution)/shard_map/ppermute | solution.py:296
  12.0 2.3 %collective-permute-start.20 = (s32[2,3,128]{2,1,0:T(4,128)S(1)}, s32[2,3,128]{2,1,0:T(4,128)S(1)}, u32[]{:S(2)}, u32[]{:S(2)}) collective-permute-start(s32[2,3,128]{2,1,0:T(4,128)S(1)} %get-tuple-element.75), channel_id=1, source_target_pairs={{0,32},{8,40},{16,48},{24,56},{32,0},{40,8},{48,16},{56,24},{64,96... | collective-permute-start | bytes 9224 | tf_op jit(solution)/shard_map/ppermute | solution.py:296
  15.5 3.1 %collective-permute-done.21 = s32[2,3,128]{2,1,0:T(4,128)S(1)} collective-permute-done((s32[2,3,128]{2,1,0:T(4,128)S(1)}, s32[2,3,128]{2,1,0:T(4,128)S(1)}, u32[]{:S(2)}, u32[]{:S(2)}) %collective-permute-start.21) | collective-permute-done | bytes 3104 | tf_op jit(solution)/shard_map/ppermute | solution.py:296
  19.8 2.5 %collective-permute-start.23 = (s32[8,3,128]{2,1,0:T(4,128)S(1)}, s32[8,3,128]{2,1,0:T(4,128)S(1)}, u32[]{:S(2)}, u32[]{:S(2)}) collective-permute-start(s32[8,3,128]{2,1,0:T(4,128)S(1)} %get-tuple-element.54), channel_id=1, source_target_pairs={{0,2},{1,3},{2,0},{3,1},{4,6},{5,7},{6,4},{7,5},{8,10},{9,11},{10,... | collective-permute-start | bytes 36872 | tf_op jit(solution)/shard_map/ppermute | solution.py:296
  23.5 2.6 %collective-permute-start.3 = (f32[8,512]{1,0:T(8,128)S(1)}, f32[8,512]{1,0:T(8,128)S(1)}, u32[]{:S(2)}, u32[]{:S(2)}) collective-permute-start(f32[8,512]{1,0:T(8,128)S(1)} %pad_maximum_fusion.1), channel_id=1, source_target_pairs={{0,48},{8,56},{16,32},{24,40},{32,16},{40,24},{48,0},{56,8},{64,11... | collective-permute-start | bytes 49160 | tf_op jit(solution)/shard_map/ppermute | solution.py:296
  26.2 1.7 %collective-permute-done.3 = f32[8,512]{1,0:T(8,128)S(1)} collective-permute-done((f32[8,512]{1,0:T(8,128)S(1)}, f32[8,512]{1,0:T(8,128)S(1)}, u32[]{:S(2)}, u32[]{:S(2)}) %collective-permute-start.3) | collective-permute-done | bytes 16416 | tf_op jit(solution)/shard_map/ppermute | solution.py:296
  27.9 1.3 collective-permute-start.4
  29.2 2.6 %collective-permute-start.5 = (f32[8,2048]{1,0:T(8,128)S(1)}, f32[8,2048]{1,0:T(8,128)S(1)}, u32[]{:S(2)}, u32[]{:S(2)}) collective-permute-start(f32[8,2048]{1,0:T(8,128)S(1)} %constant_dynamic-update-slice_fusion.refs_3_), channel_id=1, source_target_pairs={{0,128},{8,136},{16,144},{24,152},{32,160},{40,168},{48,176},{56,1... | collective-permute-start | bytes 196616 | tf_op jit(solution)/shard_map/ppermute | solution.py:296
  31.9 4.9 %phases.2.refs_6_ = f32[9,128,128]{2,1,0:T(8,128)S(1)} custom-call(bf16[512,48]{1,0:T(8,128)(2,1)S(1)} %copy.24.refs_0_, f32[128,128]{1,0:T(8,128)S(1)} %broadcast_in_dim.23.refs_1_, f32[16,128]{1,0:T(8,128)S(1)} %pad.9.refs_2_, f32[8,2048]{1,0:T(8,128)S(1)} %constant_dynamic-update-slice_fusion.refs_3_), custom_call_target="tpu_custom_call" | custom-call | flops 23068672 | bytes 1048576 | tf_op jit(solution)/shard_map/phases/pallas_call | solution.py:154
  37.5 14.9 %phases.3 = f32[8,128]{1,0:T(8,128)S(1)} custom-call(bf16[512,48]{1,0:T(8,128)(2,1)S(1)} %copy.24.refs_0_, f32[128,128]{1,0:T(8,128)S(1)} %broadcast_in_dim.23.refs_1_, f32[16,128]{1,0:T(8,128)S(1)} %pad.9.refs_2_, f32[8,2048]{1,0:T(8,128)S(1)} %collective-permute-done.4.refs_3_, f32[8,2048]{1,0:T(8,128)S(1)} %collective-permute-done.5.refs_4_, ...), custom_call_target="tpu_custom_call" | custom-call | flops 69206016 | bytes 1048576 | tf_op jit(solution)/shard_map/phases/pallas_call | solution.py:154
  52.4 5.3 %collective-permute-start.7 = (f32[1,8,128]{2,1,0:T(8,128)S(1)}, f32[1,8,128]{2,1,0:T(8,128)S(1)}, u32[]{:S(2)}, u32[]{:S(2)}) collective-permute-start(f32[1,8,128]{2,1,0:T(8,128)S(1)} %bitcast.37), channel_id=1, source_target_pairs={{0,4},{1,5},{2,6},{3,7},{4,0},{5,1},{6,2},{7,3},{8,12},{9,13},{10,... | collective-permute-start | bytes 12296 | tf_op jit(solution)/shard_map/ppermute | solution.py:296
  58.9 2.9 %collective-permute-start.9 = (f32[2,8,128]{2,1,0:T(8,128)S(1)}, f32[2,8,128]{2,1,0:T(8,128)S(1)}, u32[]{:S(2)}, u32[]{:S(2)}) collective-permute-start(f32[2,8,128]{2,1,0:T(8,128)S(1)} %pad_maximum_fusion.3), channel_id=1, source_target_pairs={{0,32},{8,40},{16,48},{24,56},{32,0},{40,8},{48,16},{56,24},{64,96... | collective-permute-start | bytes 24584 | tf_op jit(solution)/shard_map/ppermute | solution.py:296
  62.8 3.3 %collective-permute-done.10 = f32[2,8,128]{2,1,0:T(8,128)S(1)} collective-permute-done((f32[2,8,128]{2,1,0:T(8,128)S(1)}, f32[2,8,128]{2,1,0:T(8,128)S(1)}, u32[]{:S(2)}, u32[]{:S(2)}) %collective-permute-start.10) | collective-permute-done | bytes 8224 | tf_op jit(solution)/shard_map/ppermute | solution.py:296
  66.2 3.7 %collective-permute-start.12 = (f32[8,8,128]{2,1,0:T(8,128)S(1)}, f32[8,8,128]{2,1,0:T(8,128)S(1)}, u32[]{:S(2)}, u32[]{:S(2)}) collective-permute-start(f32[8,8,128]{2,1,0:T(8,128)S(1)} %get-tuple-element.42), channel_id=1, source_target_pairs={{0,2},{1,3},{2,0},{3,1},{4,6},{5,7},{6,4},{7,5},{8,10},{9,11},{10,... | collective-permute-start | bytes 98312 | tf_op jit(solution)/shard_map/ppermute | solution.py:296
  71.4 2.5 %collective-permute-done.13 = f32[8,8,128]{2,1,0:T(8,128)S(1)} collective-permute-done((f32[8,8,128]{2,1,0:T(8,128)S(1)}, f32[8,8,128]{2,1,0:T(8,128)S(1)}, u32[]{:S(2)}, u32[]{:S(2)}) %collective-permute-start.13) | collective-permute-done | bytes 32800 | tf_op jit(solution)/shard_map/ppermute | solution.py:296
  74.0 1.5 collective-permute-start.14
  75.4 2.5 %collective-permute-start.26 = (s32[32,3,128]{2,1,0:T(4,128)S(1)}, s32[32,3,128]{2,1,0:T(4,128)S(1)}, u32[]{:S(2)}, u32[]{:S(2)}) collective-permute-start(s32[32,3,128]{2,1,0:T(4,128)S(1)} %get-tuple-element.30), channel_id=1, source_target_pairs={{0,128},{8,136},{16,144},{24,152},{32,160},{40,168},{48,176},{56,1... | collective-permute-start | bytes 147464 | tf_op jit(solution)/shard_map/ppermute | solution.py:296
  78.1 2.4 %collective-permute-start.15 = (f32[32,8,128]{2,1,0:T(8,128)S(1)}, f32[32,8,128]{2,1,0:T(8,128)S(1)}, u32[]{:S(2)}, u32[]{:S(2)}) collective-permute-start(f32[32,8,128]{2,1,0:T(8,128)S(1)} %get-tuple-element.21), channel_id=1, source_target_pairs={{0,128},{8,136},{16,144},{24,152},{32,160},{40,168},{48,176},{56,1... | collective-permute-start | bytes 393224 | tf_op jit(solution)/shard_map/ppermute | solution.py:296
  81.2 2.3 %collective-permute-done.15 = f32[32,8,128]{2,1,0:T(8,128)S(1)} collective-permute-done((f32[32,8,128]{2,1,0:T(8,128)S(1)}, f32[32,8,128]{2,1,0:T(8,128)S(1)}, u32[]{:S(2)}, u32[]{:S(2)}) %collective-permute-start.15) | collective-permute-done | bytes 131104 | tf_op jit(solution)/shard_map/ppermute | solution.py:296
  83.5 2.1 %collective-permute-done.16 = f32[32,8,128]{2,1,0:T(8,128)S(1)} collective-permute-done((f32[32,8,128]{2,1,0:T(8,128)S(1)}, f32[32,8,128]{2,1,0:T(8,128)S(1)}, u32[]{:S(2)}, u32[]{:S(2)}) %collective-permute-start.16) | collective-permute-done | bytes 131104 | tf_op jit(solution)/shard_map/ppermute | solution.py:296
  85.6 13.5 %collective-permute-start.17 = (f32[128,8,128]{2,1,0:T(8,128)S(1)}, f32[128,8,128]{2,1,0:T(8,128)S(1)}, u32[]{:S(2)}, u32[]{:S(2)}) collective-permute-start(f32[128,8,128]{2,1,0:T(8,128)S(1)} %get-tuple-element.5), channel_id=1, source_target_pairs={{0,8},{8,0},{16,24},{24,16},{32,40},{40,32},{48,56},{56,48},{64,72... | collective-permute-start | bytes 1572872 | tf_op jit(solution)/shard_map/ppermute | solution.py:296
  99.5 1.6 %collective-permute-done.28 = s32[128,3,128]{2,1,0:T(4,128)S(1)} collective-permute-done((s32[128,3,128]{2,1,0:T(4,128)S(1)}, s32[128,3,128]{2,1,0:T(4,128)S(1)}, u32[]{:S(2)}, u32[]{:S(2)}) %collective-permute-start.28) | collective-permute-done | bytes 196640 | tf_op jit(solution)/shard_map/ppermute | solution.py:296
  102.3 50.1 %transform.1 = f32[4,32,8,256]{3,2,1,0:T(8,128)} custom-call(s32[3]{0:T(128)S(1)} %pad_add_fusion.own_ref, f32[256,8,128]{2,1,0:T(8,128)S(1)} %constant_dynamic-update-slice_fusion.29.c_ref, s32[256,3,128]{2,1,0:T(4,128)S(1)} %constant_dynamic-update-slice_fusion.67.m_ref, bf16[4,256,256]{2,1,0:T(8,128)(2,1)S(1)} %copy-done, bf16[2,512,256]{2,1,0:T(8,128)(2,1)S(1)} %copy-done.1), custom_call_target="tpu_custom_call" | custom-call | tf_op jit(solution)/shard_map/transform/pallas_call | solution.py:280
  (104 shorter events, 14.1 us)
Async XLA Ops:
  0.7 21.7 %collective-permute-start = (f32[8,256]{1,0:T(8,128)S(1)}, f32[8,256]{1,0:T(8,128)S(1)}, u32[]{:S(2)}, u32[]{:S(2)}) collective-permute-start(f32[8,256]{1,0:T(8,128)S(1)} %get-tuple-element.37), channel_id=1, source_target_pairs={{0,8},{8,0},{16,24},{24,16},{32,40},{40,32},{48,56},{56,48},{64,72... | collective-permute-start | bytes 24584 | tf_op jit(solution)/shard_map/ppermute | solution.py:296
  4.7 6.3 %collective-permute-start.18 = (s32[1,3,128]{2,1,0:T(4,128)S(1)}, s32[1,3,128]{2,1,0:T(4,128)S(1)}, u32[]{:S(2)}, u32[]{:S(2)}) collective-permute-start(s32[1,3,128]{2,1,0:T(4,128)S(1)} %get-tuple-element.89), channel_id=1, source_target_pairs={{0,4},{1,5},{2,6},{3,7},{4,0},{5,1},{6,2},{7,3},{8,12},{9,13},{10,... | collective-permute-start | bytes 4616 | tf_op jit(solution)/shard_map/ppermute | solution.py:296
  11.1 3.9 %collective-permute-start.19 = (s32[2,3,128]{2,1,0:T(4,128)S(1)}, s32[2,3,128]{2,1,0:T(4,128)S(1)}, u32[]{:S(2)}, u32[]{:S(2)}) collective-permute-start(s32[2,3,128]{2,1,0:T(4,128)S(1)} %get-tuple-element.75), channel_id=1, source_target_pairs={{0,16},{8,24},{16,0},{24,8},{32,48},{40,56},{48,32},{56,40},{64,80... | collective-permute-start | bytes 9224 | tf_op jit(solution)/shard_map/ppermute | solution.py:296
  14.3 4.3 %collective-permute-start.21 = (s32[2,3,128]{2,1,0:T(4,128)S(1)}, s32[2,3,128]{2,1,0:T(4,128)S(1)}, u32[]{:S(2)}, u32[]{:S(2)}) collective-permute-start(s32[2,3,128]{2,1,0:T(4,128)S(1)} %get-tuple-element.75), channel_id=1, source_target_pairs={{0,48},{8,56},{16,32},{24,40},{32,16},{40,24},{48,0},{56,8},{64,11... | collective-permute-start | bytes 9224 | tf_op jit(solution)/shard_map/ppermute | solution.py:296
  18.6 4.9 %collective-permute-start.22 = (s32[8,3,128]{2,1,0:T(4,128)S(1)}, s32[8,3,128]{2,1,0:T(4,128)S(1)}, u32[]{:S(2)}, u32[]{:S(2)}) collective-permute-start(s32[8,3,128]{2,1,0:T(4,128)S(1)} %get-tuple-element.54), channel_id=1, source_target_pairs={{0,1},{1,0},{2,3},{3,2},{4,5},{5,4},{6,7},{7,6},{8,9},{9,8},{10,11... | collective-permute-start | bytes 36872 | tf_op jit(solution)/shard_map/ppermute | solution.py:296
  19.8 12.0 %collective-permute-start.23 = (s32[8,3,128]{2,1,0:T(4,128)S(1)}, s32[8,3,128]{2,1,0:T(4,128)S(1)}, u32[]{:S(2)}, u32[]{:S(2)}) collective-permute-start(s32[8,3,128]{2,1,0:T(4,128)S(1)} %get-tuple-element.54), channel_id=1, source_target_pairs={{0,2},{1,3},{2,0},{3,1},{4,6},{5,7},{6,4},{7,5},{8,10},{9,11},{10,... | collective-permute-start | bytes 36872 | tf_op jit(solution)/shard_map/ppermute | solution.py:296
  22.3 43.9 %collective-permute-start.24 = (s32[8,3,128]{2,1,0:T(4,128)S(1)}, s32[8,3,128]{2,1,0:T(4,128)S(1)}, u32[]{:S(2)}, u32[]{:S(2)}) collective-permute-start(s32[8,3,128]{2,1,0:T(4,128)S(1)} %get-tuple-element.54), channel_id=1, source_target_pairs={{0,3},{1,2},{2,1},{3,0},{4,7},{5,6},{6,5},{7,4},{8,11},{9,10},{10,... | collective-permute-start | bytes 36872 | tf_op jit(solution)/shard_map/ppermute | solution.py:296
  23.5 4.4 %collective-permute-start.3 = (f32[8,512]{1,0:T(8,128)S(1)}, f32[8,512]{1,0:T(8,128)S(1)}, u32[]{:S(2)}, u32[]{:S(2)}) collective-permute-start(f32[8,512]{1,0:T(8,128)S(1)} %pad_maximum_fusion.1), channel_id=1, source_target_pairs={{0,48},{8,56},{16,32},{24,40},{32,16},{40,24},{48,0},{56,8},{64,11... | collective-permute-start | bytes 49160 | tf_op jit(solution)/shard_map/ppermute | solution.py:296
  27.9 8.9 %collective-permute-start.4 = (f32[8,2048]{1,0:T(8,128)S(1)}, f32[8,2048]{1,0:T(8,128)S(1)}, u32[]{:S(2)}, u32[]{:S(2)}) collective-permute-start(f32[8,2048]{1,0:T(8,128)S(1)} %constant_dynamic-update-slice_fusion.refs_3_), channel_id=1, source_target_pairs={{0,64},{8,72},{16,80},{24,88},{32,96},{40,104},{48,112},{56,120},{... | collective-permute-start | bytes 196616 | tf_op jit(solution)/shard_map/ppermute | solution.py:296
  29.2 7.7 %collective-permute-start.5 = (f32[8,2048]{1,0:T(8,128)S(1)}, f32[8,2048]{1,0:T(8,128)S(1)}, u32[]{:S(2)}, u32[]{:S(2)}) collective-permute-start(f32[8,2048]{1,0:T(8,128)S(1)} %constant_dynamic-update-slice_fusion.refs_3_), channel_id=1, source_target_pairs={{0,128},{8,136},{16,144},{24,152},{32,160},{40,168},{48,176},{56,1... | collective-permute-start | bytes 196616 | tf_op jit(solution)/shard_map/ppermute | solution.py:296
  31.8 5.1 %collective-permute-start.6 = (f32[8,2048]{1,0:T(8,128)S(1)}, f32[8,2048]{1,0:T(8,128)S(1)}, u32[]{:S(2)}, u32[]{:S(2)}) collective-permute-start(f32[8,2048]{1,0:T(8,128)S(1)} %constant_dynamic-update-slice_fusion.refs_3_), channel_id=1, source_target_pairs={{0,192},{8,200},{16,208},{24,216},{32,224},{40,232},{48,240},{56,2... | collective-permute-start | bytes 196616 | tf_op jit(solution)/shard_map/ppermute | solution.py:296
  52.4 6.5 %collective-permute-start.7 = (f32[1,8,128]{2,1,0:T(8,128)S(1)}, f32[1,8,128]{2,1,0:T(8,128)S(1)}, u32[]{:S(2)}, u32[]{:S(2)}) collective-permute-start(f32[1,8,128]{2,1,0:T(8,128)S(1)} %bitcast.37), channel_id=1, source_target_pairs={{0,4},{1,5},{2,6},{3,7},{4,0},{5,1},{6,2},{7,3},{8,12},{9,13},{10,... | collective-permute-start | bytes 12296 | tf_op jit(solution)/shard_map/ppermute | solution.py:296
  58.9 3.9 %collective-permute-start.9 = (f32[2,8,128]{2,1,0:T(8,128)S(1)}, f32[2,8,128]{2,1,0:T(8,128)S(1)}, u32[]{:S(2)}, u32[]{:S(2)}) collective-permute-start(f32[2,8,128]{2,1,0:T(8,128)S(1)} %pad_maximum_fusion.3), channel_id=1, source_target_pairs={{0,32},{8,40},{16,48},{24,56},{32,0},{40,8},{48,16},{56,24},{64,96... | collective-permute-start | bytes 24584 | tf_op jit(solution)/shard_map/ppermute | solution.py:296
  61.8 4.3 %collective-permute-start.10 = (f32[2,8,128]{2,1,0:T(8,128)S(1)}, f32[2,8,128]{2,1,0:T(8,128)S(1)}, u32[]{:S(2)}, u32[]{:S(2)}) collective-permute-start(f32[2,8,128]{2,1,0:T(8,128)S(1)} %pad_maximum_fusion.3), channel_id=1, source_target_pairs={{0,48},{8,56},{16,32},{24,40},{32,16},{40,24},{48,0},{56,8},{64,11... | collective-permute-start | bytes 24584 | tf_op jit(solution)/shard_map/ppermute | solution.py:296
  66.1 4.1 %collective-permute-start.11 = (f32[8,8,128]{2,1,0:T(8,128)S(1)}, f32[8,8,128]{2,1,0:T(8,128)S(1)}, u32[]{:S(2)}, u32[]{:S(2)}) collective-permute-start(f32[8,8,128]{2,1,0:T(8,128)S(1)} %get-tuple-element.42), channel_id=1, source_target_pairs={{0,1},{1,0},{2,3},{3,2},{4,5},{5,4},{6,7},{7,6},{8,9},{9,8},{10,11... | collective-permute-start | bytes 98312 | tf_op jit(solution)/shard_map/ppermute | solution.py:296
  66.1 14.3 %collective-permute-start.25 = (s32[32,3,128]{2,1,0:T(4,128)S(1)}, s32[32,3,128]{2,1,0:T(4,128)S(1)}, u32[]{:S(2)}, u32[]{:S(2)}) collective-permute-start(s32[32,3,128]{2,1,0:T(4,128)S(1)} %get-tuple-element.30), channel_id=1, source_target_pairs={{0,64},{8,72},{16,80},{24,88},{32,96},{40,104},{48,112},{56,120},{... | collective-permute-start | bytes 147464 | tf_op jit(solution)/shard_map/ppermute | solution.py:296
  66.2 5.2 %collective-permute-start.12 = (f32[8,8,128]{2,1,0:T(8,128)S(1)}, f32[8,8,128]{2,1,0:T(8,128)S(1)}, u32[]{:S(2)}, u32[]{:S(2)}) collective-permute-start(f32[8,8,128]{2,1,0:T(8,128)S(1)} %get-tuple-element.42), channel_id=1, source_target_pairs={{0,2},{1,3},{2,0},{3,1},{4,6},{5,7},{6,4},{7,5},{8,10},{9,11},{10,... | collective-permute-start | bytes 98312 | tf_op jit(solution)/shard_map/ppermute | solution.py:296
  70.0 4.0 %collective-permute-start.13 = (f32[8,8,128]{2,1,0:T(8,128)S(1)}, f32[8,8,128]{2,1,0:T(8,128)S(1)}, u32[]{:S(2)}, u32[]{:S(2)}) collective-permute-start(f32[8,8,128]{2,1,0:T(8,128)S(1)} %get-tuple-element.42), channel_id=1, source_target_pairs={{0,3},{1,2},{2,1},{3,0},{4,7},{5,6},{6,5},{7,4},{8,11},{9,10},{10,... | collective-permute-start | bytes 98312 | tf_op jit(solution)/shard_map/ppermute | solution.py:296
  74.0 7.2 %collective-permute-start.14 = (f32[32,8,128]{2,1,0:T(8,128)S(1)}, f32[32,8,128]{2,1,0:T(8,128)S(1)}, u32[]{:S(2)}, u32[]{:S(2)}) collective-permute-start(f32[32,8,128]{2,1,0:T(8,128)S(1)} %get-tuple-element.21), channel_id=1, source_target_pairs={{0,64},{8,72},{16,80},{24,88},{32,96},{40,104},{48,112},{56,120},{... | collective-permute-start | bytes 393224 | tf_op jit(solution)/shard_map/ppermute | solution.py:296
  75.4 23.7 %collective-permute-start.26 = (s32[32,3,128]{2,1,0:T(4,128)S(1)}, s32[32,3,128]{2,1,0:T(4,128)S(1)}, u32[]{:S(2)}, u32[]{:S(2)}) collective-permute-start(s32[32,3,128]{2,1,0:T(4,128)S(1)} %get-tuple-element.30), channel_id=1, source_target_pairs={{0,128},{8,136},{16,144},{24,152},{32,160},{40,168},{48,176},{56,1... | collective-permute-start | bytes 147464 | tf_op jit(solution)/shard_map/ppermute | solution.py:296
  77.9 21.3 %collective-permute-start.27 = (s32[32,3,128]{2,1,0:T(4,128)S(1)}, s32[32,3,128]{2,1,0:T(4,128)S(1)}, u32[]{:S(2)}, u32[]{:S(2)}) collective-permute-start(s32[32,3,128]{2,1,0:T(4,128)S(1)} %get-tuple-element.30), channel_id=1, source_target_pairs={{0,192},{8,200},{16,208},{24,216},{32,224},{40,232},{48,240},{56,2... | collective-permute-start | bytes 147464 | tf_op jit(solution)/shard_map/ppermute | solution.py:296
  78.1 5.4 %collective-permute-start.15 = (f32[32,8,128]{2,1,0:T(8,128)S(1)}, f32[32,8,128]{2,1,0:T(8,128)S(1)}, u32[]{:S(2)}, u32[]{:S(2)}) collective-permute-start(f32[32,8,128]{2,1,0:T(8,128)S(1)} %get-tuple-element.21), channel_id=1, source_target_pairs={{0,128},{8,136},{16,144},{24,152},{32,160},{40,168},{48,176},{56,1... | collective-permute-start | bytes 393224 | tf_op jit(solution)/shard_map/ppermute | solution.py:296
  80.5 5.1 %collective-permute-start.16 = (f32[32,8,128]{2,1,0:T(8,128)S(1)}, f32[32,8,128]{2,1,0:T(8,128)S(1)}, u32[]{:S(2)}, u32[]{:S(2)}) collective-permute-start(f32[32,8,128]{2,1,0:T(8,128)S(1)} %get-tuple-element.21), channel_id=1, source_target_pairs={{0,192},{8,200},{16,208},{24,216},{32,224},{40,232},{48,240},{56,2... | collective-permute-start | bytes 393224 | tf_op jit(solution)/shard_map/ppermute | solution.py:296
  85.6 15.5 %collective-permute-start.17 = (f32[128,8,128]{2,1,0:T(8,128)S(1)}, f32[128,8,128]{2,1,0:T(8,128)S(1)}, u32[]{:S(2)}, u32[]{:S(2)}) collective-permute-start(f32[128,8,128]{2,1,0:T(8,128)S(1)} %get-tuple-element.5), channel_id=1, source_target_pairs={{0,8},{8,0},{16,24},{24,16},{32,40},{40,32},{48,56},{56,48},{64,72... | collective-permute-start | bytes 1572872 | tf_op jit(solution)/shard_map/ppermute | solution.py:296
  (12 other events, 21.8 us)

commit v2 on v1

--- a/solution.py
+++ b/solution.py
@@ -12,6 +12,7 @@
 G = 256
 TILE = 256
 LOG2E = math.log2(math.e)
+ROWS = 11
 
 SIN_C = (3.141592640183972, -5.167710090328514, 2.550077659663962, -0.5982921590533228, 0.07765940739590604)
 COS_C = (0.9999999534665512, -4.934792858660287, 4.058411913867176, -1.3318801593277205, 0.21969679475921783)
@@ -79,8 +80,8 @@
         acc_in = refs[pos]
         pos += 1
     if last:
-        obs_ref = refs[pos]
-        pos += 1
+        obs_ref, ind_ref = refs[pos : pos + 2]
+        pos += 2
     out_ref = refs[pos]
     pos += 1
     if last:
@@ -139,17 +140,18 @@
             f_im = ((2.0 * SIN_K * COS_K) * sums[4 + r]) * atom_scale
             reals.append((obs0 * f_re + obs1 * f_im) * refl_scale)
             imags.append((obs1 * f_re - obs0 * f_im) * refl_scale)
-        out_ref[...] = jnp.concatenate(reals + imags, axis=0)
-
-
-def phase_call(lhs, s2, rc, atoms, acc, obs, scales):
+        for q, row in enumerate(reals + imags + [ind_ref[q : q + 1, :] for q in range(3)]):
+            out_ref[0:1, q * 128 : q * 128 + 128] = row
+
+
+def phase_call(lhs, s2, rc, atoms, acc, obs, indices, scales):
     first, last = acc is None, obs is not None
-    operands = [lhs, s2, rc, *atoms] + ([] if first else [acc]) + ([obs] if last else [])
+    operands = [lhs, s2, rc, *atoms] + ([] if first else [acc]) + ([obs, indices] if last else [])
     acc_shape = (9, 128, 128)
     scratch = [pltpu.VMEM((512, TILE), jnp.float32)]
     if last:
         scratch = [pltpu.VMEM(acc_shape, jnp.float32)] + scratch
-    out = jax.ShapeDtypeStruct((8, 128) if last else acc_shape, jnp.float32)
+    out = jax.ShapeDtypeStruct((1, ROWS * 128) if last else acc_shape, jnp.float32)
     count = sum(a.shape[1] for a in atoms)
     return pl.pallas_call(
         functools.partial(phase_kernel, len(atoms), first, last, scales),
@@ -165,66 +167,81 @@
     )(*operands)
 
 
-def block_id(core, y, x, z_lo, z_hi):
-    return (((core * 4 + y) * 4 + x) * 4 + z_lo) * 2 + z_hi
-
-
-def transform_kernel(own_ref, c_ref, m_ref, tt_ref, d_ref, out_ref, x_ref, z_ref):
-    own = own_ref[0]
-    own_j = own_ref[1]
-    own_g = own_ref[2]
-    cells = lax.broadcasted_iota(jnp.int32, (128, 128), 0)
-    w_index = lax.broadcasted_iota(jnp.int32, (8, 128), 0) + own_j * 8
-
-    def scatter(b):
-        where = own ^ b
-        z_hi = where & 1
-        z_lo = (where >> 1) & 3
-        x = (where >> 3) & 3
-        y = (where >> 5) & 3
-        core = (where >> 7) & 1
-        g = z_hi * 4 + x
-        j = (y * 4 + z_lo) * 2 + core
-        m = m_ref[b]
-        h = (m[0:1] & 255) - g * 32
-        k = (m[1:2] & 255) - j * 8
-        row = (h >> 1) * 8 + k
-        odd = (h & 1).astype(jnp.float32)
-        one_hot = jnp.where(cells == row, 1.0, 0.0).astype(jnp.bfloat16)
-        product = (m[2:3] * w_index) & 255
-        sine, cosine = sincos_turns(product.astype(jnp.float32) * (1.0 / G))
-        c = c_ref[b]
-        reals, imags = [], []
-        for r in range(4):
-            re, im = c[r : r + 1], c[4 + r : 5 + r]
-            reals.append(re * cosine - im * sine)
-            imags.append(re * sine + im * cosine)
-        real, imag = jnp.concatenate(reals, axis=0), jnp.concatenate(imags, axis=0)
-        value = jnp.concatenate(
-            [real * (1.0 - odd), real * odd, imag * (1.0 - odd), imag * odd], axis=0
-        )
-        rows = jnp.concatenate(split2(value), axis=0)
-        both = lax.dot_general(
-            one_hot, rows, (((1,), (1,)), ((), ())), preferred_element_type=jnp.float32
-        )
-        total = both[:, :128] + both[:, 128:]
-        x_ref[pl.ds(g * 16, 16), pl.ds(pl.multiple_of(j * 8, 8), 8), :] = total.reshape(16, 8, 128)
-
-    @pl.loop(0, c_ref.shape[0] // 2)
-    def _(i):
-        scatter(2 * i)
-        scatter(2 * i + 1)
-
-    table = jnp.concatenate(
-        [tt_ref[q, pl.ds(pl.multiple_of(own_g * 32, 32), 32), :] for q in range(4)], axis=0
-    )
+def scatter_kernel(piece, own_ref, p_ref, x_ref):
+    y, core = own_ref[0] ^ (piece & 3), own_ref[1] ^ (piece >> 2)
+    cells = lax.broadcasted_iota(jnp.int32, (128, 128), 0).astype(jnp.float32)
+    w_turn = (lax.broadcasted_iota(jnp.int32, (8, 128), 0) + own_ref[3] * 8).astype(
+        jnp.float32
+    ) * (1.0 / G)
+    sub = lax.broadcasted_iota(jnp.int32, (8, 128), 0)
+    for base in range(0, 32, 8):
+        h = p_ref[base : base + 8, 8 * 128 : 9 * 128]
+        k = p_ref[base : base + 8, 9 * 128 : 10 * 128]
+        third = p_ref[base : base + 8, 10 * 128 : 11 * 128]
+        h = jnp.where(h < 0.0, h + G, h) - ((base + sub) // 4 * 32).astype(jnp.float32)
+        k = jnp.where(k < 0.0, k + G, k) - (((y * 4 + (sub & 3)) * 2 + core) * 8).astype(jnp.float32)
+        pair = jnp.floor(h * 0.5)
+        odd = h - 2.0 * pair
+        row = pair * 8.0 + k
+        for q in range(8):
+            i = base + q
+            g, z_lo = i // 4, i % 4
+            one_hot = jnp.where(cells == row[q : q + 1], 1.0, 0.0).astype(jnp.bfloat16)
+            sine, cosine = sincos_turns(third[q : q + 1] * w_turn)
+            reals, imags = [], []
+            for r in range(4):
+                re = p_ref[i : i + 1, r * 128 : r * 128 + 128]
+                im = p_ref[i : i + 1, (4 + r) * 128 : (5 + r) * 128]
+                reals.append(re * cosine - im * sine)
+                imags.append(re * sine + im * cosine)
+            hi, lo = split2(jnp.concatenate(reals + imags, axis=0))
+            odd_row = jnp.broadcast_to(odd[q : q + 1], (32, 128)).astype(jnp.bfloat16)
+            even_row = jnp.broadcast_to(1.0 - odd[q : q + 1], (32, 128)).astype(jnp.bfloat16)
+
+            def masked(part):
+                return jnp.concatenate(
+                    [part[:32] * even_row, part[:32] * odd_row, part[32:] * even_row, part[32:] * odd_row],
+                    axis=0,
+                )
+
+            total = lax.dot_general(
+                jnp.concatenate([one_hot, one_hot], axis=1),
+                jnp.concatenate([masked(hi), masked(lo)], axis=1),
+                (((1,), (1,)), ((), ())),
+                preferred_element_type=jnp.float32,
+            )
+            x_ref[g * 16 : g * 16 + 16, z_lo * 8 : z_lo * 8 + 8, :] = total.reshape(16, 8, 128)
+
+
+def scatter_call(piece, own, payload):
+    vmem = pl.BlockSpec(memory_space=pltpu.VMEM)
+    return pl.pallas_call(
+        functools.partial(scatter_kernel, piece),
+        out_shape=jax.ShapeDtypeStruct((128, 32, 128), jnp.float32),
+        in_specs=[pl.BlockSpec(memory_space=pltpu.SMEM), vmem],
+        out_specs=vmem,
+        compiler_params=pltpu.CompilerParams(vmem_limit_bytes=16 << 20),
+        cost_estimate=pl.CostEstimate(flops=2 << 30, bytes_accessed=1 << 20, transcendentals=0),
+        name="scatter",
+    )(own, payload)
+
+
+def transform_kernel(own_ref, *refs):
+    x_refs, (d_ref, out_ref, z_ref) = refs[:8], refs[8:]
+    own_y, own_core, own_g = own_ref[0], own_ref[1], own_ref[2]
+    column = lax.broadcasted_iota(jnp.int32, (32, G), 1)
+    y, core = own_y ^ ((column >> 5) & 3), own_core ^ (column >> 7)
+    k = ((y * 4 + ((column >> 3) & 3)) * 2 + core) * 8 + (column & 7)
+    v = lax.broadcasted_iota(jnp.int32, (32, G), 0) + own_g * 32
+    sine, cosine = sincos_turns(((k * v) & (G - 1)).astype(jnp.float32) * (1.0 / G))
+    table = jnp.concatenate(split2(jnp.concatenate([cosine, sine], axis=0)), axis=0)
     lane = lax.broadcasted_iota(jnp.int32, (32, 128), 1)
     sign = jnp.where(lane < 64, -1.0, 1.0)
 
-    @pl.loop(0, 64)
+    @pl.loop(0, 64, unroll=8)
     def _(i):
-        block = jnp.concatenate([x_ref[2 * i], x_ref[2 * i + 1]], axis=1)
-        hi, lo = split2(block)
+        sides = [jnp.concatenate([x_ref[2 * i + q] for x_ref in x_refs], axis=0) for q in range(2)]
+        hi, lo = split2(jnp.concatenate(sides, axis=1))
         o1 = jnp.dot(table, hi, preferred_element_type=jnp.float32)
         o2 = jnp.dot(table[:64], lo, preferred_element_type=jnp.float32)
         z = o1[:64] + o1[64:] + o2
@@ -233,7 +250,7 @@
             combined = z[:32, lanes] + sign * pltpu.roll(z[32:, lanes], 64, 1)
             z_ref[pl.ds(2 * i + half, 32, stride=128), :] = combined
 
-    @pl.loop(0, 4)
+    @pl.loop(0, 4, unroll=4)
     def _(i):
         parts = []
         for q in range(8):
@@ -259,36 +276,31 @@
     return hi, lo
 
 
-def tables():
+def first_table():
     index = np.arange(G)
     angle = 2.0 * np.pi * ((index[:, None] * index[None, :]) % G) / G
     cos_hi, cos_lo = split_np(np.cos(angle))
     sin_hi, sin_lo = split_np(np.sin(angle))
-    second = np.stack([cos_hi, sin_hi, cos_lo, sin_lo])
     order = np.concatenate([np.arange(0, G, 2), np.arange(1, G, 2)])
-    first = np.stack(
+    return np.stack(
         [
             np.concatenate([cos_hi[order], -sin_hi[order]]),
             np.concatenate([cos_lo[order], -sin_lo[order]]),
         ]
     )
-    return second, first
-
-
-def transform_call(own, coefs, miller, second, first):
+
+
+def transform_call(own, pieces, first):
     vmem = pl.BlockSpec(memory_space=pltpu.VMEM)
     return pl.pallas_call(
         transform_kernel,
         out_shape=jax.ShapeDtypeStruct((4, 32, 8, G), jnp.float32),
-        in_specs=[pl.BlockSpec(memory_space=pltpu.SMEM)] + [vmem] * 4,
+        in_specs=[pl.BlockSpec(memory_space=pltpu.SMEM)] + [vmem] * 9,
         out_specs=vmem,
-        scratch_shapes=[
-            pltpu.VMEM((128, G, 128), jnp.float32),
-            pltpu.VMEM((32 * 128, 128), jnp.float32),
-        ],
+        scratch_shapes=[pltpu.VMEM((32 * 128, 128), jnp.float32)],
         compiler_params=pltpu.CompilerParams(vmem_limit_bytes=40 << 20),
         name="transform",
-    )(own, coefs, miller, second, first)
+    )(own, *pieces, first)
 
 
 def swap(x, axis, mask):
@@ -296,16 +308,12 @@
     return lax.ppermute(x, axis, [(i, i ^ mask) for i in range(count)])
 
 
-def spread(x, axis, masks, dim=0):
-    return jnp.concatenate([x] + [swap(x, axis, mask) for mask in masks], axis=dim)
-
-
-def spread_all(x):
-    x = spread(x, "refl", (4,))
-    x = spread(x, "atom", (2, 4, 6))
-    x = spread(x, "refl", (1, 2, 3))
-    x = spread(x, "atom", (8, 16, 24))
-    return spread(x, "atom", (1,))
+def column_groups():
+    return [
+        [((y * 4 + z_lo) * 2 + core) * 8 + g for g in range(8) for z_lo in range(4)]
+        for y in range(4)
+        for core in range(2)
+    ]
 
 
 def shards(coords, weights, thermal, angles, miller, observed):
@@ -319,9 +327,10 @@
         1.0 / math.sqrt(own_count * atom_count * refl_count),
     )
     atoms = jnp.concatenate([coords, weights[None], thermal[None], jnp.zeros_like(coords)], axis=0)
-    atoms = spread(atoms, "atom", (1,), 1)
-    atoms = spread(atoms, "atom", (2, 4, 6), 1)
-    others = [swap(atoms, "atom", mask) for mask in (8, 16, 24)]
+    atoms = jnp.concatenate([atoms, swap(atoms, "atom", 1)], axis=1)
+    near = [swap(atoms, "atom", mask) for mask in (2, 6, 4)]
+    run = jnp.concatenate([atoms, *near], axis=1)
+    far = [swap(run, "atom", mask) for mask in (8, 24, 16)]
 
     own_miller = lax.dynamic_slice_in_dim(miller[:, 0, :], j * own_count, own_count, 1)
     indices = own_miller.astype(jnp.float32)
@@ -334,16 +343,26 @@
     rc = jnp.transpose(matrices, (0, 2, 1)).reshape(12, 3)
     rc = jnp.pad(rc, ((0, 4), (0, 125)))
 
-    all_miller = spread_all(own_miller[None])
-    acc = phase_call(lhs, s2, rc, [atoms], None, None, scales)
-    coefs = phase_call(lhs, s2, rc, others, acc, observed[:, 0, :], scales)
-    coefs = spread_all(coefs[None])
-
-    z_hi, x = g // 4, g % 4
-    y, z_lo, core = j // 8, (j // 2) % 4, j % 2
-    own = jnp.stack([block_id(core, y, x, z_lo, z_hi), j, g]).astype(jnp.int32)
-    second, first = tables()
-    return transform_call(own, coefs, all_miller, second, first)
+    acc = phase_call(lhs, s2, rc, [atoms], None, None, None, scales)
+    acc = phase_call(lhs, s2, rc, near, acc, None, None, scales)
+    payload = phase_call(lhs, s2, rc, far, acc, observed[:, 0, :], indices, scales)
+
+    own = jnp.stack([j // 8, j % 2, g, j]).astype(jnp.int32)
+    plane = lax.all_to_all(
+        jnp.broadcast_to(payload, (32, payload.shape[1])),
+        ("atom", "refl"),
+        0,
+        0,
+        tiled=True,
+        axis_index_groups=column_groups(),
+    )
+    pieces = [plane] + [None] * 7
+    for m in (1, 3, 2):
+        pieces[m] = swap(plane, "atom", 8 * m)
+    for m in (0, 1, 3, 2):
+        pieces[4 + m] = swap(pieces[m], "atom", 1)
+    lines = [scatter_call(q, own, piece) for q, piece in enumerate(pieces)]
+    return transform_call(own, lines, first_table())
 
 
 def solution(mesh):

time: 153 us -> 96.3 us (0.63)
  Pallas kernels: 70 us -> 40.4 us
  starting transfers between devices: 57.2 us -> 28.4 us
  other arithmetic: 1.03 us -> 3.43 us
    pallas_call x1, Pallas kernels: 50.1 us -> 10.2 us  [transform_call(): pl.pallas_call(transform_kernel, out_shape=jax.ShapeDtypeStruct((4, 32, 8...]
    ppermute x29 -> x14, starting transfers between devices: 57.2 us -> 19.2 us  [swap(): return lax.ppermute(x, axis, [(i, i ^ mask) for i in range(count)])]
    ppermute x29 -> x14, waiting for transfers between devices: 20 us -> 9.42 us  [swap(): return lax.ppermute(x, axis, [(i, i ^ mask) for i in range(count)])]
    pallas_call x0 -> x8, Pallas kernels: none -> 10.3 us  [scatter_call(): pl.pallas_call(functools.partial(scatter_kernel, piece), out_shape=jax.Sh...]
    all_to_all x0 -> x1, waiting for transfers between devices: none -> 10.2 us  [shards(): lax.all_to_all(jnp.broadcast_to(payload, (32, payload.shape[1])), ('atom'...]
    all_to_all x0 -> x1, starting transfers between devices: none -> 9.25 us  [shards(): lax.all_to_all(jnp.broadcast_to(payload, (32, payload.shape[1])), ('atom'...]
    unnamed x40 -> x16, local copies, waits for them, and re-layouts: 3.39 us -> 2.7 us
    pallas_call x2 -> x3, Pallas kernels: 19.9 us -> 20 us  [phase_call(): pl.pallas_call(functools.partial(phase_kernel, len(atoms), first, last, s...]
  transfers between devices with their start and end apart: 29 -> 15, of which waited for: 12 -> 4; matrix products, arithmetic and copies ran while one was open for 1% -> 2% of each run, Pallas kernels for 13% -> 15%
where the time goes in v2:
time: 96.3 us; the launch traced here: 95.9 us
  Pallas kernels  40.4 us (42%)
  starting transfers between devices  28.4 us (29%)
  waiting for transfers between devices  19.6 us (20%)
  local copies, waits for them, and re-layouts  3.79 us (4%)
  other arithmetic  3.43 us (4%)
    pallas_call x3, Pallas kernels, phase_call(): pl.pallas_call(functools.partial(phase_kernel, len(atoms), first, last, s...  20 us
    ppermute x14, starting transfers between devices, swap(): return lax.ppermute(x, axis, [(i, i ^ mask) for i in range(count)])  19.2 us
    pallas_call x8, Pallas kernels, scatter_call(): pl.pallas_call(functools.partial(scatter_kernel, piece), out_shape=jax.Sh...  10.3 us
    all_to_all x1, waiting for transfers between devices, shards(): lax.all_to_all(jnp.broadcast_to(payload, (32, payload.shape[1])), ('atom'...  10.2 us
    pallas_call x1, Pallas kernels, transform_call(): pl.pallas_call(transform_kernel, out_shape=jax.ShapeDtypeStruct((4, 32, 8...  10.2 us
    ppermute x14, waiting for transfers between devices, swap(): return lax.ppermute(x, axis, [(i, i ^ mask) for i in range(count)])  9.42 us
    all_to_all x1, starting transfers between devices, shards(): lax.all_to_all(jnp.broadcast_to(payload, (32, payload.shape[1])), ('atom'...  9.25 us
    unnamed x16, local copies, waits for them, and re-layouts  2.7 us
  transfers between devices with their start and end apart: 15, of which 4 were waited for; matrix products, arithmetic and copies ran while one was open for 2% of the time, Pallas kernels for 15%

profile of v2, /device:TPU:1, one launch (start us, length us, event | category | flops | bytes accessed | tf_op | source)
XLA Modules:
  0.0 95.9 jit_solution(2224705643820475399)
XLA Ops:
  0.8 3.3 %collective-permute-start = (f32[8,256]{1,0:T(8,128)S(1)}, f32[8,256]{1,0:T(8,128)S(1)}, u32[]{:S(2)}, u32[]{:S(2)}) collective-permute-start(f32[8,256]{1,0:T(8,128)S(1)} %get-tuple-element.5), channel_id=1, source_target_pairs={{0,8},{8,0},{16,24},{24,16},{32,40},{40,32},{48,56},{56,48},{64,72... | collective-permute-start | bytes 24584 | tf_op jit(solution)/shard_map/ppermute | solution.py:308
  6.9 1.4 %collective-permute-start.3 = (f32[8,512]{1,0:T(8,128)S(1)}, f32[8,512]{1,0:T(8,128)S(1)}, u32[]{:S(2)}, u32[]{:S(2)}) collective-permute-start(f32[8,512]{1,0:T(8,128)S(1)} %pad_maximum_fusion.1.refs_3_), channel_id=1, source_target_pairs={{0,32},{8,40},{16,48},{24,56},{32,0},{40,8},{48,16},{56,24},{64,96... | collective-permute-start | bytes 49160 | tf_op jit(solution)/shard_map/ppermute | solution.py:308
  8.2 1.5 %collective-permute-start.2 = (f32[8,512]{1,0:T(8,128)S(1)}, f32[8,512]{1,0:T(8,128)S(1)}, u32[]{:S(2)}, u32[]{:S(2)}) collective-permute-start(f32[8,512]{1,0:T(8,128)S(1)} %pad_maximum_fusion.1.refs_3_), channel_id=1, source_target_pairs={{0,48},{8,56},{16,32},{24,40},{32,16},{40,24},{48,0},{56,8},{64,11... | collective-permute-start | bytes 49160 | tf_op jit(solution)/shard_map/ppermute | solution.py:308
  9.9 2.4 %collective-permute-done.1.refs_3_ = f32[8,512]{1,0:T(8,128)S(1)} collective-permute-done((f32[8,512]{1,0:T(8,128)S(1)}, f32[8,512]{1,0:T(8,128)S(1)}, u32[]{:S(2)}, u32[]{:S(2)}) %collective-permute-start.1) | collective-permute-done | bytes 16416 | tf_op jit(solution)/shard_map/ppermute | solution.py:308
  12.6 3.0 %collective-permute-start.6 = (f32[8,2048]{1,0:T(8,128)S(1)}, f32[8,2048]{1,0:T(8,128)S(1)}, u32[]{:S(2)}, u32[]{:S(2)}) collective-permute-start(f32[8,2048]{1,0:T(8,128)S(1)} %constant_dynamic-update-slice_fusion), channel_id=1, source_target_pairs={{0,128},{8,136},{16,144},{24,152},{32,160},{40,168},{48,176},{56,1... | collective-permute-start | bytes 196616 | tf_op jit(solution)/shard_map/ppermute | solution.py:308
  16.6 1.3 %phases.3.refs_6_ = f32[9,128,128]{2,1,0:T(8,128)S(1)} custom-call(bf16[512,48]{1,0:T(8,128)(2,1)S(1)} %copy.21.refs_0_, f32[128,128]{1,0:T(8,128)S(1)} %broadcast_in_dim.10.refs_1_, f32[16,128]{1,0:T(8,128)S(1)} %pad.9.refs_2_, f32[8,512]{1,0:T(8,128)S(1)} %pad_maximum_fusion.1.refs_3_), custom_call_target="tpu_custom_call" | custom-call | flops 5767168 | bytes 1048576 | tf_op jit(solution)/shard_map/phases/pallas_call | solution.py:156
  17.9 3.7 %phases.4.refs_6_ = f32[9,128,128]{2,1,0:T(8,128)S(1)} custom-call(bf16[512,48]{1,0:T(8,128)(2,1)S(1)} %copy.21.refs_0_, f32[128,128]{1,0:T(8,128)S(1)} %broadcast_in_dim.10.refs_1_, f32[16,128]{1,0:T(8,128)S(1)} %pad.9.refs_2_, f32[8,512]{1,0:T(8,128)S(1)} %collective-permute-done.1.refs_3_, f32[8,512]{1,0:T(8,128)S(1)} %collective-permute-done.2.refs_4_, ...), custom_call_target="tpu_custom_call" | custom-call | flops 17301504 | bytes 1048576 | tf_op jit(solution)/shard_map/phases/pallas_call | solution.py:156
  21.7 14.9 %phases.5 = f32[1,1408]{1,0:T(1,128)S(1)} custom-call(bf16[512,48]{1,0:T(8,128)(2,1)S(1)} %copy.21.refs_0_, f32[128,128]{1,0:T(8,128)S(1)} %broadcast_in_dim.10.refs_1_, f32[16,128]{1,0:T(8,128)S(1)} %pad.9.refs_2_, f32[8,2048]{1,0:T(8,128)S(1)} %collective-permute-done.4.refs_3_, f32[8,2048]{1,0:T(8,128)S(1)} %collective-permute-done.5.refs_4_, ...), custom_call_target="tpu_custom_call" | custom-call | flops 69206016 | bytes 1048576 | tf_op jit(solution)/shard_map/phases/pallas_call | solution.py:156
  37.4 9.3 %all-to-all-start = ((f32[32,1,1408]{2,1,0:T(1,128)}), f32[32,1,1408]{2,1,0:T(1,128)S(1)}, u32[]{:S(2)}, u32[]{:S(2)}) async-start(f32[32,1,1408]{2,1,0:T(1,128)} %broadcast_in_dim.26), calls=%async_computation | async-start | bytes 360448 | tf_op jit(solution)/shard_map/all_to_all | solution.py:351
  46.8 10.2 %all-to-all-done = f32[32,1,1408]{2,1,0:T(1,128)S(1)} async-done(((f32[32,1,1408]{2,1,0:T(1,128)}), f32[32,1,1408]{2,1,0:T(1,128)S(1)}, u32[]{:S(2)}, u32[]{:S(2)}) %all-to-all-start) | async-done | bytes 180256 | tf_op jit(solution)/shard_map/all_to_all | solution.py:351
  57.0 3.7 %collective-permute-start.10 = (f32[32,1408]{1,0:T(8,128)S(1)}, f32[32,1408]{1,0:T(8,128)S(1)}, u32[]{:S(2)}, u32[]{:S(2)}) collective-permute-start(f32[32,1408]{1,0:T(8,128)S(1)} %bitcast.31), channel_id=1, source_target_pairs={{0,8},{8,0},{16,24},{24,16},{32,40},{40,32},{48,56},{56,48},{64,72... | collective-permute-start | bytes 540680 | tf_op jit(solution)/shard_map/ppermute | solution.py:308
  60.7 2.0 %collective-permute-start.9 = (f32[32,1408]{1,0:T(8,128)S(1)}, f32[32,1408]{1,0:T(8,128)S(1)}, u32[]{:S(2)}, u32[]{:S(2)}) collective-permute-start(f32[32,1408]{1,0:T(8,128)S(1)} %bitcast.32), channel_id=1, source_target_pairs={{0,192},{8,200},{16,208},{24,216},{32,224},{40,232},{48,240},{56,2... | collective-permute-start | bytes 540680 | tf_op jit(solution)/shard_map/ppermute | solution.py:308
  62.7 1.6 %collective-permute-start.8 = (f32[32,1408]{1,0:T(8,128)S(1)}, f32[32,1408]{1,0:T(8,128)S(1)}, u32[]{:S(2)}, u32[]{:S(2)}) collective-permute-start(f32[32,1408]{1,0:T(8,128)S(1)} %bitcast.33), channel_id=1, source_target_pairs={{0,128},{8,136},{16,144},{24,152},{32,160},{40,168},{48,176},{56,1... | collective-permute-start | bytes 540680 | tf_op jit(solution)/shard_map/ppermute | solution.py:308
  64.2 1.3 %scatter.8.refs_0_ = f32[128,32,128]{2,1,0:T(8,128)S(1)} custom-call(s32[4]{0:T(128)S(1)} %pad_add_fusion.own_ref, f32[32,1408]{1,0:T(8,128)S(1)} %bitcast.35), custom_call_target="tpu_custom_call" | custom-call | flops 2147483648 | bytes 1048576 | tf_op jit(solution)/shard_map/scatter/pallas_call | solution.py:218
  65.5 6.6 %collective-permute-done.7.p_ref = f32[32,1408]{1,0:T(8,128)S(1)} collective-permute-done((f32[32,1408]{1,0:T(8,128)S(1)}, f32[32,1408]{1,0:T(8,128)S(1)}, u32[]{:S(2)}, u32[]{:S(2)}) %collective-permute-start.7) | collective-permute-done | bytes 180256 | tf_op jit(solution)/shard_map/ppermute | solution.py:308
  73.3 1.3 %scatter.9.refs_1_ = f32[128,32,128]{2,1,0:T(8,128)S(1)} custom-call(s32[4]{0:T(128)S(1)} %pad_add_fusion.own_ref, f32[32,1408]{1,0:T(8,128)S(1)} %collective-permute-done.7.p_ref), custom_call_target="tpu_custom_call" | custom-call | flops 2147483648 | bytes 1048576 | tf_op jit(solution)/shard_map/scatter/pallas_call | solution.py:218
  74.7 1.3 %scatter.10.refs_2_ = f32[128,32,128]{2,1,0:T(8,128)S(1)} custom-call(s32[4]{0:T(128)S(1)} %pad_add_fusion.own_ref, f32[32,1408]{1,0:T(8,128)S(1)} %collective-permute-done.8.p_ref), custom_call_target="tpu_custom_call" | custom-call | flops 2147483648 | bytes 1048576 | tf_op jit(solution)/shard_map/scatter/pallas_call | solution.py:218
  77.9 1.3 %scatter.12.refs_4_ = f32[128,32,128]{2,1,0:T(8,128)S(1)} custom-call(s32[4]{0:T(128)S(1)} %pad_add_fusion.own_ref, f32[32,1408]{1,0:T(8,128)S(1)} %collective-permute-done.10.p_ref), custom_call_target="tpu_custom_call" | custom-call | flops 2147483648 | bytes 1048576 | tf_op jit(solution)/shard_map/scatter/pallas_call | solution.py:218
  79.2 1.3 %scatter.13.refs_5_ = f32[128,32,128]{2,1,0:T(8,128)S(1)} custom-call(s32[4]{0:T(128)S(1)} %pad_add_fusion.own_ref, f32[32,1408]{1,0:T(8,128)S(1)} %collective-permute-done.11.p_ref), custom_call_target="tpu_custom_call" | custom-call | flops 2147483648 | bytes 1048576 | tf_op jit(solution)/shard_map/scatter/pallas_call | solution.py:218
  80.5 1.3 %scatter.14.refs_6_ = f32[128,32,128]{2,1,0:T(8,128)S(1)} custom-call(s32[4]{0:T(128)S(1)} %pad_add_fusion.own_ref, f32[32,1408]{1,0:T(8,128)S(1)} %collective-permute-done.12.p_ref), custom_call_target="tpu_custom_call" | custom-call | flops 2147483648 | bytes 1048576 | tf_op jit(solution)/shard_map/scatter/pallas_call | solution.py:218
  81.8 1.3 %copy-done.1 = f32[128,32,128]{2,1,0:T(8,128)} copy-done((f32[128,32,128]{2,1,0:T(8,128)}, f32[128,32,128]{2,1,0:T(8,128)S(1)}, u32[]{:S(2)}) %copy-start.1) | copy-done | bytes 2097176
  83.2 1.3 %scatter.15.refs_7_ = f32[128,32,128]{2,1,0:T(8,128)S(1)} custom-call(s32[4]{0:T(128)S(1)} %pad_add_fusion.own_ref, f32[32,1408]{1,0:T(8,128)S(1)} %collective-permute-done.13.p_ref), custom_call_target="tpu_custom_call" | custom-call | flops 2147483648 | bytes 1048576 | tf_op jit(solution)/shard_map/scatter/pallas_call | solution.py:218
  84.5 1.3 %copy-done.2 = f32[128,32,128]{2,1,0:T(8,128)} copy-done((f32[128,32,128]{2,1,0:T(8,128)}, f32[128,32,128]{2,1,0:T(8,128)S(1)}, u32[]{:S(2)}) %copy-start.2) | copy-done | bytes 2097176
  85.8 10.2 %transform.1 = f32[4,32,8,256]{3,2,1,0:T(8,128)} custom-call(s32[4]{0:T(128)S(1)} %pad_add_fusion.own_ref, f32[128,32,128]{2,1,0:T(8,128)S(1)} %scatter.8.refs_0_, f32[128,32,128]{2,1,0:T(8,128)S(1)} %scatter.9.refs_1_, f32[128,32,128]{2,1,0:T(8,128)S(1)} %scatter.10.refs_2_, f32[128,32,128]{2,1,0:T(8,128)S(1)} %scatter.11.refs_3_, ...), custom_call_target="tpu_custom_call" | custom-call | tf_op jit(solution)/shard_map/transform/pallas_call | solution.py:295
  (59 shorter events, 9.1 us)
Async XLA Ops:
  0.0 4.1 %copy-start = (s32[3,1,4096]{2,1,0:T(1,128)S(1)}, s32[3,1,4096]{2,1,0:T(1,128)}, u32[]{:S(2)}) copy-start(s32[3,1,4096]{2,1,0:T(1,128)} %param.11) | copy-start | bytes 147460
  0.0 21.7 %copy-start.4 = (f32[2,1,128]{2,1,0:T(1,128)S(1)}, f32[2,1,128]{2,1,0:T(1,128)}, u32[]{:S(2)}) copy-start(f32[2,1,128]{2,1,0:T(1,128)} %param.12) | copy-start | bytes 3076
  0.8 5.4 %collective-permute-start = (f32[8,256]{1,0:T(8,128)S(1)}, f32[8,256]{1,0:T(8,128)S(1)}, u32[]{:S(2)}, u32[]{:S(2)}) collective-permute-start(f32[8,256]{1,0:T(8,128)S(1)} %get-tuple-element.5), channel_id=1, source_target_pairs={{0,8},{8,0},{16,24},{24,16},{32,40},{40,32},{48,56},{56,48},{64,72... | collective-permute-start | bytes 24584 | tf_op jit(solution)/shard_map/ppermute | solution.py:308
  6.9 5.8 %collective-permute-start.3 = (f32[8,512]{1,0:T(8,128)S(1)}, f32[8,512]{1,0:T(8,128)S(1)}, u32[]{:S(2)}, u32[]{:S(2)}) collective-permute-start(f32[8,512]{1,0:T(8,128)S(1)} %pad_maximum_fusion.1.refs_3_), channel_id=1, source_target_pairs={{0,32},{8,40},{16,48},{24,56},{32,0},{40,8},{48,16},{56,24},{64,96... | collective-permute-start | bytes 49160 | tf_op jit(solution)/shard_map/ppermute | solution.py:308
  8.2 4.4 %collective-permute-start.2 = (f32[8,512]{1,0:T(8,128)S(1)}, f32[8,512]{1,0:T(8,128)S(1)}, u32[]{:S(2)}, u32[]{:S(2)}) collective-permute-start(f32[8,512]{1,0:T(8,128)S(1)} %pad_maximum_fusion.1.refs_3_), channel_id=1, source_target_pairs={{0,48},{8,56},{16,32},{24,40},{32,16},{40,24},{48,0},{56,8},{64,11... | collective-permute-start | bytes 49160 | tf_op jit(solution)/shard_map/ppermute | solution.py:308
  9.7 2.6 %collective-permute-start.1 = (f32[8,512]{1,0:T(8,128)S(1)}, f32[8,512]{1,0:T(8,128)S(1)}, u32[]{:S(2)}, u32[]{:S(2)}) collective-permute-start(f32[8,512]{1,0:T(8,128)S(1)} %pad_maximum_fusion.1.refs_3_), channel_id=1, source_target_pairs={{0,16},{8,24},{16,0},{24,8},{32,48},{40,56},{48,32},{56,40},{64,80... | collective-permute-start | bytes 49160 | tf_op jit(solution)/shard_map/ppermute | solution.py:308
  12.6 9.0 %collective-permute-start.6 = (f32[8,2048]{1,0:T(8,128)S(1)}, f32[8,2048]{1,0:T(8,128)S(1)}, u32[]{:S(2)}, u32[]{:S(2)}) collective-permute-start(f32[8,2048]{1,0:T(8,128)S(1)} %constant_dynamic-update-slice_fusion), channel_id=1, source_target_pairs={{0,128},{8,136},{16,144},{24,152},{32,160},{40,168},{48,176},{56,1... | collective-permute-start | bytes 196616 | tf_op jit(solution)/shard_map/ppermute | solution.py:308
  15.6 6.0 %collective-permute-start.5 = (f32[8,2048]{1,0:T(8,128)S(1)}, f32[8,2048]{1,0:T(8,128)S(1)}, u32[]{:S(2)}, u32[]{:S(2)}) collective-permute-start(f32[8,2048]{1,0:T(8,128)S(1)} %constant_dynamic-update-slice_fusion), channel_id=1, source_target_pairs={{0,192},{8,200},{16,208},{24,216},{32,224},{40,232},{48,240},{56,2... | collective-permute-start | bytes 196616 | tf_op jit(solution)/shard_map/ppermute | solution.py:308
  16.4 5.3 %collective-permute-start.4 = (f32[8,2048]{1,0:T(8,128)S(1)}, f32[8,2048]{1,0:T(8,128)S(1)}, u32[]{:S(2)}, u32[]{:S(2)}) collective-permute-start(f32[8,2048]{1,0:T(8,128)S(1)} %constant_dynamic-update-slice_fusion), channel_id=1, source_target_pairs={{0,64},{8,72},{16,80},{24,88},{32,96},{40,104},{48,112},{56,120},{... | collective-permute-start | bytes 196616 | tf_op jit(solution)/shard_map/ppermute | solution.py:308
  37.4 19.5 %all-to-all-start = ((f32[32,1,1408]{2,1,0:T(1,128)}), f32[32,1,1408]{2,1,0:T(1,128)S(1)}, u32[]{:S(2)}, u32[]{:S(2)}) async-start(f32[32,1,1408]{2,1,0:T(1,128)} %broadcast_in_dim.26), calls=%async_computation | async-start | bytes 360448 | tf_op jit(solution)/shard_map/all_to_all | solution.py:351
  57.0 20.9 %collective-permute-start.10 = (f32[32,1408]{1,0:T(8,128)S(1)}, f32[32,1408]{1,0:T(8,128)S(1)}, u32[]{:S(2)}, u32[]{:S(2)}) collective-permute-start(f32[32,1408]{1,0:T(8,128)S(1)} %bitcast.31), channel_id=1, source_target_pairs={{0,8},{8,0},{16,24},{24,16},{32,40},{40,32},{48,56},{56,48},{64,72... | collective-permute-start | bytes 540680 | tf_op jit(solution)/shard_map/ppermute | solution.py:308
  60.7 15.4 %collective-permute-start.9 = (f32[32,1408]{1,0:T(8,128)S(1)}, f32[32,1408]{1,0:T(8,128)S(1)}, u32[]{:S(2)}, u32[]{:S(2)}) collective-permute-start(f32[32,1408]{1,0:T(8,128)S(1)} %bitcast.32), channel_id=1, source_target_pairs={{0,192},{8,200},{16,208},{24,216},{32,224},{40,232},{48,240},{56,2... | collective-permute-start | bytes 540680 | tf_op jit(solution)/shard_map/ppermute | solution.py:308
  62.7 12.0 %collective-permute-start.8 = (f32[32,1408]{1,0:T(8,128)S(1)}, f32[32,1408]{1,0:T(8,128)S(1)}, u32[]{:S(2)}, u32[]{:S(2)}) collective-permute-start(f32[32,1408]{1,0:T(8,128)S(1)} %bitcast.33), channel_id=1, source_target_pairs={{0,128},{8,136},{16,144},{24,152},{32,160},{40,168},{48,176},{56,1... | collective-permute-start | bytes 540680 | tf_op jit(solution)/shard_map/ppermute | solution.py:308
  64.2 7.9 %collective-permute-start.7 = (f32[32,1408]{1,0:T(8,128)S(1)}, f32[32,1408]{1,0:T(8,128)S(1)}, u32[]{:S(2)}, u32[]{:S(2)}) collective-permute-start(f32[32,1408]{1,0:T(8,128)S(1)} %bitcast.34), channel_id=1, source_target_pairs={{0,64},{8,72},{16,80},{24,88},{32,96},{40,104},{48,112},{56,120},{... | collective-permute-start | bytes 540680 | tf_op jit(solution)/shard_map/ppermute | solution.py:308
  72.2 7.1 %collective-permute-start.11 = (f32[32,1408]{1,0:T(8,128)S(1)}, f32[32,1408]{1,0:T(8,128)S(1)}, u32[]{:S(2)}, u32[]{:S(2)}) collective-permute-start(f32[32,1408]{1,0:T(8,128)S(1)} %collective-permute-done.7.p_ref), channel_id=1, source_target_pairs={{0,8},{8,0},{16,24},{24,16},{32,40},{40,32},{48,56},{56,48},{64,72... | collective-permute-start | bytes 540680 | tf_op jit(solution)/shard_map/ppermute | solution.py:308
  74.6 5.9 %collective-permute-start.12 = (f32[32,1408]{1,0:T(8,128)S(1)}, f32[32,1408]{1,0:T(8,128)S(1)}, u32[]{:S(2)}, u32[]{:S(2)}) collective-permute-start(f32[32,1408]{1,0:T(8,128)S(1)} %collective-permute-done.8.p_ref), channel_id=1, source_target_pairs={{0,8},{8,0},{16,24},{24,16},{32,40},{40,32},{48,56},{56,48},{64,72... | collective-permute-start | bytes 540680 | tf_op jit(solution)/shard_map/ppermute | solution.py:308
  76.0 7.1 %collective-permute-start.13 = (f32[32,1408]{1,0:T(8,128)S(1)}, f32[32,1408]{1,0:T(8,128)S(1)}, u32[]{:S(2)}, u32[]{:S(2)}) collective-permute-start(f32[32,1408]{1,0:T(8,128)S(1)} %collective-permute-done.9.p_ref), channel_id=1, source_target_pairs={{0,8},{8,0},{16,24},{24,16},{32,40},{40,32},{48,56},{56,48},{64,72... | collective-permute-start | bytes 540680 | tf_op jit(solution)/shard_map/ppermute | solution.py:308
  81.8 1.3 %copy-start.1 = (f32[128,32,128]{2,1,0:T(8,128)}, f32[128,32,128]{2,1,0:T(8,128)S(1)}, u32[]{:S(2)}) copy-start(f32[128,32,128]{2,1,0:T(8,128)S(1)} %scatter.14.refs_6_) | copy-start | bytes 6291460
  83.2 2.6 %copy-start.3 = (bf16[2,512,256]{2,1,0:T(8,128)(2,1)S(1)}, bf16[2,512,256]{2,1,0:T(8,128)(2,1)}, u32[]{:S(2)}) copy-start(bf16[2,512,256]{2,1,0:T(8,128)(2,1)} %constant.50.clone.refs_8_) | copy-start | bytes 1572868
  84.5 1.3 %copy-start.2 = (f32[128,32,128]{2,1,0:T(8,128)}, f32[128,32,128]{2,1,0:T(8,128)S(1)}, u32[]{:S(2)}) copy-start(f32[128,32,128]{2,1,0:T(8,128)S(1)} %scatter.15.refs_7_) | copy-start | bytes 6291460

commit v3 on v2

--- a/solution.py
+++ b/solution.py
@@ -12,19 +12,17 @@
 G = 256
 TILE = 256
 LOG2E = math.log2(math.e)
+PLANE = 32
 ROWS = 11
 
 SIN_C = (3.141592640183972, -5.167710090328514, 2.550077659663962, -0.5982921590533228, 0.07765940739590604)
 COS_C = (0.9999999534665512, -4.934792858660287, 4.058411913867176, -1.3318801593277205, 0.21969679475921783)
 
 
-def rotations(angle_batch):
-    cos_first = jnp.cos(angle_batch[0])
-    sin_first = jnp.sin(angle_batch[0])
-    cos_tilt = jnp.cos(angle_batch[1])
-    sin_tilt = jnp.sin(angle_batch[1])
-    cos_last = jnp.cos(angle_batch[2])
-    sin_last = jnp.sin(angle_batch[2])
+def rotation_columns(angles):
+    cosine, sine = jnp.cos(angles), jnp.sin(angles)
+    cos_first, cos_tilt, cos_last = (cosine[:, q : q + 1] for q in range(3))
+    sin_first, sin_tilt, sin_last = (sine[:, q : q + 1] for q in range(3))
     top_row = [
         cos_first * cos_tilt * cos_last - sin_first * sin_last,
         -cos_first * cos_tilt * sin_last - sin_first * cos_last,
@@ -36,7 +34,12 @@
         sin_first * sin_tilt,
     ]
     low_row = [-sin_tilt * cos_last, sin_tilt * sin_last, cos_tilt]
-    return jnp.stack([jnp.stack(top_row), jnp.stack(mid_row), jnp.stack(low_row)])
+    row = lax.broadcasted_iota(jnp.int32, (16, 1), 0)
+    low_row = [jnp.where(row < 12, low, 0.0) for low in low_row]
+    return [
+        jnp.where(row < 4, top, jnp.where(row < 8, mid, low))
+        for top, mid, low in zip(top_row, mid_row, low_row)
+    ]
 
 
 def monic(coefs):
@@ -72,7 +75,7 @@
     return hi, lo
 
 
-def phase_kernel(n_in, first, last, scales, *refs):
+def phase_kernel(n_in, skip, first, last, scales, *refs):
     lhs_ref, s2_ref, rc_ref = refs[:3]
     atom_refs = refs[3 : 3 + n_in]
     pos = 3 + n_in
@@ -84,51 +87,73 @@
         pos += 2
     out_ref = refs[pos]
     pos += 1
+    if first:
+        rc_out = refs[pos]
+        pos += 1
     if last:
         acc_ref = refs[pos]
         pos += 1
     else:
         acc_ref = out_ref
-    turns_ref = refs[pos]
+    even_ref, odd_ref = refs[pos : pos + 2]
 
     if first:
         acc_ref[...] = jnp.zeros_like(acc_ref)
     else:
         acc_ref[...] = acc_in[...]
 
-    rc0, rc1, rc2 = rc_ref[:, 0:1], rc_ref[:, 1:2], rc_ref[:, 2:3]
+    if first:
+        rc0, rc1, rc2 = rotation_columns(rc_ref[...])
+        for q, column in enumerate((rc0, rc1, rc2)):
+            rc_out[:, q : q + 1] = column
+    else:
+        rc0, rc1, rc2 = rc_ref[:, 0:1], rc_ref[:, 1:2], rc_ref[:, 2:3]
     lhs = lhs_ref[...]
 
+    def set_turns(a_ref, i, turns_ref):
+        a = a_ref[:, pl.ds(pl.multiple_of(i * TILE, TILE), TILE)]
+        placed = rc0 * a[0:1] + rc1 * a[1:2] + rc2 * a[2:3]
+        p1 = placed.astype(jnp.bfloat16)
+        rest = placed - p1.astype(jnp.float32)
+        p2 = rest.astype(jnp.bfloat16)
+        p3 = (rest - p2.astype(jnp.float32)).astype(jnp.bfloat16)
+        rhs = jnp.concatenate([p1, p2, p3], axis=0)
+        turns_ref[...] = jnp.dot(lhs, rhs, preferred_element_type=jnp.float32)
+
+    def add_tile(a_ref, i, turns_ref):
+        a = a_ref[:, pl.ds(pl.multiple_of(i * TILE, TILE), TILE)]
+        for nb in range(16):
+            rows = slice(nb * 8, nb * 8 + 8)
+            s2 = s2_ref[rows, :]
+            amps = []
+            for part in range(TILE // 128):
+                lanes = slice(part * 128, part * 128 + 128)
+                amps.append(a[3:4, lanes] * jnp.exp2(a[4:5, lanes] * s2))
+            acc_ref[8, rows, :] += sum(amps[1:], amps[0])
+            for r in range(4):
+                ms = mc = None
+                for part in range(TILE // 128):
+                    lanes = slice(part * 128, part * 128 + 128)
+                    s, c = half_angle(turns_ref[r * 128 + nb * 8 : r * 128 + nb * 8 + 8, lanes])
+                    m = amps[part] * s
+                    ms = m * s if ms is None else ms + m * s
+                    mc = m * c if mc is None else mc + m * c
+                acc_ref[r, rows, :] += ms
+                acc_ref[4 + r, rows, :] += mc
+
     for a_ref in atom_refs:
-
-        @pl.loop(0, a_ref.shape[1] // TILE)
-        def _(i):
-            a = a_ref[:, pl.ds(pl.multiple_of(i * TILE, TILE), TILE)]
-            placed = rc0 * a[0:1] + rc1 * a[1:2] + rc2 * a[2:3]
-            p1 = placed.astype(jnp.bfloat16)
-            rest = placed - p1.astype(jnp.float32)
-            p2 = rest.astype(jnp.bfloat16)
-            p3 = (rest - p2.astype(jnp.float32)).astype(jnp.bfloat16)
-            rhs = jnp.concatenate([p1, p2, p3], axis=0)
-            turns_ref[...] = jnp.dot(lhs, rhs, preferred_element_type=jnp.float32)
-            for nb in range(16):
-                rows = slice(nb * 8, nb * 8 + 8)
-                s2 = s2_ref[rows, :]
-                amps = []
-                for half in range(2):
-                    lanes = slice(half * 128, half * 128 + 128)
-                    amps.append(a[3:4, lanes] * jnp.exp2(a[4:5, lanes] * s2))
-                acc_ref[8, rows, :] += amps[0] + amps[1]
-                for r in range(4):
-                    ms = mc = None
-                    for half in range(2):
-                        lanes = slice(half * 128, half * 128 + 128)
-                        s, c = half_angle(turns_ref[r * 128 + nb * 8 : r * 128 + nb * 8 + 8, lanes])
-                        m = amps[half] * s
-                        ms = m * s if ms is None else ms + m * s
-                        mc = m * c if mc is None else mc + m * c
-                    acc_ref[r, rows, :] += ms
-                    acc_ref[4 + r, rows, :] += mc
+        begin, tiles = skip // TILE, a_ref.shape[1] // TILE
+        set_turns(a_ref, begin, even_ref)
+        if tiles == begin + 1:
+            add_tile(a_ref, begin, even_ref)
+        else:
+
+            @pl.loop(begin // 2, tiles // 2)
+            def _(i):
+                set_turns(a_ref, 2 * i + 1, odd_ref)
+                add_tile(a_ref, 2 * i, even_ref)
+                set_turns(a_ref, jnp.minimum(2 * i + 2, tiles - 1), even_ref)
+                add_tile(a_ref, 2 * i + 1, odd_ref)
 
     if last:
         atom_scale, refl_scale = scales
@@ -141,23 +166,26 @@
             reals.append((obs0 * f_re + obs1 * f_im) * refl_scale)
             imags.append((obs1 * f_re - obs0 * f_im) * refl_scale)
         for q, row in enumerate(reals + imags + [ind_ref[q : q + 1, :] for q in range(3)]):
-            out_ref[0:1, q * 128 : q * 128 + 128] = row
-
-
-def phase_call(lhs, s2, rc, atoms, acc, obs, indices, scales):
+            out_ref[:, q * 128 : q * 128 + 128] = jnp.broadcast_to(row, (out_ref.shape[0], 128))
+
+
+def phase_call(lhs, s2, rc, atoms, skip, acc, obs, indices, scales):
     first, last = acc is None, obs is not None
     operands = [lhs, s2, rc, *atoms] + ([] if first else [acc]) + ([obs, indices] if last else [])
     acc_shape = (9, 128, 128)
-    scratch = [pltpu.VMEM((512, TILE), jnp.float32)]
+    scratch = [pltpu.VMEM((512, TILE), jnp.float32)] * 2
     if last:
         scratch = [pltpu.VMEM(acc_shape, jnp.float32)] + scratch
-    out = jax.ShapeDtypeStruct((1, ROWS * 128) if last else acc_shape, jnp.float32)
-    count = sum(a.shape[1] for a in atoms)
+    vmem = pl.BlockSpec(memory_space=pltpu.VMEM)
+    out, out_specs = jax.ShapeDtypeStruct((PLANE, ROWS * 128) if last else acc_shape, jnp.float32), vmem
+    if first:
+        out, out_specs = (out, jax.ShapeDtypeStruct((16, 128), jnp.float32)), (vmem, vmem)
+    count = sum(a.shape[1] for a in atoms) - skip
     return pl.pallas_call(
-        functools.partial(phase_kernel, len(atoms), first, last, scales),
+        functools.partial(phase_kernel, len(atoms), skip, first, last, scales),
         out_shape=out,
-        in_specs=[pl.BlockSpec(memory_space=pltpu.VMEM)] * len(operands),
-        out_specs=pl.BlockSpec(memory_space=pltpu.VMEM),
+        in_specs=[vmem] * len(operands),
+        out_specs=out_specs,
         scratch_shapes=scratch,
         compiler_params=pltpu.CompilerParams(vmem_limit_bytes=16 << 20),
         cost_estimate=pl.CostEstimate(
@@ -167,25 +195,26 @@
     )(*operands)
 
 
-def scatter_kernel(piece, own_ref, p_ref, x_ref):
-    y, core = own_ref[0] ^ (piece & 3), own_ref[1] ^ (piece >> 2)
+def scatter_kernel(other, step, own_ref, p_ref, x_ref):
+    core, y, own_j = own_ref[0:1] ^ other, own_ref[3:4] ^ step, own_ref[2:3]
     cells = lax.broadcasted_iota(jnp.int32, (128, 128), 0).astype(jnp.float32)
-    w_turn = (lax.broadcasted_iota(jnp.int32, (8, 128), 0) + own_ref[3] * 8).astype(
+    w_turn = (lax.broadcasted_iota(jnp.int32, (8, 128), 0) + own_j * 8).astype(
         jnp.float32
     ) * (1.0 / G)
     sub = lax.broadcasted_iota(jnp.int32, (8, 128), 0)
-    for base in range(0, 32, 8):
+    for base in range(0, PLANE, 8):
+        x = base // 8
         h = p_ref[base : base + 8, 8 * 128 : 9 * 128]
         k = p_ref[base : base + 8, 9 * 128 : 10 * 128]
         third = p_ref[base : base + 8, 10 * 128 : 11 * 128]
-        h = jnp.where(h < 0.0, h + G, h) - ((base + sub) // 4 * 32).astype(jnp.float32)
+        h = jnp.where(h < 0.0, h + G, h) - (((sub >> 2) * 4 + x) * 32).astype(jnp.float32)
         k = jnp.where(k < 0.0, k + G, k) - (((y * 4 + (sub & 3)) * 2 + core) * 8).astype(jnp.float32)
         pair = jnp.floor(h * 0.5)
         odd = h - 2.0 * pair
         row = pair * 8.0 + k
         for q in range(8):
             i = base + q
-            g, z_lo = i // 4, i % 4
+            g, line = q // 4 * 4 + x, q % 4 * 8
             one_hot = jnp.where(cells == row[q : q + 1], 1.0, 0.0).astype(jnp.bfloat16)
             sine, cosine = sincos_turns(third[q : q + 1] * w_turn)
             reals, imags = [], []
@@ -210,25 +239,25 @@
                 (((1,), (1,)), ((), ())),
                 preferred_element_type=jnp.float32,
             )
-            x_ref[g * 16 : g * 16 + 16, z_lo * 8 : z_lo * 8 + 8, :] = total.reshape(16, 8, 128)
-
-
-def scatter_call(piece, own, payload):
+            x_ref[g * 16 : g * 16 + 16, line : line + 8, :] = total.reshape(16, 8, 128)
+
+
+def scatter_call(other, step, own, plane):
     vmem = pl.BlockSpec(memory_space=pltpu.VMEM)
     return pl.pallas_call(
-        functools.partial(scatter_kernel, piece),
+        functools.partial(scatter_kernel, other, step),
         out_shape=jax.ShapeDtypeStruct((128, 32, 128), jnp.float32),
-        in_specs=[pl.BlockSpec(memory_space=pltpu.SMEM), vmem],
+        in_specs=[vmem] * 2,
         out_specs=vmem,
         compiler_params=pltpu.CompilerParams(vmem_limit_bytes=16 << 20),
-        cost_estimate=pl.CostEstimate(flops=2 << 30, bytes_accessed=1 << 20, transcendentals=0),
+        cost_estimate=pl.CostEstimate(flops=1 << 29, bytes_accessed=1 << 20, transcendentals=0),
         name="scatter",
-    )(own, payload)
+    )(own, plane)
 
 
 def transform_kernel(own_ref, *refs):
     x_refs, (d_ref, out_ref, z_ref) = refs[:8], refs[8:]
-    own_y, own_core, own_g = own_ref[0], own_ref[1], own_ref[2]
+    own_core, own_g, own_y = (jnp.concatenate([own_ref[q : q + 1]] * 2, axis=1) for q in (0, 1, 3))
     column = lax.broadcasted_iota(jnp.int32, (32, G), 1)
     y, core = own_y ^ ((column >> 5) & 3), own_core ^ (column >> 7)
     k = ((y * 4 + ((column >> 3) & 3)) * 2 + core) * 8 + (column & 7)
@@ -295,10 +324,10 @@
     return pl.pallas_call(
         transform_kernel,
         out_shape=jax.ShapeDtypeStruct((4, 32, 8, G), jnp.float32),
-        in_specs=[pl.BlockSpec(memory_space=pltpu.SMEM)] + [vmem] * 9,
+        in_specs=[vmem] * 10,
         out_specs=vmem,
         scratch_shapes=[pltpu.VMEM((32 * 128, 128), jnp.float32)],
-        compiler_params=pltpu.CompilerParams(vmem_limit_bytes=40 << 20),
+        compiler_params=pltpu.CompilerParams(vmem_limit_bytes=8 << 20),
         name="transform",
     )(own, *pieces, first)
 
@@ -308,12 +337,32 @@
     return lax.ppermute(x, axis, [(i, i ^ mask) for i in range(count)])
 
 
-def column_groups():
+def flat(y, z, core, x):
+    return ((y * 4 + z % 4) * 2 + core) * 8 + z // 4 * 4 + x
+
+
+def plane_groups():
     return [
-        [((y * 4 + z_lo) * 2 + core) * 8 + g for g in range(8) for z_lo in range(4)]
-        for y in range(4)
-        for core in range(2)
+        [flat(y, z, core, x) for x in range(4) for z in range(8)] for y in range(4) for core in range(2)
     ]
+
+
+def join_kernel(a_ref, b_ref, out_ref):
+    size = a_ref.shape[1]
+    out_ref[:, :size] = a_ref[...]
+    out_ref[:, size:] = b_ref[...]
+
+
+def join(a, b):
+    vmem = pl.BlockSpec(memory_space=pltpu.VMEM)
+    return pl.pallas_call(
+        join_kernel,
+        out_shape=jax.ShapeDtypeStruct((a.shape[0], 2 * a.shape[1]), jnp.float32),
+        in_specs=[vmem, vmem],
+        out_specs=vmem,
+        compiler_params=pltpu.CompilerParams(vmem_limit_bytes=4 << 20),
+        name="join",
+    )(a, b)
 
 
 def shards(coords, weights, thermal, angles, miller, observed):
@@ -327,10 +376,7 @@
         1.0 / math.sqrt(own_count * atom_count * refl_count),
     )
     atoms = jnp.concatenate([coords, weights[None], thermal[None], jnp.zeros_like(coords)], axis=0)
-    atoms = jnp.concatenate([atoms, swap(atoms, "atom", 1)], axis=1)
-    near = [swap(atoms, "atom", mask) for mask in (2, 6, 4)]
-    run = jnp.concatenate([atoms, *near], axis=1)
-    far = [swap(run, "atom", mask) for mask in (8, 24, 16)]
+    atoms = join(atoms, swap(atoms, "atom", 1))
 
     own_miller = lax.dynamic_slice_in_dim(miller[:, 0, :], j * own_count, own_count, 1)
     indices = own_miller.astype(jnp.float32)
@@ -339,29 +385,30 @@
     lhs = indices.T[None, :, :, None] * jnp.eye(4, dtype=jnp.float32)[:, None, None, :]
     lhs = jnp.pad(lhs.reshape(4 * own_count, 12), ((0, 0), (0, 4)))
     lhs = jnp.concatenate([lhs, lhs, lhs], axis=1).astype(jnp.bfloat16)
-    matrices = rotations(angles)
-    rc = jnp.transpose(matrices, (0, 2, 1)).reshape(12, 3)
-    rc = jnp.pad(rc, ((0, 4), (0, 125)))
-
-    acc = phase_call(lhs, s2, rc, [atoms], None, None, None, scales)
-    acc = phase_call(lhs, s2, rc, near, acc, None, None, scales)
-    payload = phase_call(lhs, s2, rc, far, acc, observed[:, 0, :], indices, scales)
-
-    own = jnp.stack([j // 8, j % 2, g, j]).astype(jnp.int32)
+    rc = jnp.pad(jnp.tile(angles.T, (3, 1)), ((0, 4), (0, 0)))
+    y, core = j // 8, j % 2
+    own = jnp.stack([core, g, j, y]).astype(jnp.int32)
+    own = jnp.broadcast_to(own[:, None], (4, 128))
+    indices, observed, own, atoms = lax.optimization_barrier((indices, observed[:, 0, :], own, atoms))
+
+    acc, skip = None, 0
+    for mask in (2, 8, 4, 16):
+        more = swap(atoms, "atom", mask)
+        acc = phase_call(lhs, s2, rc, [atoms], skip, acc, None, None, scales)
+        if skip == 0:
+            acc, rc = acc
+        more, acc = lax.optimization_barrier((more, acc))
+        if mask != 16:
+            skip = atoms.shape[1]
+            atoms = join(atoms, more)
+    payload = phase_call(lhs, s2, rc, [more], 0, acc, observed, indices, scales)
+
     plane = lax.all_to_all(
-        jnp.broadcast_to(payload, (32, payload.shape[1])),
-        ("atom", "refl"),
-        0,
-        0,
-        tiled=True,
-        axis_index_groups=column_groups(),
+        payload, ("atom", "refl"), 0, 0, tiled=True, axis_index_groups=plane_groups()
     )
-    pieces = [plane] + [None] * 7
-    for m in (1, 3, 2):
-        pieces[m] = swap(plane, "atom", 8 * m)
-    for m in (0, 1, 3, 2):
-        pieces[4 + m] = swap(pieces[m], "atom", 1)
-    lines = [scatter_call(q, own, piece) for q, piece in enumerate(pieces)]
+    planes = [plane] + [swap(plane, "atom", 8 * step) for step in range(1, 4)]
+    planes += [swap(plane, "atom", 1) for plane in planes]
+    lines = [scatter_call(q // 4, q % 4, own, plane) for q, plane in enumerate(planes)]
     return transform_call(own, lines, first_table())
 
 

time: 96.3 us -> 77.2 us (0.80)
  blocking collectives: 0 us -> 18.7 us
  waiting for transfers between devices: 19.6 us -> 1.6 us
  Pallas kernels: 40.4 us -> 30.2 us
  starting transfers between devices: 28.4 us -> 23.9 us
  other arithmetic: 3.43 us -> 0.98 us
  local copies, waits for them, and re-layouts: 3.79 us -> 1.46 us
    all_to_all x0 -> x1, blocking collectives: none -> 18.7 us  [shards(): lax.all_to_all(payload, ('atom', 'refl'), 0, 0, tiled=True, axis_index_gr...]
    all_to_all x1 -> x0, waiting for transfers between devices: 10.2 us -> none  [shards(): lax.all_to_all(jnp.broadcast_to(payload, (32, payload.shape[1])), ('atom'...]
    all_to_all x1 -> x0, starting transfers between devices: 9.25 us -> none  [shards(): lax.all_to_all(jnp.broadcast_to(payload, (32, payload.shape[1])), ('atom'...]
    pallas_call x11 -> x17, Pallas kernels: 30.2 us -> 22.2 us  [the longest x5 16.2 us: phase_call(): pl.pallas_call(functools.partial(phase_kernel, len(atoms), skip, first, l...]
    ppermute x14 -> x12, waiting for transfers between devices: 9.42 us -> 1.6 us  [swap(): return lax.ppermute(x, axis, [(i, i ^ mask) for i in range(count)])]
    ppermute x14 -> x12, starting transfers between devices: 19.2 us -> 23.9 us  [swap(): return lax.ppermute(x, axis, [(i, i ^ mask) for i in range(count)])]
    unnamed x16 -> x9, local copies, waits for them, and re-layouts: 2.7 us -> 0.05 us
    pallas_call x1, Pallas kernels: 10.2 us -> 7.93 us  [transform_call(): pl.pallas_call(transform_kernel, out_shape=jax.ShapeDtypeStruct((4, 32, 8...]
  transfers between devices with their start and end apart: 15 -> 12, of which waited for: 4 -> 3; matrix products, arithmetic and copies ran while one was open for 2% -> 2% of each run, Pallas kernels for 15% -> 18%
where the time goes in v3:
time: 77.2 us; the launch traced here: 77 us
  Pallas kernels  30.2 us (39%)
  starting transfers between devices  23.9 us (31%)
  blocking collectives  18.7 us (24%)
  waiting for transfers between devices  1.6 us (2%)
  local copies, waits for them, and re-layouts  1.46 us (2%)
  other arithmetic  0.98 us (1%)
    ppermute x12, starting transfers between devices, swap(): return lax.ppermute(x, axis, [(i, i ^ mask) for i in range(count)])  23.9 us
    all_to_all x1, blocking collectives, shards(): lax.all_to_all(payload, ('atom', 'refl'), 0, 0, tiled=True, axis_index_gr...  18.7 us
    pallas_call x5, Pallas kernels, phase_call(): pl.pallas_call(functools.partial(phase_kernel, len(atoms), skip, first, l...  16.2 us
    pallas_call x1, Pallas kernels, transform_call(): pl.pallas_call(transform_kernel, out_shape=jax.ShapeDtypeStruct((4, 32, 8...  7.93 us
    pallas_call x8, Pallas kernels, scatter_call(): pl.pallas_call(functools.partial(scatter_kernel, other, step), out_shape=...  5.96 us
    ppermute x12, waiting for transfers between devices, swap(): return lax.ppermute(x, axis, [(i, i ^ mask) for i in range(count)])  1.6 us
  transfers between devices with their start and end apart: 12, of which 3 were waited for; matrix products, arithmetic and copies ran while one was open for 2% of the time, Pallas kernels for 18%

profile of v3, /device:TPU:1, one launch (start us, length us, event | category | flops | bytes accessed | tf_op | source)
XLA Modules:
  0.0 77.0 jit_solution(11938189824143936363)
XLA Ops:
  0.1 0.8 %maximum_maximum_fusion.a_ref = f32[8,256]{1,0:T(8,128)S(1)} fusion(f32[1,256]{1,0:T(1,128)} %bitcast.38, f32[1,256]{1,0:T(1,128)} %bitcast.39, f32[3,256]{1,0:T(4,128)} %param.7, f32[8]{0:T(128)S(1)} %pad.16.clone), kind=kLoop, calls=%fused_computation.4 | loop fusion | flops 6144 | bytes 13344 | tf_op jit(solution)/shard_map/concatenate | solution.py:378
  0.9 3.3 %collective-permute-start = (f32[8,256]{1,0:T(8,128)S(1)}, f32[8,256]{1,0:T(8,128)S(1)}, u32[]{:S(2)}, u32[]{:S(2)}) collective-permute-start(f32[8,256]{1,0:T(8,128)S(1)} %maximum_maximum_fusion.a_ref), channel_id=1, source_target_pairs={{0,8},{8,0},{16,24},{24,16},{32,40},{40,32},{48,56},{56,48},{64,72... | collective-permute-start | bytes 24584 | tf_op jit(solution)/shard_map/ppermute | solution.py:337
  6.1 1.2 %phases.5 = (f32[9,128,128]{2,1,0:T(8,128)S(1)}, f32[16,128]{1,0:T(8,128)S(1)}) custom-call(bf16[512,48]{1,0:T(8,128)(2,1)S(1)} %copy.20.refs_0_, f32[128,128]{1,0:T(8,128)S(1)} %broadcast_in_dim.27.refs_1_, f32[16,3]{1,0:T(8,128)S(1)} %pad.9.refs_2_, f32[8,512]{1,0:T(8,128)S(1)} %join.4.refs_3_.a_ref), custom_call_target="tpu_custom_call" | custom-call | flops 5767168 | bytes 1048576 | tf_op jit(solution)/shard_map/phases/pallas_call | solution.py:184
  7.6 1.0 %collective-permute-start.2 = (f32[8,1024]{1,0:T(8,128)S(1)}, f32[8,1024]{1,0:T(8,128)S(1)}, u32[]{:S(2)}, u32[]{:S(2)}) collective-permute-start(f32[8,1024]{1,0:T(8,128)S(1)} %join.5.refs_3_.a_ref), channel_id=1, source_target_pairs={{0,64},{8,72},{16,80},{24,88},{32,96},{40,104},{48,112},{56,120},{... | collective-permute-start | bytes 98312 | tf_op jit(solution)/shard_map/ppermute | solution.py:337
  8.6 1.0 %phases.6.refs_4_ = f32[9,128,128]{2,1,0:T(8,128)S(1)} custom-call(bf16[512,48]{1,0:T(8,128)(2,1)S(1)} %copy.20.refs_0_, f32[128,128]{1,0:T(8,128)S(1)} %broadcast_in_dim.27.refs_1_, f32[16,128]{1,0:T(8,128)S(1)} %get-tuple-element.21.refs_2_, f32[8,1024]{1,0:T(8,128)S(1)} %join.5.refs_3_.a_ref, f32[9,128,128]{2,1,0:T(8,128)S(1)} %get-tuple-element.24.refs_4_), custom_call_target="tpu_custom_call" | custom-call | flops 5767168 | bytes 1048576 | tf_op jit(solution)/shard_map/phases/pallas_call | solution.py:184
  10.4 2.7 %collective-permute-start.3 = (f32[8,2048]{1,0:T(8,128)S(1)}, f32[8,2048]{1,0:T(8,128)S(1)}, u32[]{:S(2)}, u32[]{:S(2)}) collective-permute-start(f32[8,2048]{1,0:T(8,128)S(1)} %join.6.refs_3_.a_ref), channel_id=1, source_target_pairs={{0,32},{8,40},{16,48},{24,56},{32,0},{40,8},{48,16},{56,24},{64,96... | collective-permute-start | bytes 196616 | tf_op jit(solution)/shard_map/ppermute | solution.py:337
  13.1 2.1 %phases.7.refs_4_ = f32[9,128,128]{2,1,0:T(8,128)S(1)} custom-call(bf16[512,48]{1,0:T(8,128)(2,1)S(1)} %copy.20.refs_0_, f32[128,128]{1,0:T(8,128)S(1)} %broadcast_in_dim.27.refs_1_, f32[16,128]{1,0:T(8,128)S(1)} %get-tuple-element.21.refs_2_, f32[8,2048]{1,0:T(8,128)S(1)} %join.6.refs_3_.a_ref, f32[9,128,128]{2,1,0:T(8,128)S(1)} %phases.6.refs_4_), custom_call_target="tpu_custom_call" | custom-call | flops 11534336 | bytes 1048576 | tf_op jit(solution)/shard_map/phases/pallas_call | solution.py:184
  15.3 3.1 %collective-permute-start.4 = (f32[8,4096]{1,0:T(8,128)S(1)}, f32[8,4096]{1,0:T(8,128)S(1)}, u32[]{:S(2)}, u32[]{:S(2)}) collective-permute-start(f32[8,4096]{1,0:T(8,128)S(1)} %join.7.refs_3_), channel_id=1, source_target_pairs={{0,128},{8,136},{16,144},{24,152},{32,160},{40,168},{48,176},{56,1... | collective-permute-start | bytes 393224 | tf_op jit(solution)/shard_map/ppermute | solution.py:337
  18.4 4.0 %phases.8.refs_4_ = f32[9,128,128]{2,1,0:T(8,128)S(1)} custom-call(bf16[512,48]{1,0:T(8,128)(2,1)S(1)} %copy.20.refs_0_, f32[128,128]{1,0:T(8,128)S(1)} %broadcast_in_dim.27.refs_1_, f32[16,128]{1,0:T(8,128)S(1)} %get-tuple-element.21.refs_2_, f32[8,4096]{1,0:T(8,128)S(1)} %join.7.refs_3_, f32[9,128,128]{2,1,0:T(8,128)S(1)} %phases.7.refs_4_), custom_call_target="tpu_custom_call" | custom-call | flops 23068672 | bytes 1048576 | tf_op jit(solution)/shard_map/phases/pallas_call | solution.py:184
  22.4 7.9 %phases.9 = f32[32,1408]{1,0:T(8,128)S(1)} custom-call(bf16[512,48]{1,0:T(8,128)(2,1)S(1)} %copy.20.refs_0_, f32[128,128]{1,0:T(8,128)S(1)} %broadcast_in_dim.27.refs_1_, f32[16,128]{1,0:T(8,128)S(1)} %get-tuple-element.21.refs_2_, f32[8,4096]{1,0:T(8,128)S(1)} %collective-permute-done.4.refs_3_, f32[9,128,128]{2,1,0:T(8,128)S(1)} %phases.8.refs_4_, ...), custom_call_target="tpu_custom_call" | custom-call | flops 46137344 | bytes 1048576 | tf_op jit(solution)/shard_map/phases/pallas_call | solution.py:184
  30.5 18.7 %all_to_all.11 = f32[32,1,1408]{2,1,0:T(1,128)S(1)} all-to-all(f32[32,1,1408]{2,1,0:T(1,128)S(1)} %copy.21), channel_id=1, replica_groups={{0,16,32,48,4,20,36,52,1,17,33,49,5,21,37,53,2,18,34,50,6,22,38,54,3,19..., dimensions={0} | all-to-all | bytes 360448 | tf_op jit(solution)/shard_map/all_to_all | solution.py:406
  49.2 1.2 %collective-permute-start.7 = (f32[32,1408]{1,0:T(8,128)S(1)}, f32[32,1408]{1,0:T(8,128)S(1)}, u32[]{:S(2)}, u32[]{:S(2)}) collective-permute-start(f32[32,1408]{1,0:T(8,128)S(1)} %bitcast.28), channel_id=1, source_target_pairs={{0,192},{8,200},{16,208},{24,216},{32,224},{40,232},{48,240},{56,2... | collective-permute-start | bytes 540680 | tf_op jit(solution)/shard_map/ppermute | solution.py:337
  50.4 1.0 %collective-permute-start.6 = (f32[32,1408]{1,0:T(8,128)S(1)}, f32[32,1408]{1,0:T(8,128)S(1)}, u32[]{:S(2)}, u32[]{:S(2)}) collective-permute-start(f32[32,1408]{1,0:T(8,128)S(1)} %bitcast.29), channel_id=1, source_target_pairs={{0,128},{8,136},{16,144},{24,152},{32,160},{40,168},{48,176},{56,1... | collective-permute-start | bytes 540680 | tf_op jit(solution)/shard_map/ppermute | solution.py:337
  51.5 1.1 %collective-permute-start.5 = (f32[32,1408]{1,0:T(8,128)S(1)}, f32[32,1408]{1,0:T(8,128)S(1)}, u32[]{:S(2)}, u32[]{:S(2)}) collective-permute-start(f32[32,1408]{1,0:T(8,128)S(1)} %bitcast.30), channel_id=1, source_target_pairs={{0,64},{8,72},{16,80},{24,88},{32,96},{40,104},{48,112},{56,120},{... | collective-permute-start | bytes 540680 | tf_op jit(solution)/shard_map/ppermute | solution.py:337
  52.6 5.8 %collective-permute-start.8 = (f32[32,1408]{1,0:T(8,128)S(1)}, f32[32,1408]{1,0:T(8,128)S(1)}, u32[]{:S(2)}, u32[]{:S(2)}) collective-permute-start(f32[32,1408]{1,0:T(8,128)S(1)} %bitcast.31), channel_id=1, source_target_pairs={{0,8},{8,0},{16,24},{24,16},{32,40},{40,32},{48,56},{56,48},{64,72... | collective-permute-start | bytes 540680 | tf_op jit(solution)/shard_map/ppermute | solution.py:337
  58.4 0.8 scatter.8.refs_0_
  59.1 2.4 %collective-permute-start.11 = (f32[32,1408]{1,0:T(8,128)S(1)}, f32[32,1408]{1,0:T(8,128)S(1)}, u32[]{:S(2)}, u32[]{:S(2)}) collective-permute-start(f32[32,1408]{1,0:T(8,128)S(1)} %collective-permute-done.7.p_ref), channel_id=1, source_target_pairs={{0,8},{8,0},{16,24},{24,16},{32,40},{40,32},{48,56},{56,48},{64,72... | collective-permute-start | bytes 540680 | tf_op jit(solution)/shard_map/ppermute | solution.py:337
  61.5 2.0 %collective-permute-start.10 = (f32[32,1408]{1,0:T(8,128)S(1)}, f32[32,1408]{1,0:T(8,128)S(1)}, u32[]{:S(2)}, u32[]{:S(2)}) collective-permute-start(f32[32,1408]{1,0:T(8,128)S(1)} %collective-permute-done.6.p_ref), channel_id=1, source_target_pairs={{0,8},{8,0},{16,24},{24,16},{32,40},{40,32},{48,56},{56,48},{64,72... | collective-permute-start | bytes 540680 | tf_op jit(solution)/shard_map/ppermute | solution.py:337
  63.8 0.7 scatter.9.refs_1_
  64.6 0.7 scatter.10.refs_2_
  65.3 0.7 scatter.11.refs_3_
  66.1 0.7 scatter.12.refs_4_
  68.4 0.7 scatter.15.refs_7_
  69.1 7.9 %transform.1 = f32[4,32,8,256]{3,2,1,0:T(8,128)} custom-call(s32[4,128]{1,0:T(4,128)S(1)} %broadcast_in_dim.10.own_ref, f32[128,32,128]{2,1,0:T(8,128)S(1)} %scatter.8.refs_0_, f32[128,32,128]{2,1,0:T(8,128)S(1)} %scatter.9.refs_1_, f32[128,32,128]{2,1,0:T(8,128)S(1)} %scatter.10.refs_2_, f32[128,32,128]{2,1,0:T(8,128)S(1)} %scatter.11.refs_3_, ...), custom_call_target="tpu_custom_call" | custom-call | tf_op jit(solution)/shard_map/transform/pallas_call | solution.py:324
  (48 shorter events, 5.0 us)
Async XLA Ops:
  0.0 4.1 %copy-start = (s32[3,1,4096]{2,1,0:T(1,128)S(1)}, s32[3,1,4096]{2,1,0:T(1,128)}, u32[]{:S(2)}) copy-start(s32[3,1,4096]{2,1,0:T(1,128)} %param.11) | copy-start | bytes 147460
  0.9 4.1 %collective-permute-start = (f32[8,256]{1,0:T(8,128)S(1)}, f32[8,256]{1,0:T(8,128)S(1)}, u32[]{:S(2)}, u32[]{:S(2)}) collective-permute-start(f32[8,256]{1,0:T(8,128)S(1)} %maximum_maximum_fusion.a_ref), channel_id=1, source_target_pairs={{0,8},{8,0},{16,24},{24,16},{32,40},{40,32},{48,56},{56,48},{64,72... | collective-permute-start | bytes 24584 | tf_op jit(solution)/shard_map/ppermute | solution.py:337
  5.0 2.6 %collective-permute-start.1 = (f32[8,512]{1,0:T(8,128)S(1)}, f32[8,512]{1,0:T(8,128)S(1)}, u32[]{:S(2)}, u32[]{:S(2)}) collective-permute-start(f32[8,512]{1,0:T(8,128)S(1)} %join.4.refs_3_.a_ref), channel_id=1, source_target_pairs={{0,16},{8,24},{16,0},{24,8},{32,48},{40,56},{48,32},{56,40},{64,80... | collective-permute-start | bytes 49160 | tf_op jit(solution)/shard_map/ppermute | solution.py:337
  7.6 2.8 %collective-permute-start.2 = (f32[8,1024]{1,0:T(8,128)S(1)}, f32[8,1024]{1,0:T(8,128)S(1)}, u32[]{:S(2)}, u32[]{:S(2)}) collective-permute-start(f32[8,1024]{1,0:T(8,128)S(1)} %join.5.refs_3_.a_ref), channel_id=1, source_target_pairs={{0,64},{8,72},{16,80},{24,88},{32,96},{40,104},{48,112},{56,120},{... | collective-permute-start | bytes 98312 | tf_op jit(solution)/shard_map/ppermute | solution.py:337
  8.6 13.7 %copy-start.2 = (f32[2,1,128]{2,1,0:T(1,128)S(1)}, f32[2,1,128]{2,1,0:T(1,128)}, u32[]{:S(2)}) copy-start(f32[2,1,128]{2,1,0:T(1,128)} %param.12) | copy-start | bytes 3076
  10.4 4.8 %collective-permute-start.3 = (f32[8,2048]{1,0:T(8,128)S(1)}, f32[8,2048]{1,0:T(8,128)S(1)}, u32[]{:S(2)}, u32[]{:S(2)}) collective-permute-start(f32[8,2048]{1,0:T(8,128)S(1)} %join.6.refs_3_.a_ref), channel_id=1, source_target_pairs={{0,32},{8,40},{16,48},{24,56},{32,0},{40,8},{48,16},{56,24},{64,96... | collective-permute-start | bytes 196616 | tf_op jit(solution)/shard_map/ppermute | solution.py:337
  15.3 7.1 %collective-permute-start.4 = (f32[8,4096]{1,0:T(8,128)S(1)}, f32[8,4096]{1,0:T(8,128)S(1)}, u32[]{:S(2)}, u32[]{:S(2)}) collective-permute-start(f32[8,4096]{1,0:T(8,128)S(1)} %join.7.refs_3_), channel_id=1, source_target_pairs={{0,128},{8,136},{16,144},{24,152},{32,160},{40,168},{48,176},{56,1... | collective-permute-start | bytes 393224 | tf_op jit(solution)/shard_map/ppermute | solution.py:337
  49.2 9.9 %collective-permute-start.7 = (f32[32,1408]{1,0:T(8,128)S(1)}, f32[32,1408]{1,0:T(8,128)S(1)}, u32[]{:S(2)}, u32[]{:S(2)}) collective-permute-start(f32[32,1408]{1,0:T(8,128)S(1)} %bitcast.28), channel_id=1, source_target_pairs={{0,192},{8,200},{16,208},{24,216},{32,224},{40,232},{48,240},{56,2... | collective-permute-start | bytes 540680 | tf_op jit(solution)/shard_map/ppermute | solution.py:337
  50.4 11.1 %collective-permute-start.6 = (f32[32,1408]{1,0:T(8,128)S(1)}, f32[32,1408]{1,0:T(8,128)S(1)}, u32[]{:S(2)}, u32[]{:S(2)}) collective-permute-start(f32[32,1408]{1,0:T(8,128)S(1)} %bitcast.29), channel_id=1, source_target_pairs={{0,128},{8,136},{16,144},{24,152},{32,160},{40,168},{48,176},{56,1... | collective-permute-start | bytes 540680 | tf_op jit(solution)/shard_map/ppermute | solution.py:337
  51.5 12.1 %collective-permute-start.5 = (f32[32,1408]{1,0:T(8,128)S(1)}, f32[32,1408]{1,0:T(8,128)S(1)}, u32[]{:S(2)}, u32[]{:S(2)}) collective-permute-start(f32[32,1408]{1,0:T(8,128)S(1)} %bitcast.30), channel_id=1, source_target_pairs={{0,64},{8,72},{16,80},{24,88},{32,96},{40,104},{48,112},{56,120},{... | collective-permute-start | bytes 540680 | tf_op jit(solution)/shard_map/ppermute | solution.py:337
  52.6 13.5 %collective-permute-start.8 = (f32[32,1408]{1,0:T(8,128)S(1)}, f32[32,1408]{1,0:T(8,128)S(1)}, u32[]{:S(2)}, u32[]{:S(2)}) collective-permute-start(f32[32,1408]{1,0:T(8,128)S(1)} %bitcast.31), channel_id=1, source_target_pairs={{0,8},{8,0},{16,24},{24,16},{32,40},{40,32},{48,56},{56,48},{64,72... | collective-permute-start | bytes 540680 | tf_op jit(solution)/shard_map/ppermute | solution.py:337
  59.1 9.2 %collective-permute-start.11 = (f32[32,1408]{1,0:T(8,128)S(1)}, f32[32,1408]{1,0:T(8,128)S(1)}, u32[]{:S(2)}, u32[]{:S(2)}) collective-permute-start(f32[32,1408]{1,0:T(8,128)S(1)} %collective-permute-done.7.p_ref), channel_id=1, source_target_pairs={{0,8},{8,0},{16,24},{24,16},{32,40},{40,32},{48,56},{56,48},{64,72... | collective-permute-start | bytes 540680 | tf_op jit(solution)/shard_map/ppermute | solution.py:337
  61.5 6.0 %collective-permute-start.10 = (f32[32,1408]{1,0:T(8,128)S(1)}, f32[32,1408]{1,0:T(8,128)S(1)}, u32[]{:S(2)}, u32[]{:S(2)}) collective-permute-start(f32[32,1408]{1,0:T(8,128)S(1)} %collective-permute-done.6.p_ref), channel_id=1, source_target_pairs={{0,8},{8,0},{16,24},{24,16},{32,40},{40,32},{48,56},{56,48},{64,72... | collective-permute-start | bytes 540680 | tf_op jit(solution)/shard_map/ppermute | solution.py:337
  63.6 3.3 %collective-permute-start.9 = (f32[32,1408]{1,0:T(8,128)S(1)}, f32[32,1408]{1,0:T(8,128)S(1)}, u32[]{:S(2)}, u32[]{:S(2)}) collective-permute-start(f32[32,1408]{1,0:T(8,128)S(1)} %collective-permute-done.5.p_ref), channel_id=1, source_target_pairs={{0,8},{8,0},{16,24},{24,16},{32,40},{40,32},{48,56},{56,48},{64,72... | collective-permute-start | bytes 540680 | tf_op jit(solution)/shard_map/ppermute | solution.py:337
  67.6 1.5 %copy-start.1 = (bf16[2,512,256]{2,1,0:T(8,128)(2,1)S(1)}, bf16[2,512,256]{2,1,0:T(8,128)(2,1)}, u32[]{:S(2)}) copy-start(bf16[2,512,256]{2,1,0:T(8,128)(2,1)} %constant.50.clone.refs_8_) | copy-start | bytes 1572868

commit v4 on v3

--- a/solution.py
+++ b/solution.py
@@ -75,42 +75,36 @@
     return hi, lo
 
 
-def phase_kernel(n_in, skip, first, last, scales, *refs):
-    lhs_ref, s2_ref, rc_ref = refs[:3]
-    atom_refs = refs[3 : 3 + n_in]
-    pos = 3 + n_in
+def phase_kernel(skip, first, last, *refs):
+    lhs_ref, s2_ref, rc_ref, a_ref = refs[:4]
+    pos = 4
     if not first:
         acc_in = refs[pos]
         pos += 1
-    if last:
-        obs_ref, ind_ref = refs[pos : pos + 2]
-        pos += 2
     out_ref = refs[pos]
     pos += 1
-    if first:
+    if rc_ref.shape[1] == 3:
         rc_out = refs[pos]
         pos += 1
+        rc0, rc1, rc2 = rotation_columns(rc_ref[...])
+        for q, column in enumerate((rc0, rc1, rc2)):
+            rc_out[:, q : q + 1] = column
+    else:
+        rc0, rc1, rc2 = rc_ref[:, 0:1], rc_ref[:, 1:2], rc_ref[:, 2:3]
     if last:
         acc_ref = refs[pos]
         pos += 1
     else:
         acc_ref = out_ref
     even_ref, odd_ref = refs[pos : pos + 2]
+    sets = lhs_ref.shape[0]
 
     if first:
         acc_ref[...] = jnp.zeros_like(acc_ref)
     else:
         acc_ref[...] = acc_in[...]
 
-    if first:
-        rc0, rc1, rc2 = rotation_columns(rc_ref[...])
-        for q, column in enumerate((rc0, rc1, rc2)):
-            rc_out[:, q : q + 1] = column
-    else:
-        rc0, rc1, rc2 = rc_ref[:, 0:1], rc_ref[:, 1:2], rc_ref[:, 2:3]
-    lhs = lhs_ref[...]
-
-    def set_turns(a_ref, i, turns_ref):
+    def set_turns(n, i, turns_ref):
         a = a_ref[:, pl.ds(pl.multiple_of(i * TILE, TILE), TILE)]
         placed = rc0 * a[0:1] + rc1 * a[1:2] + rc2 * a[2:3]
         p1 = placed.astype(jnp.bfloat16)
@@ -118,18 +112,18 @@
         p2 = rest.astype(jnp.bfloat16)
         p3 = (rest - p2.astype(jnp.float32)).astype(jnp.bfloat16)
         rhs = jnp.concatenate([p1, p2, p3], axis=0)
-        turns_ref[...] = jnp.dot(lhs, rhs, preferred_element_type=jnp.float32)
-
-    def add_tile(a_ref, i, turns_ref):
+        turns_ref[...] = jnp.dot(lhs_ref[n], rhs, preferred_element_type=jnp.float32)
+
+    def add_tile(n, i, turns_ref):
         a = a_ref[:, pl.ds(pl.multiple_of(i * TILE, TILE), TILE)]
         for nb in range(16):
             rows = slice(nb * 8, nb * 8 + 8)
-            s2 = s2_ref[rows, :]
+            s2 = s2_ref[n, rows, :]
             amps = []
             for part in range(TILE // 128):
                 lanes = slice(part * 128, part * 128 + 128)
                 amps.append(a[3:4, lanes] * jnp.exp2(a[4:5, lanes] * s2))
-            acc_ref[8, rows, :] += sum(amps[1:], amps[0])
+            acc_ref[n, 8, rows, :] += sum(amps[1:], amps[0])
             for r in range(4):
                 ms = mc = None
                 for part in range(TILE // 128):
@@ -138,54 +132,44 @@
                     m = amps[part] * s
                     ms = m * s if ms is None else ms + m * s
                     mc = m * c if mc is None else mc + m * c
-                acc_ref[r, rows, :] += ms
-                acc_ref[4 + r, rows, :] += mc
-
-    for a_ref in atom_refs:
-        begin, tiles = skip // TILE, a_ref.shape[1] // TILE
-        set_turns(a_ref, begin, even_ref)
-        if tiles == begin + 1:
-            add_tile(a_ref, begin, even_ref)
-        else:
-
-            @pl.loop(begin // 2, tiles // 2)
-            def _(i):
-                set_turns(a_ref, 2 * i + 1, odd_ref)
-                add_tile(a_ref, 2 * i, even_ref)
-                set_turns(a_ref, jnp.minimum(2 * i + 2, tiles - 1), even_ref)
-                add_tile(a_ref, 2 * i + 1, odd_ref)
-
-    if last:
-        atom_scale, refl_scale = scales
-        sums = [jnp.sum(acc_ref[q].T, axis=0, keepdims=True) for q in range(9)]
-        obs0, obs1 = obs_ref[0:1, :], obs_ref[1:2, :]
-        reals, imags = [], []
-        for r in range(4):
-            f_re = (sums[8] - (2.0 * SIN_K * SIN_K) * sums[r]) * atom_scale
-            f_im = ((2.0 * SIN_K * COS_K) * sums[4 + r]) * atom_scale
-            reals.append((obs0 * f_re + obs1 * f_im) * refl_scale)
-            imags.append((obs1 * f_re - obs0 * f_im) * refl_scale)
-        for q, row in enumerate(reals + imags + [ind_ref[q : q + 1, :] for q in range(3)]):
-            out_ref[:, q * 128 : q * 128 + 128] = jnp.broadcast_to(row, (out_ref.shape[0], 128))
-
-
-def phase_call(lhs, s2, rc, atoms, skip, acc, obs, indices, scales):
-    first, last = acc is None, obs is not None
-    operands = [lhs, s2, rc, *atoms] + ([] if first else [acc]) + ([obs, indices] if last else [])
-    acc_shape = (9, 128, 128)
+                acc_ref[n, r, rows, :] += ms
+                acc_ref[n, 4 + r, rows, :] += mc
+
+    begin, tiles = skip // TILE, a_ref.shape[1] // TILE
+    for n in range(sets):
+        set_turns(n, begin, even_ref)
+
+        @pl.loop(begin // 2, tiles // 2)
+        def _(i):
+            set_turns(n, 2 * i + 1, odd_ref)
+            add_tile(n, 2 * i, even_ref)
+            set_turns(n, jnp.minimum(2 * i + 2, tiles - 1), even_ref)
+            add_tile(n, 2 * i + 1, odd_ref)
+
+        if last:
+            out_ref[n] = jnp.concatenate(
+                [jnp.sum(acc_ref[n, q].T, axis=0, keepdims=True) for q in range(9)]
+                + [jnp.zeros((7, 128), jnp.float32)],
+                axis=0,
+            )
+
+
+def phase_call(lhs, s2, rc, atoms, skip, acc, last):
+    first, sets, vmem = acc is None, lhs.shape[0], pl.BlockSpec(memory_space=pltpu.VMEM)
+    operands = [lhs, s2, rc, atoms] + ([] if first else [acc])
+    acc_shape = (sets, 9, 128, 128)
     scratch = [pltpu.VMEM((512, TILE), jnp.float32)] * 2
     if last:
         scratch = [pltpu.VMEM(acc_shape, jnp.float32)] + scratch
-    vmem = pl.BlockSpec(memory_space=pltpu.VMEM)
-    out, out_specs = jax.ShapeDtypeStruct((PLANE, ROWS * 128) if last else acc_shape, jnp.float32), vmem
-    if first:
-        out, out_specs = (out, jax.ShapeDtypeStruct((16, 128), jnp.float32)), (vmem, vmem)
-    count = sum(a.shape[1] for a in atoms) - skip
+    out = [jax.ShapeDtypeStruct((sets, 16, 128) if last else acc_shape, jnp.float32)]
+    if rc.shape[1] == 3:
+        out.append(jax.ShapeDtypeStruct((16, 128), jnp.float32))
+    count = (atoms.shape[1] - skip) * sets
     return pl.pallas_call(
-        functools.partial(phase_kernel, len(atoms), skip, first, last, scales),
+        functools.partial(phase_kernel, skip, first, last),
         out_shape=out,
         in_specs=[vmem] * len(operands),
-        out_specs=out_specs,
+        out_specs=[vmem] * len(out),
         scratch_shapes=scratch,
         compiler_params=pltpu.CompilerParams(vmem_limit_bytes=16 << 20),
         cost_estimate=pl.CostEstimate(
@@ -193,6 +177,32 @@
         ),
         name="phases",
     )(*operands)
+
+
+def coefficient_kernel(scales, own_ref, first_ref, second_ref, obs_ref, ind_ref, out_ref):
+    atom_scale, refl_scale = scales
+    sums = own_ref[0] + first_ref[0] + second_ref[0]
+    obs0, obs1 = obs_ref[0:1, :], obs_ref[1:2, :]
+    reals, imags = [], []
+    for r in range(4):
+        f_re = (sums[8:9] - (2.0 * SIN_K * SIN_K) * sums[r : r + 1]) * atom_scale
+        f_im = ((2.0 * SIN_K * COS_K) * sums[4 + r : 5 + r]) * atom_scale
+        reals.append((obs0 * f_re + obs1 * f_im) * refl_scale)
+        imags.append((obs1 * f_re - obs0 * f_im) * refl_scale)
+    for q, row in enumerate(reals + imags + [ind_ref[q : q + 1, :] for q in range(3)]):
+        out_ref[:, q * 128 : q * 128 + 128] = jnp.broadcast_to(row, (PLANE, 128))
+
+
+def coefficient_call(own, first, second, obs, indices, scales):
+    vmem = pl.BlockSpec(memory_space=pltpu.VMEM)
+    return pl.pallas_call(
+        functools.partial(coefficient_kernel, scales),
+        out_shape=jax.ShapeDtypeStruct((PLANE, ROWS * 128), jnp.float32),
+        in_specs=[vmem] * 5,
+        out_specs=vmem,
+        compiler_params=pltpu.CompilerParams(vmem_limit_bytes=4 << 20),
+        name="coefficients",
+    )(own, first, second, obs, indices)
 
 
 def scatter_kernel(other, step, own_ref, p_ref, x_ref):
@@ -267,7 +277,7 @@
     lane = lax.broadcasted_iota(jnp.int32, (32, 128), 1)
     sign = jnp.where(lane < 64, -1.0, 1.0)
 
-    @pl.loop(0, 64, unroll=8)
+    @pl.loop(0, 64, unroll=16)
     def _(i):
         sides = [jnp.concatenate([x_ref[2 * i + q] for x_ref in x_refs], axis=0) for q in range(2)]
         hi, lo = split2(jnp.concatenate(sides, axis=1))
@@ -378,30 +388,41 @@
     atoms = jnp.concatenate([coords, weights[None], thermal[None], jnp.zeros_like(coords)], axis=0)
     atoms = join(atoms, swap(atoms, "atom", 1))
 
-    own_miller = lax.dynamic_slice_in_dim(miller[:, 0, :], j * own_count, own_count, 1)
-    indices = own_miller.astype(jnp.float32)
-    resolution = jnp.sum(indices * indices, axis=0) * (-LOG2E / (G * G))
-    s2 = jnp.broadcast_to(resolution[:, None], (own_count, 128))
-    lhs = indices.T[None, :, :, None] * jnp.eye(4, dtype=jnp.float32)[:, None, None, :]
-    lhs = jnp.pad(lhs.reshape(4 * own_count, 12), ((0, 0), (0, 4)))
-    lhs = jnp.concatenate([lhs, lhs, lhs], axis=1).astype(jnp.bfloat16)
+    sets = [
+        lax.dynamic_slice_in_dim(miller[:, 0, :], (j ^ mask) * own_count, own_count, 1).astype(jnp.float32)
+        for mask in (16, 20, 4, 0)
+    ]
+    indices = sets[3]
+    sets = jnp.stack(sets)
+    resolution = jnp.sum(sets * sets, axis=1) * (-LOG2E / (G * G))
+    s2 = jnp.broadcast_to(resolution[:, :, None], (4, own_count, 128))
+    lhs = jnp.transpose(sets, (0, 2, 1))[:, None, :, :, None] * jnp.eye(4, dtype=jnp.float32)[:, None, None, :]
+    lhs = jnp.pad(lhs.reshape(4, 4 * own_count, 12), ((0, 0), (0, 0), (0, 4)))
+    lhs = jnp.concatenate([lhs, lhs, lhs], axis=2).astype(jnp.bfloat16)
     rc = jnp.pad(jnp.tile(angles.T, (3, 1)), ((0, 4), (0, 0)))
     y, core = j // 8, j % 2
     own = jnp.stack([core, g, j, y]).astype(jnp.int32)
     own = jnp.broadcast_to(own[:, None], (4, 128))
-    indices, observed, own, atoms = lax.optimization_barrier((indices, observed[:, 0, :], own, atoms))
-
-    acc, skip = None, 0
-    for mask in (2, 8, 4, 16):
-        more = swap(atoms, "atom", mask)
-        acc = phase_call(lhs, s2, rc, [atoms], skip, acc, None, None, scales)
-        if skip == 0:
-            acc, rc = acc
-        more, acc = lax.optimization_barrier((more, acc))
-        if mask != 16:
-            skip = atoms.shape[1]
-            atoms = join(atoms, more)
-    payload = phase_call(lhs, s2, rc, [more], 0, acc, observed, indices, scales)
+    indices, observed, own, rc, atoms = lax.optimization_barrier(
+        (indices, observed[:, 0, :], own, rc, atoms)
+    )
+
+    more = swap(atoms, "atom", 2)
+    acc, rc = phase_call(lhs[:2], s2[:2], rc, atoms, 0, None, False)
+    more, acc = lax.optimization_barrier((more, acc))
+    atoms = join(atoms, more)
+    more = swap(atoms, "atom", 8)
+    (acc,) = phase_call(lhs[:2], s2[:2], rc, atoms, atoms.shape[1] // 2, acc, False)
+    more, acc = lax.optimization_barrier((more, acc))
+    atoms = join(atoms, more)
+    (away,) = phase_call(lhs[:2], s2[:2], rc, atoms, atoms.shape[1] // 2, acc, True)
+    near = swap(away, "atom", 16)
+    (side,) = phase_call(lhs[2:3], s2[2:3], rc, atoms, 0, None, True)
+    near, side = lax.optimization_barrier((near, side))
+    across = swap(side + near[1:], "atom", 4)
+    (here,) = phase_call(lhs[3:], s2[3:], rc, atoms, 0, None, True)
+    across, here = lax.optimization_barrier((across, here))
+    payload = coefficient_call(here, near, across, observed, indices, scales)
 
     plane = lax.all_to_all(
         payload, ("atom", "refl"), 0, 0, tiled=True, axis_index_groups=plane_groups()

time: 77.2 us -> 75.3 us (0.975)
  waiting for transfers between devices: 1.6 us -> 0.06 us
  blocking collectives: 18.7 us -> 17.5 us
  starting transfers between devices: 23.9 us -> 23 us
  local copies, waits for them, and re-layouts: 1.46 us -> 2.32 us
    ppermute x12, waiting for transfers between devices: 1.6 us -> 0.06 us  [swap(): return lax.ppermute(x, axis, [(i, i ^ mask) for i in range(count)])]
    all_to_all x1, blocking collectives: 18.7 us -> 17.5 us  [shards(): lax.all_to_all(payload, ('atom', 'refl'), 0, 0, tiled=True, axis_index_gr...]
    ppermute x12, starting transfers between devices: 23.9 us -> 23 us  [swap(): return lax.ppermute(x, axis, [(i, i ^ mask) for i in range(count)])]
    pallas_call x5 -> x6, Pallas kernels: 16.2 us -> 16.6 us  [the longest x5 16.6 us: phase_call(): pl.pallas_call(functools.partial(phase_kernel, skip, first, last), out_sh...]
  transfers between devices with their start and end apart: 12 -> 12, of which waited for: 3 -> 0; matrix products, arithmetic and copies ran while one was open for 2% -> 4% of each run, Pallas kernels for 18% -> 23%
where the time goes in v4:
time: 75.3 us; the launch traced here: 75.1 us
  Pallas kernels  30.2 us (40%)
  starting transfers between devices  23 us (31%)
  blocking collectives  17.5 us (23%)
  local copies, waits for them, and re-layouts  2.32 us (3%)
  other arithmetic  1.65 us (2%)
    ppermute x12, starting transfers between devices, swap(): return lax.ppermute(x, axis, [(i, i ^ mask) for i in range(count)])  23 us
    all_to_all x1, blocking collectives, shards(): lax.all_to_all(payload, ('atom', 'refl'), 0, 0, tiled=True, axis_index_gr...  17.5 us
    pallas_call x5, Pallas kernels, phase_call(): pl.pallas_call(functools.partial(phase_kernel, skip, first, last), out_sh...  16.6 us
    pallas_call x1, Pallas kernels, transform_call(): pl.pallas_call(transform_kernel, out_shape=jax.ShapeDtypeStruct((4, 32, 8...  7.66 us
    pallas_call x8, Pallas kernels, scatter_call(): pl.pallas_call(functools.partial(scatter_kernel, other, step), out_shape=...  5.97 us
  transfers between devices with their start and end apart: 12, of which 0 were waited for; matrix products, arithmetic and copies ran while one was open for 4% of the time, Pallas kernels for 23%

profile of v4, /device:TPU:1, one launch (start us, length us, event | category | flops | bytes accessed | tf_op | source)
XLA Modules:
  0.0 75.1 jit_solution(9655499683721056994)
XLA Ops:
  0.1 0.8 %maximum_maximum_fusion.a_ref = f32[8,256]{1,0:T(8,128)S(1)} fusion(f32[1,256]{1,0:T(1,128)} %bitcast.49, f32[1,256]{1,0:T(1,128)} %bitcast.50, f32[3,256]{1,0:T(4,128)} %param.7, f32[8]{0:T(128)S(1)} %pad.20.clone), kind=kLoop, calls=%fused_computation.6 | loop fusion | flops 6144 | bytes 13344 | tf_op jit(solution)/shard_map/concatenate | solution.py:388
  0.9 3.3 %collective-permute-start = (f32[8,256]{1,0:T(8,128)S(1)}, f32[8,256]{1,0:T(8,128)S(1)}, u32[]{:S(2)}, u32[]{:S(2)}) collective-permute-start(f32[8,256]{1,0:T(8,128)S(1)} %maximum_maximum_fusion.a_ref), channel_id=1, source_target_pairs={{0,8},{8,0},{16,24},{24,16},{32,40},{40,32},{48,56},{56,48},{64,72... | collective-permute-start | bytes 24584 | tf_op jit(solution)/shard_map/ppermute | solution.py:347
  6.8 2.0 %phases.5 = (f32[2,9,128,128]{3,2,1,0:T(8,128)S(1)}, f32[16,128]{1,0:T(8,128)S(1)}) custom-call(bf16[2,512,48]{2,1,0:T(8,128)(2,1)S(1)} %slice.47.refs_0_, f32[2,128,128]{2,1,0:T(8,128)S(1)} %broadcast_in_dim.30.refs_1_, f32[16,3]{1,0:T(8,128)S(1)} %pad.8.refs_2_, f32[8,512]{1,0:T(8,128)S(1)} %join.3.refs_3_.a_ref), custom_call_target="tpu_custom_call" | custom-call | flops 11534336 | bytes 1048576 | tf_op jit(solution)/shard_map/phases/pallas_call | solution.py:168
  8.9 1.3 %collective-permute-start.2 = (f32[8,1024]{1,0:T(8,128)S(1)}, f32[8,1024]{1,0:T(8,128)S(1)}, u32[]{:S(2)}, u32[]{:S(2)}) collective-permute-start(f32[8,1024]{1,0:T(8,128)S(1)} %join.4.refs_3_.a_ref), channel_id=1, source_target_pairs={{0,64},{8,72},{16,80},{24,88},{32,96},{40,104},{48,112},{56,120},{... | collective-permute-start | bytes 98312 | tf_op jit(solution)/shard_map/ppermute | solution.py:347
  10.1 1.8 %phases.6.refs_4_ = f32[2,9,128,128]{3,2,1,0:T(8,128)S(1)} custom-call(bf16[2,512,48]{2,1,0:T(8,128)(2,1)S(1)} %slice.47.refs_0_, f32[2,128,128]{2,1,0:T(8,128)S(1)} %broadcast_in_dim.30.refs_1_, f32[16,128]{1,0:T(8,128)S(1)} %get-tuple-element.23.refs_2_, f32[8,1024]{1,0:T(8,128)S(1)} %join.4.refs_3_.a_ref, f32[2,9,128,128]{3,2,1,0:T(8,128)S(1)} %get-tuple-element.26.refs_4_), custom_call_target="tpu_custom_call" | custom-call | flops 11534336 | bytes 1048576 | tf_op jit(solution)/shard_map/phases/pallas_call | solution.py:168
  12.0 4.4 %phases.7 = f32[2,16,128]{2,1,0:T(8,128)S(1)} custom-call(bf16[2,512,48]{2,1,0:T(8,128)(2,1)S(1)} %slice.47.refs_0_, f32[2,128,128]{2,1,0:T(8,128)S(1)} %broadcast_in_dim.30.refs_1_, f32[16,128]{1,0:T(8,128)S(1)} %get-tuple-element.23.refs_2_, f32[8,2048]{1,0:T(8,128)S(1)} %join.5.refs_3_, f32[2,9,128,128]{3,2,1,0:T(8,128)S(1)} %phases.6.refs_4_), custom_call_target="tpu_custom_call" | custom-call | flops 23068672 | bytes 1048576 | tf_op jit(solution)/shard_map/phases/pallas_call | solution.py:168
  16.4 2.7 %collective-permute-start.3 = (f32[2,16,128]{2,1,0:T(8,128)S(1)}, f32[2,16,128]{2,1,0:T(8,128)S(1)}, u32[]{:S(2)}, u32[]{:S(2)}) collective-permute-start(f32[2,16,128]{2,1,0:T(8,128)S(1)} %phases.7), channel_id=1, source_target_pairs={{0,128},{8,136},{16,144},{24,152},{32,160},{40,168},{48,176},{56,1... | collective-permute-start | bytes 49160 | tf_op jit(solution)/shard_map/ppermute | solution.py:347
  19.4 4.2 %phases.8 = f32[1,16,128]{2,1,0:T(8,128)S(1)} custom-call(bf16[1,512,48]{2,1,0:T(8,128)(2,1)S(1)} %get-tuple-element.36.refs_0_, f32[1,128,128]{2,1,0:T(8,128)S(1)} %broadcast_in_dim.31.refs_1_, f32[16,128]{1,0:T(8,128)S(1)} %get-tuple-element.23.refs_2_, f32[8,2048]{1,0:T(8,128)S(1)} %join.5.refs_3_), custom_call_target="tpu_custom_call" | custom-call | flops 23068672 | bytes 1048576 | tf_op jit(solution)/shard_map/phases/pallas_call | solution.py:168
  23.6 3.3 %collective-permute-start.4 = (f32[1,16,128]{2,1,0:T(8,128)S(1)}, f32[1,16,128]{2,1,0:T(8,128)S(1)}, u32[]{:S(2)}, u32[]{:S(2)}) collective-permute-start(f32[1,16,128]{2,1,0:T(8,128)S(1)} %slice_add_fusion), channel_id=1, source_target_pairs={{0,32},{8,40},{16,48},{24,56},{32,0},{40,8},{48,16},{56,24},{64,96... | collective-permute-start | bytes 24584 | tf_op jit(solution)/shard_map/ppermute | solution.py:347
  26.9 4.2 %phases.9.own_ref = f32[1,16,128]{2,1,0:T(8,128)S(1)} custom-call(bf16[1,512,48]{2,1,0:T(8,128)(2,1)S(1)} %get-tuple-element.35.refs_0_, f32[1,128,128]{2,1,0:T(8,128)S(1)} %broadcast_in_dim.32.refs_1_, f32[16,128]{1,0:T(8,128)S(1)} %get-tuple-element.23.refs_2_, f32[8,2048]{1,0:T(8,128)S(1)} %join.5.refs_3_), custom_call_target="tpu_custom_call" | custom-call | flops 23068672 | bytes 1048576 | tf_op jit(solution)/shard_map/phases/pallas_call | solution.py:168
  31.4 17.5 %all_to_all.11 = f32[32,1,1408]{2,1,0:T(1,128)S(1)} all-to-all(f32[32,1,1408]{2,1,0:T(1,128)S(1)} %copy.43), channel_id=1, replica_groups={{0,16,32,48,4,20,36,52,1,17,33,49,5,21,37,53,2,18,34,50,6,22,38,54,3,19..., dimensions={0} | all-to-all | bytes 360448 | tf_op jit(solution)/shard_map/all_to_all | solution.py:427
  49.6 1.4 %collective-permute-start.6 = (f32[32,1408]{1,0:T(8,128)S(1)}, f32[32,1408]{1,0:T(8,128)S(1)}, u32[]{:S(2)}, u32[]{:S(2)}) collective-permute-start(f32[32,1408]{1,0:T(8,128)S(1)} %bitcast.40), channel_id=1, source_target_pairs={{0,128},{8,136},{16,144},{24,152},{32,160},{40,168},{48,176},{56,1... | collective-permute-start | bytes 540680 | tf_op jit(solution)/shard_map/ppermute | solution.py:347
  51.0 1.2 %collective-permute-start.5 = (f32[32,1408]{1,0:T(8,128)S(1)}, f32[32,1408]{1,0:T(8,128)S(1)}, u32[]{:S(2)}, u32[]{:S(2)}) collective-permute-start(f32[32,1408]{1,0:T(8,128)S(1)} %bitcast.41), channel_id=1, source_target_pairs={{0,64},{8,72},{16,80},{24,88},{32,96},{40,104},{48,112},{56,120},{... | collective-permute-start | bytes 540680 | tf_op jit(solution)/shard_map/ppermute | solution.py:347
  52.2 4.5 %collective-permute-start.8 = (f32[32,1408]{1,0:T(8,128)S(1)}, f32[32,1408]{1,0:T(8,128)S(1)}, u32[]{:S(2)}, u32[]{:S(2)}) collective-permute-start(f32[32,1408]{1,0:T(8,128)S(1)} %bitcast.42), channel_id=1, source_target_pairs={{0,8},{8,0},{16,24},{24,16},{32,40},{40,32},{48,56},{56,48},{64,72... | collective-permute-start | bytes 540680 | tf_op jit(solution)/shard_map/ppermute | solution.py:347
  56.7 0.8 %scatter.8.refs_0_ = f32[128,32,128]{2,1,0:T(8,128)S(1)} custom-call(s32[4,128]{1,0:T(4,128)S(1)} %broadcast_in_dim.26.own_ref, f32[32,1408]{1,0:T(8,128)S(1)} %bitcast.43), custom_call_target="tpu_custom_call" | custom-call | flops 536870912 | bytes 1048576 | tf_op jit(solution)/shard_map/scatter/pallas_call | solution.py:257
  57.5 3.8 %collective-permute-start.11 = (f32[32,1408]{1,0:T(8,128)S(1)}, f32[32,1408]{1,0:T(8,128)S(1)}, u32[]{:S(2)}, u32[]{:S(2)}) collective-permute-start(f32[32,1408]{1,0:T(8,128)S(1)} %collective-permute-done.7.p_ref), channel_id=1, source_target_pairs={{0,8},{8,0},{16,24},{24,16},{32,40},{40,32},{48,56},{56,48},{64,72... | collective-permute-start | bytes 540680 | tf_op jit(solution)/shard_map/ppermute | solution.py:347
  61.3 0.8 %collective-permute-start.9 = (f32[32,1408]{1,0:T(8,128)S(1)}, f32[32,1408]{1,0:T(8,128)S(1)}, u32[]{:S(2)}, u32[]{:S(2)}) collective-permute-start(f32[32,1408]{1,0:T(8,128)S(1)} %collective-permute-done.5.p_ref), channel_id=1, source_target_pairs={{0,8},{8,0},{16,24},{24,16},{32,40},{40,32},{48,56},{56,48},{64,72... | collective-permute-start | bytes 540680 | tf_op jit(solution)/shard_map/ppermute | solution.py:347
  62.1 0.7 scatter.9.refs_1_
  62.9 0.8 %scatter.10.refs_2_ = f32[128,32,128]{2,1,0:T(8,128)S(1)} custom-call(s32[4,128]{1,0:T(4,128)S(1)} %broadcast_in_dim.26.own_ref, f32[32,1408]{1,0:T(8,128)S(1)} %collective-permute-done.6.p_ref), custom_call_target="tpu_custom_call" | custom-call | flops 536870912 | bytes 1048576 | tf_op jit(solution)/shard_map/scatter/pallas_call | solution.py:257
  63.6 0.8 %scatter.11.refs_3_ = f32[128,32,128]{2,1,0:T(8,128)S(1)} custom-call(s32[4,128]{1,0:T(4,128)S(1)} %broadcast_in_dim.26.own_ref, f32[32,1408]{1,0:T(8,128)S(1)} %collective-permute-done.7.p_ref), custom_call_target="tpu_custom_call" | custom-call | flops 536870912 | bytes 1048576 | tf_op jit(solution)/shard_map/scatter/pallas_call | solution.py:257
  64.4 0.7 scatter.12.refs_4_
  65.2 0.7 scatter.13.refs_5_
  65.9 0.7 scatter.14.refs_6_
  67.4 7.7 %transform.1 = f32[4,32,8,256]{3,2,1,0:T(8,128)} custom-call(s32[4,128]{1,0:T(4,128)S(1)} %broadcast_in_dim.26.own_ref, f32[128,32,128]{2,1,0:T(8,128)S(1)} %scatter.8.refs_0_, f32[128,32,128]{2,1,0:T(8,128)S(1)} %scatter.9.refs_1_, f32[128,32,128]{2,1,0:T(8,128)S(1)} %scatter.10.refs_2_, f32[128,32,128]{2,1,0:T(8,128)S(1)} %scatter.11.refs_3_, ...), custom_call_target="tpu_custom_call" | custom-call | tf_op jit(solution)/shard_map/transform/pallas_call | solution.py:334
  (62 shorter events, 4.8 us)
Async XLA Ops:
  0.9 5.3 %collective-permute-start = (f32[8,256]{1,0:T(8,128)S(1)}, f32[8,256]{1,0:T(8,128)S(1)}, u32[]{:S(2)}, u32[]{:S(2)}) collective-permute-start(f32[8,256]{1,0:T(8,128)S(1)} %maximum_maximum_fusion.a_ref), channel_id=1, source_target_pairs={{0,8},{8,0},{16,24},{24,16},{32,40},{40,32},{48,56},{56,48},{64,72... | collective-permute-start | bytes 24584 | tf_op jit(solution)/shard_map/ppermute | solution.py:347
  5.3 0.7 copy-start.2
  6.2 2.6 %collective-permute-start.1 = (f32[8,512]{1,0:T(8,128)S(1)}, f32[8,512]{1,0:T(8,128)S(1)}, u32[]{:S(2)}, u32[]{:S(2)}) collective-permute-start(f32[8,512]{1,0:T(8,128)S(1)} %join.3.refs_3_.a_ref), channel_id=1, source_target_pairs={{0,16},{8,24},{16,0},{24,8},{32,48},{40,56},{48,32},{56,40},{64,80... | collective-permute-start | bytes 49160 | tf_op jit(solution)/shard_map/ppermute | solution.py:347
  8.9 3.1 %collective-permute-start.2 = (f32[8,1024]{1,0:T(8,128)S(1)}, f32[8,1024]{1,0:T(8,128)S(1)}, u32[]{:S(2)}, u32[]{:S(2)}) collective-permute-start(f32[8,1024]{1,0:T(8,128)S(1)} %join.4.refs_3_.a_ref), channel_id=1, source_target_pairs={{0,64},{8,72},{16,80},{24,88},{32,96},{40,104},{48,112},{56,120},{... | collective-permute-start | bytes 98312 | tf_op jit(solution)/shard_map/ppermute | solution.py:347
  12.0 19.2 %copy-start.1 = (f32[2,1,128]{2,1,0:T(1,128)S(1)}, f32[2,1,128]{2,1,0:T(1,128)}, u32[]{:S(2)}) copy-start(f32[2,1,128]{2,1,0:T(1,128)} %param.12) | copy-start | bytes 3076
  16.4 7.2 %collective-permute-start.3 = (f32[2,16,128]{2,1,0:T(8,128)S(1)}, f32[2,16,128]{2,1,0:T(8,128)S(1)}, u32[]{:S(2)}, u32[]{:S(2)}) collective-permute-start(f32[2,16,128]{2,1,0:T(8,128)S(1)} %phases.7), channel_id=1, source_target_pairs={{0,128},{8,136},{16,144},{24,152},{32,160},{40,168},{48,176},{56,1... | collective-permute-start | bytes 49160 | tf_op jit(solution)/shard_map/ppermute | solution.py:347
  23.6 7.5 %collective-permute-start.4 = (f32[1,16,128]{2,1,0:T(8,128)S(1)}, f32[1,16,128]{2,1,0:T(8,128)S(1)}, u32[]{:S(2)}, u32[]{:S(2)}) collective-permute-start(f32[1,16,128]{2,1,0:T(8,128)S(1)} %slice_add_fusion), channel_id=1, source_target_pairs={{0,32},{8,40},{16,48},{24,56},{32,0},{40,8},{48,16},{56,24},{64,96... | collective-permute-start | bytes 24584 | tf_op jit(solution)/shard_map/ppermute | solution.py:347
  48.9 8.6 %collective-permute-start.7 = (f32[32,1408]{1,0:T(8,128)S(1)}, f32[32,1408]{1,0:T(8,128)S(1)}, u32[]{:S(2)}, u32[]{:S(2)}) collective-permute-start(f32[32,1408]{1,0:T(8,128)S(1)} %bitcast.39), channel_id=1, source_target_pairs={{0,192},{8,200},{16,208},{24,216},{32,224},{40,232},{48,240},{56,2... | collective-permute-start | bytes 540680 | tf_op jit(solution)/shard_map/ppermute | solution.py:347
  49.6 11.7 %collective-permute-start.6 = (f32[32,1408]{1,0:T(8,128)S(1)}, f32[32,1408]{1,0:T(8,128)S(1)}, u32[]{:S(2)}, u32[]{:S(2)}) collective-permute-start(f32[32,1408]{1,0:T(8,128)S(1)} %bitcast.40), channel_id=1, source_target_pairs={{0,128},{8,136},{16,144},{24,152},{32,160},{40,168},{48,176},{56,1... | collective-permute-start | bytes 540680 | tf_op jit(solution)/shard_map/ppermute | solution.py:347
  51.0 10.3 %collective-permute-start.5 = (f32[32,1408]{1,0:T(8,128)S(1)}, f32[32,1408]{1,0:T(8,128)S(1)}, u32[]{:S(2)}, u32[]{:S(2)}) collective-permute-start(f32[32,1408]{1,0:T(8,128)S(1)} %bitcast.41), channel_id=1, source_target_pairs={{0,64},{8,72},{16,80},{24,88},{32,96},{40,104},{48,112},{56,120},{... | collective-permute-start | bytes 540680 | tf_op jit(solution)/shard_map/ppermute | solution.py:347
  52.2 12.2 %collective-permute-start.8 = (f32[32,1408]{1,0:T(8,128)S(1)}, f32[32,1408]{1,0:T(8,128)S(1)}, u32[]{:S(2)}, u32[]{:S(2)}) collective-permute-start(f32[32,1408]{1,0:T(8,128)S(1)} %bitcast.42), channel_id=1, source_target_pairs={{0,8},{8,0},{16,24},{24,16},{32,40},{40,32},{48,56},{56,48},{64,72... | collective-permute-start | bytes 540680 | tf_op jit(solution)/shard_map/ppermute | solution.py:347
  57.5 9.2 %collective-permute-start.11 = (f32[32,1408]{1,0:T(8,128)S(1)}, f32[32,1408]{1,0:T(8,128)S(1)}, u32[]{:S(2)}, u32[]{:S(2)}) collective-permute-start(f32[32,1408]{1,0:T(8,128)S(1)} %collective-permute-done.7.p_ref), channel_id=1, source_target_pairs={{0,8},{8,0},{16,24},{24,16},{32,40},{40,32},{48,56},{56,48},{64,72... | collective-permute-start | bytes 540680 | tf_op jit(solution)/shard_map/ppermute | solution.py:347
  61.3 4.6 %collective-permute-start.10 = (f32[32,1408]{1,0:T(8,128)S(1)}, f32[32,1408]{1,0:T(8,128)S(1)}, u32[]{:S(2)}, u32[]{:S(2)}) collective-permute-start(f32[32,1408]{1,0:T(8,128)S(1)} %collective-permute-done.6.p_ref), channel_id=1, source_target_pairs={{0,8},{8,0},{16,24},{24,16},{32,40},{40,32},{48,56},{56,48},{64,72... | collective-permute-start | bytes 540680 | tf_op jit(solution)/shard_map/ppermute | solution.py:347
  61.3 3.9 %collective-permute-start.9 = (f32[32,1408]{1,0:T(8,128)S(1)}, f32[32,1408]{1,0:T(8,128)S(1)}, u32[]{:S(2)}, u32[]{:S(2)}) collective-permute-start(f32[32,1408]{1,0:T(8,128)S(1)} %collective-permute-done.5.p_ref), channel_id=1, source_target_pairs={{0,8},{8,0},{16,24},{24,16},{32,40},{40,32},{48,56},{56,48},{64,72... | collective-permute-start | bytes 540680 | tf_op jit(solution)/shard_map/ppermute | solution.py:347
  65.9 1.5 %copy-start = (bf16[2,512,256]{2,1,0:T(8,128)(2,1)S(1)}, bf16[2,512,256]{2,1,0:T(8,128)(2,1)}, u32[]{:S(2)}) copy-start(bf16[2,512,256]{2,1,0:T(8,128)(2,1)} %constant.59.clone.refs_8_) | copy-start | bytes 1572868

commit v5 on v4

--- a/solution.py
+++ b/solution.py
@@ -75,7 +75,7 @@
     return hi, lo
 
 
-def phase_kernel(skip, first, last, *refs):
+def phase_kernel(tile, skip, first, last, *refs):
     lhs_ref, s2_ref, rc_ref, a_ref = refs[:4]
     pos = 4
     if not first:
@@ -105,7 +105,7 @@
         acc_ref[...] = acc_in[...]
 
     def set_turns(n, i, turns_ref):
-        a = a_ref[:, pl.ds(pl.multiple_of(i * TILE, TILE), TILE)]
+        a = a_ref[:, pl.ds(pl.multiple_of(i * tile, tile), tile)]
         placed = rc0 * a[0:1] + rc1 * a[1:2] + rc2 * a[2:3]
         p1 = placed.astype(jnp.bfloat16)
         rest = placed - p1.astype(jnp.float32)
@@ -115,18 +115,18 @@
         turns_ref[...] = jnp.dot(lhs_ref[n], rhs, preferred_element_type=jnp.float32)
 
     def add_tile(n, i, turns_ref):
-        a = a_ref[:, pl.ds(pl.multiple_of(i * TILE, TILE), TILE)]
+        a = a_ref[:, pl.ds(pl.multiple_of(i * tile, tile), tile)]
         for nb in range(16):
             rows = slice(nb * 8, nb * 8 + 8)
             s2 = s2_ref[n, rows, :]
             amps = []
-            for part in range(TILE // 128):
+            for part in range(tile // 128):
                 lanes = slice(part * 128, part * 128 + 128)
                 amps.append(a[3:4, lanes] * jnp.exp2(a[4:5, lanes] * s2))
             acc_ref[n, 8, rows, :] += sum(amps[1:], amps[0])
             for r in range(4):
                 ms = mc = None
-                for part in range(TILE // 128):
+                for part in range(tile // 128):
                     lanes = slice(part * 128, part * 128 + 128)
                     s, c = half_angle(turns_ref[r * 128 + nb * 8 : r * 128 + nb * 8 + 8, lanes])
                     m = amps[part] * s
@@ -135,7 +135,7 @@
                 acc_ref[n, r, rows, :] += ms
                 acc_ref[n, 4 + r, rows, :] += mc
 
-    begin, tiles = skip // TILE, a_ref.shape[1] // TILE
+    begin, tiles = skip // tile, a_ref.shape[1] // tile
     for n in range(sets):
         set_turns(n, begin, even_ref)
 
@@ -158,7 +158,9 @@
     first, sets, vmem = acc is None, lhs.shape[0], pl.BlockSpec(memory_space=pltpu.VMEM)
     operands = [lhs, s2, rc, atoms] + ([] if first else [acc])
     acc_shape = (sets, 9, 128, 128)
-    scratch = [pltpu.VMEM((512, TILE), jnp.float32)] * 2
+    tile = TILE if skip % (2 * TILE) or (atoms.shape[1] - skip) % (2 * TILE) else 2 * TILE
+    tile = TILE if atoms.shape[1] - skip < 4 * TILE or skip % (4 * TILE) else tile
+    scratch = [pltpu.VMEM((512, tile), jnp.float32)] * 2
     if last:
         scratch = [pltpu.VMEM(acc_shape, jnp.float32)] + scratch
     out = [jax.ShapeDtypeStruct((sets, 16, 128) if last else acc_shape, jnp.float32)]
@@ -166,7 +168,7 @@
         out.append(jax.ShapeDtypeStruct((16, 128), jnp.float32))
     count = (atoms.shape[1] - skip) * sets
     return pl.pallas_call(
-        functools.partial(phase_kernel, skip, first, last),
+        functools.partial(phase_kernel, tile, skip, first, last),
         out_shape=out,
         in_specs=[vmem] * len(operands),
         out_specs=[vmem] * len(out),

time: 75.3 us -> 74.5 us (0.989)
  Pallas kernels: 30.2 us -> 29.4 us
    pallas_call x5, Pallas kernels: 16.6 us -> 15.8 us  [phase_call(): pl.pallas_call(functools.partial(phase_kernel, tile, skip, first, last),...]
where the time goes in v5:
time: 74.5 us; the launch traced here: 74.3 us
  Pallas kernels  29.4 us (39%)
  starting transfers between devices  23 us (31%)
  blocking collectives  17.5 us (23%)
  local copies, waits for them, and re-layouts  2.32 us (3%)
  other arithmetic  1.65 us (2%)
    ppermute x12, starting transfers between devices, swap(): return lax.ppermute(x, axis, [(i, i ^ mask) for i in range(count)])  23 us
    all_to_all x1, blocking collectives, shards(): lax.all_to_all(payload, ('atom', 'refl'), 0, 0, tiled=True, axis_index_gr...  17.5 us
    pallas_call x5, Pallas kernels, phase_call(): pl.pallas_call(functools.partial(phase_kernel, tile, skip, first, last),...  15.8 us
    pallas_call x1, Pallas kernels, transform_call(): pl.pallas_call(transform_kernel, out_shape=jax.ShapeDtypeStruct((4, 32, 8...  7.66 us
    pallas_call x8, Pallas kernels, scatter_call(): pl.pallas_call(functools.partial(scatter_kernel, other, step), out_shape=...  5.97 us
  transfers between devices with their start and end apart: 12, of which 0 were waited for; matrix products, arithmetic and copies ran while one was open for 4% of the time, Pallas kernels for 23%

profile of v5, /device:TPU:1, one launch (start us, length us, event | category | flops | bytes accessed | tf_op | source)
XLA Modules:
  0.0 74.3 jit_solution(5281317101511599715)
XLA Ops:
  0.1 0.8 %maximum_maximum_fusion.a_ref = f32[8,256]{1,0:T(8,128)S(1)} fusion(f32[1,256]{1,0:T(1,128)} %bitcast.49, f32[1,256]{1,0:T(1,128)} %bitcast.50, f32[3,256]{1,0:T(4,128)} %param.7, f32[8]{0:T(128)S(1)} %pad.20.clone), kind=kLoop, calls=%fused_computation.6 | loop fusion | flops 6144 | bytes 13344 | tf_op jit(solution)/shard_map/concatenate | solution.py:390
  0.9 3.3 %collective-permute-start = (f32[8,256]{1,0:T(8,128)S(1)}, f32[8,256]{1,0:T(8,128)S(1)}, u32[]{:S(2)}, u32[]{:S(2)}) collective-permute-start(f32[8,256]{1,0:T(8,128)S(1)} %maximum_maximum_fusion.a_ref), channel_id=1, source_target_pairs={{0,8},{8,0},{16,24},{24,16},{32,40},{40,32},{48,56},{56,48},{64,72... | collective-permute-start | bytes 24584 | tf_op jit(solution)/shard_map/ppermute | solution.py:349
  6.8 2.0 %phases.5 = (f32[2,9,128,128]{3,2,1,0:T(8,128)S(1)}, f32[16,128]{1,0:T(8,128)S(1)}) custom-call(bf16[2,512,48]{2,1,0:T(8,128)(2,1)S(1)} %slice.47.refs_0_, f32[2,128,128]{2,1,0:T(8,128)S(1)} %broadcast_in_dim.30.refs_1_, f32[16,3]{1,0:T(8,128)S(1)} %pad.8.refs_2_, f32[8,512]{1,0:T(8,128)S(1)} %join.3.refs_3_.a_ref), custom_call_target="tpu_custom_call" | custom-call | flops 11534336 | bytes 1048576 | tf_op jit(solution)/shard_map/phases/pallas_call | solution.py:170
  8.9 1.3 %collective-permute-start.2 = (f32[8,1024]{1,0:T(8,128)S(1)}, f32[8,1024]{1,0:T(8,128)S(1)}, u32[]{:S(2)}, u32[]{:S(2)}) collective-permute-start(f32[8,1024]{1,0:T(8,128)S(1)} %join.4.refs_3_.a_ref), channel_id=1, source_target_pairs={{0,64},{8,72},{16,80},{24,88},{32,96},{40,104},{48,112},{56,120},{... | collective-permute-start | bytes 98312 | tf_op jit(solution)/shard_map/ppermute | solution.py:349
  10.1 1.8 %phases.6.refs_4_ = f32[2,9,128,128]{3,2,1,0:T(8,128)S(1)} custom-call(bf16[2,512,48]{2,1,0:T(8,128)(2,1)S(1)} %slice.47.refs_0_, f32[2,128,128]{2,1,0:T(8,128)S(1)} %broadcast_in_dim.30.refs_1_, f32[16,128]{1,0:T(8,128)S(1)} %get-tuple-element.23.refs_2_, f32[8,1024]{1,0:T(8,128)S(1)} %join.4.refs_3_.a_ref, f32[2,9,128,128]{3,2,1,0:T(8,128)S(1)} %get-tuple-element.26.refs_4_), custom_call_target="tpu_custom_call" | custom-call | flops 11534336 | bytes 1048576 | tf_op jit(solution)/shard_map/phases/pallas_call | solution.py:170
  12.0 3.7 %phases.7 = f32[2,16,128]{2,1,0:T(8,128)S(1)} custom-call(bf16[2,512,48]{2,1,0:T(8,128)(2,1)S(1)} %slice.47.refs_0_, f32[2,128,128]{2,1,0:T(8,128)S(1)} %broadcast_in_dim.30.refs_1_, f32[16,128]{1,0:T(8,128)S(1)} %get-tuple-element.23.refs_2_, f32[8,2048]{1,0:T(8,128)S(1)} %join.5.refs_3_, f32[2,9,128,128]{3,2,1,0:T(8,128)S(1)} %phases.6.refs_4_), custom_call_target="tpu_custom_call" | custom-call | flops 23068672 | bytes 1048576 | tf_op jit(solution)/shard_map/phases/pallas_call | solution.py:170
  15.7 2.9 %collective-permute-start.3 = (f32[2,16,128]{2,1,0:T(8,128)S(1)}, f32[2,16,128]{2,1,0:T(8,128)S(1)}, u32[]{:S(2)}, u32[]{:S(2)}) collective-permute-start(f32[2,16,128]{2,1,0:T(8,128)S(1)} %phases.7), channel_id=1, source_target_pairs={{0,128},{8,136},{16,144},{24,152},{32,160},{40,168},{48,176},{56,1... | collective-permute-start | bytes 49160 | tf_op jit(solution)/shard_map/ppermute | solution.py:349
  18.9 4.1 %phases.8 = f32[1,16,128]{2,1,0:T(8,128)S(1)} custom-call(bf16[1,512,48]{2,1,0:T(8,128)(2,1)S(1)} %get-tuple-element.36.refs_0_, f32[1,128,128]{2,1,0:T(8,128)S(1)} %broadcast_in_dim.31.refs_1_, f32[16,128]{1,0:T(8,128)S(1)} %get-tuple-element.23.refs_2_, f32[8,2048]{1,0:T(8,128)S(1)} %join.5.refs_3_), custom_call_target="tpu_custom_call" | custom-call | flops 23068672 | bytes 1048576 | tf_op jit(solution)/shard_map/phases/pallas_call | solution.py:170
  23.1 3.1 %collective-permute-start.4 = (f32[1,16,128]{2,1,0:T(8,128)S(1)}, f32[1,16,128]{2,1,0:T(8,128)S(1)}, u32[]{:S(2)}, u32[]{:S(2)}) collective-permute-start(f32[1,16,128]{2,1,0:T(8,128)S(1)} %slice_add_fusion), channel_id=1, source_target_pairs={{0,32},{8,40},{16,48},{24,56},{32,0},{40,8},{48,16},{56,24},{64,96... | collective-permute-start | bytes 24584 | tf_op jit(solution)/shard_map/ppermute | solution.py:349
  26.2 4.1 %phases.9.own_ref = f32[1,16,128]{2,1,0:T(8,128)S(1)} custom-call(bf16[1,512,48]{2,1,0:T(8,128)(2,1)S(1)} %get-tuple-element.35.refs_0_, f32[1,128,128]{2,1,0:T(8,128)S(1)} %broadcast_in_dim.32.refs_1_, f32[16,128]{1,0:T(8,128)S(1)} %get-tuple-element.23.refs_2_, f32[8,2048]{1,0:T(8,128)S(1)} %join.5.refs_3_), custom_call_target="tpu_custom_call" | custom-call | flops 23068672 | bytes 1048576 | tf_op jit(solution)/shard_map/phases/pallas_call | solution.py:170
  30.6 17.5 %all_to_all.11 = f32[32,1,1408]{2,1,0:T(1,128)S(1)} all-to-all(f32[32,1,1408]{2,1,0:T(1,128)S(1)} %copy.43), channel_id=1, replica_groups={{0,16,32,48,4,20,36,52,1,17,33,49,5,21,37,53,2,18,34,50,6,22,38,54,3,19..., dimensions={0} | all-to-all | bytes 360448 | tf_op jit(solution)/shard_map/all_to_all | solution.py:429
  48.1 0.7 collective-permute-start.7
  48.8 1.4 %collective-permute-start.6 = (f32[32,1408]{1,0:T(8,128)S(1)}, f32[32,1408]{1,0:T(8,128)S(1)}, u32[]{:S(2)}, u32[]{:S(2)}) collective-permute-start(f32[32,1408]{1,0:T(8,128)S(1)} %bitcast.40), channel_id=1, source_target_pairs={{0,128},{8,136},{16,144},{24,152},{32,160},{40,168},{48,176},{56,1... | collective-permute-start | bytes 540680 | tf_op jit(solution)/shard_map/ppermute | solution.py:349
  50.2 1.2 %collective-permute-start.5 = (f32[32,1408]{1,0:T(8,128)S(1)}, f32[32,1408]{1,0:T(8,128)S(1)}, u32[]{:S(2)}, u32[]{:S(2)}) collective-permute-start(f32[32,1408]{1,0:T(8,128)S(1)} %bitcast.41), channel_id=1, source_target_pairs={{0,64},{8,72},{16,80},{24,88},{32,96},{40,104},{48,112},{56,120},{... | collective-permute-start | bytes 540680 | tf_op jit(solution)/shard_map/ppermute | solution.py:349
  51.4 4.5 %collective-permute-start.8 = (f32[32,1408]{1,0:T(8,128)S(1)}, f32[32,1408]{1,0:T(8,128)S(1)}, u32[]{:S(2)}, u32[]{:S(2)}) collective-permute-start(f32[32,1408]{1,0:T(8,128)S(1)} %bitcast.42), channel_id=1, source_target_pairs={{0,8},{8,0},{16,24},{24,16},{32,40},{40,32},{48,56},{56,48},{64,72... | collective-permute-start | bytes 540680 | tf_op jit(solution)/shard_map/ppermute | solution.py:349
  55.9 0.8 %scatter.8.refs_0_ = f32[128,32,128]{2,1,0:T(8,128)S(1)} custom-call(s32[4,128]{1,0:T(4,128)S(1)} %broadcast_in_dim.26.own_ref, f32[32,1408]{1,0:T(8,128)S(1)} %bitcast.43), custom_call_target="tpu_custom_call" | custom-call | flops 536870912 | bytes 1048576 | tf_op jit(solution)/shard_map/scatter/pallas_call | solution.py:259
  56.7 3.8 %collective-permute-start.11 = (f32[32,1408]{1,0:T(8,128)S(1)}, f32[32,1408]{1,0:T(8,128)S(1)}, u32[]{:S(2)}, u32[]{:S(2)}) collective-permute-start(f32[32,1408]{1,0:T(8,128)S(1)} %collective-permute-done.7.p_ref), channel_id=1, source_target_pairs={{0,8},{8,0},{16,24},{24,16},{32,40},{40,32},{48,56},{56,48},{64,72... | collective-permute-start | bytes 540680 | tf_op jit(solution)/shard_map/ppermute | solution.py:349
  60.5 0.8 %collective-permute-start.9 = (f32[32,1408]{1,0:T(8,128)S(1)}, f32[32,1408]{1,0:T(8,128)S(1)}, u32[]{:S(2)}, u32[]{:S(2)}) collective-permute-start(f32[32,1408]{1,0:T(8,128)S(1)} %collective-permute-done.5.p_ref), channel_id=1, source_target_pairs={{0,8},{8,0},{16,24},{24,16},{32,40},{40,32},{48,56},{56,48},{64,72... | collective-permute-start | bytes 540680 | tf_op jit(solution)/shard_map/ppermute | solution.py:349
  61.3 0.7 %scatter.9.refs_1_ = f32[128,32,128]{2,1,0:T(8,128)S(1)} custom-call(s32[4,128]{1,0:T(4,128)S(1)} %broadcast_in_dim.26.own_ref, f32[32,1408]{1,0:T(8,128)S(1)} %collective-permute-done.5.p_ref), custom_call_target="tpu_custom_call" | custom-call | flops 536870912 | bytes 1048576 | tf_op jit(solution)/shard_map/scatter/pallas_call | solution.py:259
  62.1 0.8 %scatter.10.refs_2_ = f32[128,32,128]{2,1,0:T(8,128)S(1)} custom-call(s32[4,128]{1,0:T(4,128)S(1)} %broadcast_in_dim.26.own_ref, f32[32,1408]{1,0:T(8,128)S(1)} %collective-permute-done.6.p_ref), custom_call_target="tpu_custom_call" | custom-call | flops 536870912 | bytes 1048576 | tf_op jit(solution)/shard_map/scatter/pallas_call | solution.py:259
  62.8 0.8 %scatter.11.refs_3_ = f32[128,32,128]{2,1,0:T(8,128)S(1)} custom-call(s32[4,128]{1,0:T(4,128)S(1)} %broadcast_in_dim.26.own_ref, f32[32,1408]{1,0:T(8,128)S(1)} %collective-permute-done.7.p_ref), custom_call_target="tpu_custom_call" | custom-call | flops 536870912 | bytes 1048576 | tf_op jit(solution)/shard_map/scatter/pallas_call | solution.py:259
  63.6 0.7 %scatter.12.refs_4_ = f32[128,32,128]{2,1,0:T(8,128)S(1)} custom-call(s32[4,128]{1,0:T(4,128)S(1)} %broadcast_in_dim.26.own_ref, f32[32,1408]{1,0:T(8,128)S(1)} %collective-permute-done.8.p_ref), custom_call_target="tpu_custom_call" | custom-call | flops 536870912 | bytes 1048576 | tf_op jit(solution)/shard_map/scatter/pallas_call | solution.py:259
  65.1 0.7 scatter.14.refs_6_
  66.6 7.7 %transform.1 = f32[4,32,8,256]{3,2,1,0:T(8,128)} custom-call(s32[4,128]{1,0:T(4,128)S(1)} %broadcast_in_dim.26.own_ref, f32[128,32,128]{2,1,0:T(8,128)S(1)} %scatter.8.refs_0_, f32[128,32,128]{2,1,0:T(8,128)S(1)} %scatter.9.refs_1_, f32[128,32,128]{2,1,0:T(8,128)S(1)} %scatter.10.refs_2_, f32[128,32,128]{2,1,0:T(8,128)S(1)} %scatter.11.refs_3_, ...), custom_call_target="tpu_custom_call" | custom-call | tf_op jit(solution)/shard_map/transform/pallas_call | solution.py:336
  (62 shorter events, 4.8 us)
Async XLA Ops:
  0.9 5.3 %collective-permute-start = (f32[8,256]{1,0:T(8,128)S(1)}, f32[8,256]{1,0:T(8,128)S(1)}, u32[]{:S(2)}, u32[]{:S(2)}) collective-permute-start(f32[8,256]{1,0:T(8,128)S(1)} %maximum_maximum_fusion.a_ref), channel_id=1, source_target_pairs={{0,8},{8,0},{16,24},{24,16},{32,40},{40,32},{48,56},{56,48},{64,72... | collective-permute-start | bytes 24584 | tf_op jit(solution)/shard_map/ppermute | solution.py:349
  5.3 0.7 copy-start.2
  6.2 2.6 %collective-permute-start.1 = (f32[8,512]{1,0:T(8,128)S(1)}, f32[8,512]{1,0:T(8,128)S(1)}, u32[]{:S(2)}, u32[]{:S(2)}) collective-permute-start(f32[8,512]{1,0:T(8,128)S(1)} %join.3.refs_3_.a_ref), channel_id=1, source_target_pairs={{0,16},{8,24},{16,0},{24,8},{32,48},{40,56},{48,32},{56,40},{64,80... | collective-permute-start | bytes 49160 | tf_op jit(solution)/shard_map/ppermute | solution.py:349
  8.9 3.1 %collective-permute-start.2 = (f32[8,1024]{1,0:T(8,128)S(1)}, f32[8,1024]{1,0:T(8,128)S(1)}, u32[]{:S(2)}, u32[]{:S(2)}) collective-permute-start(f32[8,1024]{1,0:T(8,128)S(1)} %join.4.refs_3_.a_ref), channel_id=1, source_target_pairs={{0,64},{8,72},{16,80},{24,88},{32,96},{40,104},{48,112},{56,120},{... | collective-permute-start | bytes 98312 | tf_op jit(solution)/shard_map/ppermute | solution.py:349
  12.0 18.4 %copy-start.1 = (f32[2,1,128]{2,1,0:T(1,128)S(1)}, f32[2,1,128]{2,1,0:T(1,128)}, u32[]{:S(2)}) copy-start(f32[2,1,128]{2,1,0:T(1,128)} %param.12) | copy-start | bytes 3076
  15.7 7.3 %collective-permute-start.3 = (f32[2,16,128]{2,1,0:T(8,128)S(1)}, f32[2,16,128]{2,1,0:T(8,128)S(1)}, u32[]{:S(2)}, u32[]{:S(2)}) collective-permute-start(f32[2,16,128]{2,1,0:T(8,128)S(1)} %phases.7), channel_id=1, source_target_pairs={{0,128},{8,136},{16,144},{24,152},{32,160},{40,168},{48,176},{56,1... | collective-permute-start | bytes 49160 | tf_op jit(solution)/shard_map/ppermute | solution.py:349
  23.1 7.3 %collective-permute-start.4 = (f32[1,16,128]{2,1,0:T(8,128)S(1)}, f32[1,16,128]{2,1,0:T(8,128)S(1)}, u32[]{:S(2)}, u32[]{:S(2)}) collective-permute-start(f32[1,16,128]{2,1,0:T(8,128)S(1)} %slice_add_fusion), channel_id=1, source_target_pairs={{0,32},{8,40},{16,48},{24,56},{32,0},{40,8},{48,16},{56,24},{64,96... | collective-permute-start | bytes 24584 | tf_op jit(solution)/shard_map/ppermute | solution.py:349
  48.1 8.6 %collective-permute-start.7 = (f32[32,1408]{1,0:T(8,128)S(1)}, f32[32,1408]{1,0:T(8,128)S(1)}, u32[]{:S(2)}, u32[]{:S(2)}) collective-permute-start(f32[32,1408]{1,0:T(8,128)S(1)} %bitcast.39), channel_id=1, source_target_pairs={{0,192},{8,200},{16,208},{24,216},{32,224},{40,232},{48,240},{56,2... | collective-permute-start | bytes 540680 | tf_op jit(solution)/shard_map/ppermute | solution.py:349
  48.8 11.7 %collective-permute-start.6 = (f32[32,1408]{1,0:T(8,128)S(1)}, f32[32,1408]{1,0:T(8,128)S(1)}, u32[]{:S(2)}, u32[]{:S(2)}) collective-permute-start(f32[32,1408]{1,0:T(8,128)S(1)} %bitcast.40), channel_id=1, source_target_pairs={{0,128},{8,136},{16,144},{24,152},{32,160},{40,168},{48,176},{56,1... | collective-permute-start | bytes 540680 | tf_op jit(solution)/shard_map/ppermute | solution.py:349
  50.2 10.2 %collective-permute-start.5 = (f32[32,1408]{1,0:T(8,128)S(1)}, f32[32,1408]{1,0:T(8,128)S(1)}, u32[]{:S(2)}, u32[]{:S(2)}) collective-permute-start(f32[32,1408]{1,0:T(8,128)S(1)} %bitcast.41), channel_id=1, source_target_pairs={{0,64},{8,72},{16,80},{24,88},{32,96},{40,104},{48,112},{56,120},{... | collective-permute-start | bytes 540680 | tf_op jit(solution)/shard_map/ppermute | solution.py:349
  51.4 12.2 %collective-permute-start.8 = (f32[32,1408]{1,0:T(8,128)S(1)}, f32[32,1408]{1,0:T(8,128)S(1)}, u32[]{:S(2)}, u32[]{:S(2)}) collective-permute-start(f32[32,1408]{1,0:T(8,128)S(1)} %bitcast.42), channel_id=1, source_target_pairs={{0,8},{8,0},{16,24},{24,16},{32,40},{40,32},{48,56},{56,48},{64,72... | collective-permute-start | bytes 540680 | tf_op jit(solution)/shard_map/ppermute | solution.py:349
  56.7 9.2 %collective-permute-start.11 = (f32[32,1408]{1,0:T(8,128)S(1)}, f32[32,1408]{1,0:T(8,128)S(1)}, u32[]{:S(2)}, u32[]{:S(2)}) collective-permute-start(f32[32,1408]{1,0:T(8,128)S(1)} %collective-permute-done.7.p_ref), channel_id=1, source_target_pairs={{0,8},{8,0},{16,24},{24,16},{32,40},{40,32},{48,56},{56,48},{64,72... | collective-permute-start | bytes 540680 | tf_op jit(solution)/shard_map/ppermute | solution.py:349
  60.5 4.7 %collective-permute-start.10 = (f32[32,1408]{1,0:T(8,128)S(1)}, f32[32,1408]{1,0:T(8,128)S(1)}, u32[]{:S(2)}, u32[]{:S(2)}) collective-permute-start(f32[32,1408]{1,0:T(8,128)S(1)} %collective-permute-done.6.p_ref), channel_id=1, source_target_pairs={{0,8},{8,0},{16,24},{24,16},{32,40},{40,32},{48,56},{56,48},{64,72... | collective-permute-start | bytes 540680 | tf_op jit(solution)/shard_map/ppermute | solution.py:349
  60.5 3.9 %collective-permute-start.9 = (f32[32,1408]{1,0:T(8,128)S(1)}, f32[32,1408]{1,0:T(8,128)S(1)}, u32[]{:S(2)}, u32[]{:S(2)}) collective-permute-start(f32[32,1408]{1,0:T(8,128)S(1)} %collective-permute-done.5.p_ref), channel_id=1, source_target_pairs={{0,8},{8,0},{16,24},{24,16},{32,40},{40,32},{48,56},{56,48},{64,72... | collective-permute-start | bytes 540680 | tf_op jit(solution)/shard_map/ppermute | solution.py:349
  65.1 1.5 %copy-start = (bf16[2,512,256]{2,1,0:T(8,128)(2,1)S(1)}, bf16[2,512,256]{2,1,0:T(8,128)(2,1)}, u32[]{:S(2)}) copy-start(bf16[2,512,256]{2,1,0:T(8,128)(2,1)} %constant.59.clone.refs_8_) | copy-start | bytes 1572868

commit v6 on v5

--- a/solution.py
+++ b/solution.py
@@ -268,7 +268,7 @@
 
 
 def transform_kernel(own_ref, *refs):
-    x_refs, (d_ref, out_ref, z_ref) = refs[:8], refs[8:]
+    x_refs, (d_ref, out_ref, z_ref, field_ref, sems) = refs[:8], refs[8:]
     own_core, own_g, own_y = (jnp.concatenate([own_ref[q : q + 1]] * 2, axis=1) for q in (0, 1, 3))
     column = lax.broadcasted_iota(jnp.int32, (32, G), 1)
     y, core = own_y ^ ((column >> 5) & 3), own_core ^ (column >> 7)
@@ -291,11 +291,11 @@
             combined = z[:32, lanes] + sign * pltpu.roll(z[32:, lanes], 64, 1)
             z_ref[pl.ds(2 * i + half, 32, stride=128), :] = combined
 
-    @pl.loop(0, 4, unroll=4)
-    def _(i):
+    copies = []
+    for i in range(4):
         parts = []
         for q in range(8):
-            zv = z_ref[pl.ds(pl.multiple_of((i * 8 + q) * 128, 128), 128), :].T
+            zv = z_ref[(i * 8 + q) * 128 : (i * 8 + q + 1) * 128, :].T
             parts.append(
                 jnp.concatenate([zv[0:32], zv[32:64], zv[64:96], zv[96:128]], axis=1)
             )
@@ -308,7 +308,13 @@
         )
         for q in range(8):
             for r in range(4):
-                out_ref[r, i * 8 + q] = field[q * 32 + r * 8 : q * 32 + r * 8 + 8, :]
+                field_ref[i, r, q] = field[q * 32 + r * 8 : q * 32 + r * 8 + 8, :]
+        copies.append(
+            pltpu.make_async_copy(field_ref.at[i], out_ref.at[:, i * 8 : i * 8 + 8], sems.at[i])
+        )
+        copies[-1].start()
+    for copy in copies:
+        copy.wait()
 
 
 def split_np(x):
@@ -337,8 +343,12 @@
         transform_kernel,
         out_shape=jax.ShapeDtypeStruct((4, 32, 8, G), jnp.float32),
         in_specs=[vmem] * 10,
-        out_specs=vmem,
-        scratch_shapes=[pltpu.VMEM((32 * 128, 128), jnp.float32)],
+        out_specs=pl.BlockSpec(memory_space=pl.ANY),
+        scratch_shapes=[
+            pltpu.VMEM((32 * 128, 128), jnp.float32),
+            pltpu.VMEM((4, 4, 8, 8, G), jnp.float32),
+            pltpu.SemaphoreType.DMA((4,)),
+        ],
         compiler_params=pltpu.CompilerParams(vmem_limit_bytes=8 << 20),
         name="transform",
     )(own, *pieces, first)

time: 74.5 us -> 74.5 us (level)
  no operation moved by 1% of the time
where the time goes in v6:
time: 74.5 us; the launch traced here: 74.3 us
  Pallas kernels  29.3 us (39%)
  starting transfers between devices  23 us (31%)
  blocking collectives  17.5 us (23%)
  local copies, waits for them, and re-layouts  2.32 us (3%)
  other arithmetic  1.65 us (2%)
    ppermute x12, starting transfers between devices, swap(): return lax.ppermute(x, axis, [(i, i ^ mask) for i in range(count)])  23 us
    all_to_all x1, blocking collectives, shards(): lax.all_to_all(payload, ('atom', 'refl'), 0, 0, tiled=True, axis_index_gr...  17.5 us
    pallas_call x5, Pallas kernels, phase_call(): pl.pallas_call(functools.partial(phase_kernel, tile, skip, first, last),...  15.8 us
    pallas_call x1, Pallas kernels, transform_call(): pl.pallas_call(transform_kernel, out_shape=jax.ShapeDtypeStruct((4, 32, 8...  7.52 us
    pallas_call x8, Pallas kernels, scatter_call(): pl.pallas_call(functools.partial(scatter_kernel, other, step), out_shape=...  5.97 us
  transfers between devices with their start and end apart: 12, of which 0 were waited for; matrix products, arithmetic and copies ran while one was open for 4% of the time, Pallas kernels for 23%

profile of v6, /device:TPU:1, one launch (start us, length us, event | category | flops | bytes accessed | tf_op | source)
XLA Modules:
  0.0 74.3 jit_solution(15329038900151930088)
XLA Ops:
  0.1 0.8 %maximum_maximum_fusion.a_ref = f32[8,256]{1,0:T(8,128)S(1)} fusion(f32[1,256]{1,0:T(1,128)} %bitcast.49, f32[1,256]{1,0:T(1,128)} %bitcast.50, f32[3,256]{1,0:T(4,128)} %param.7, f32[8]{0:T(128)S(1)} %pad.20.clone), kind=kLoop, calls=%fused_computation.6 | loop fusion | flops 6144 | bytes 13344 | tf_op jit(solution)/shard_map/concatenate | solution.py:400
  0.9 3.3 %collective-permute-start = (f32[8,256]{1,0:T(8,128)S(1)}, f32[8,256]{1,0:T(8,128)S(1)}, u32[]{:S(2)}, u32[]{:S(2)}) collective-permute-start(f32[8,256]{1,0:T(8,128)S(1)} %maximum_maximum_fusion.a_ref), channel_id=1, source_target_pairs={{0,8},{8,0},{16,24},{24,16},{32,40},{40,32},{48,56},{56,48},{64,72... | collective-permute-start | bytes 24584 | tf_op jit(solution)/shard_map/ppermute | solution.py:359
  6.8 2.0 %phases.5 = (f32[2,9,128,128]{3,2,1,0:T(8,128)S(1)}, f32[16,128]{1,0:T(8,128)S(1)}) custom-call(bf16[2,512,48]{2,1,0:T(8,128)(2,1)S(1)} %slice.47.refs_0_, f32[2,128,128]{2,1,0:T(8,128)S(1)} %broadcast_in_dim.30.refs_1_, f32[16,3]{1,0:T(8,128)S(1)} %pad.8.refs_2_, f32[8,512]{1,0:T(8,128)S(1)} %join.3.refs_3_.a_ref), custom_call_target="tpu_custom_call" | custom-call | flops 11534336 | bytes 1048576 | tf_op jit(solution)/shard_map/phases/pallas_call | solution.py:170
  8.9 1.3 %collective-permute-start.2 = (f32[8,1024]{1,0:T(8,128)S(1)}, f32[8,1024]{1,0:T(8,128)S(1)}, u32[]{:S(2)}, u32[]{:S(2)}) collective-permute-start(f32[8,1024]{1,0:T(8,128)S(1)} %join.4.refs_3_.a_ref), channel_id=1, source_target_pairs={{0,64},{8,72},{16,80},{24,88},{32,96},{40,104},{48,112},{56,120},{... | collective-permute-start | bytes 98312 | tf_op jit(solution)/shard_map/ppermute | solution.py:359
  10.1 1.8 %phases.6.refs_4_ = f32[2,9,128,128]{3,2,1,0:T(8,128)S(1)} custom-call(bf16[2,512,48]{2,1,0:T(8,128)(2,1)S(1)} %slice.47.refs_0_, f32[2,128,128]{2,1,0:T(8,128)S(1)} %broadcast_in_dim.30.refs_1_, f32[16,128]{1,0:T(8,128)S(1)} %get-tuple-element.23.refs_2_, f32[8,1024]{1,0:T(8,128)S(1)} %join.4.refs_3_.a_ref, f32[2,9,128,128]{3,2,1,0:T(8,128)S(1)} %get-tuple-element.26.refs_4_), custom_call_target="tpu_custom_call" | custom-call | flops 11534336 | bytes 1048576 | tf_op jit(solution)/shard_map/phases/pallas_call | solution.py:170
  12.0 3.7 %phases.7 = f32[2,16,128]{2,1,0:T(8,128)S(1)} custom-call(bf16[2,512,48]{2,1,0:T(8,128)(2,1)S(1)} %slice.47.refs_0_, f32[2,128,128]{2,1,0:T(8,128)S(1)} %broadcast_in_dim.30.refs_1_, f32[16,128]{1,0:T(8,128)S(1)} %get-tuple-element.23.refs_2_, f32[8,2048]{1,0:T(8,128)S(1)} %join.5.refs_3_, f32[2,9,128,128]{3,2,1,0:T(8,128)S(1)} %phases.6.refs_4_), custom_call_target="tpu_custom_call" | custom-call | flops 23068672 | bytes 1048576 | tf_op jit(solution)/shard_map/phases/pallas_call | solution.py:170
  15.7 2.9 %collective-permute-start.3 = (f32[2,16,128]{2,1,0:T(8,128)S(1)}, f32[2,16,128]{2,1,0:T(8,128)S(1)}, u32[]{:S(2)}, u32[]{:S(2)}) collective-permute-start(f32[2,16,128]{2,1,0:T(8,128)S(1)} %phases.7), channel_id=1, source_target_pairs={{0,128},{8,136},{16,144},{24,152},{32,160},{40,168},{48,176},{56,1... | collective-permute-start | bytes 49160 | tf_op jit(solution)/shard_map/ppermute | solution.py:359
  18.9 4.1 %phases.8 = f32[1,16,128]{2,1,0:T(8,128)S(1)} custom-call(bf16[1,512,48]{2,1,0:T(8,128)(2,1)S(1)} %get-tuple-element.36.refs_0_, f32[1,128,128]{2,1,0:T(8,128)S(1)} %broadcast_in_dim.31.refs_1_, f32[16,128]{1,0:T(8,128)S(1)} %get-tuple-element.23.refs_2_, f32[8,2048]{1,0:T(8,128)S(1)} %join.5.refs_3_), custom_call_target="tpu_custom_call" | custom-call | flops 23068672 | bytes 1048576 | tf_op jit(solution)/shard_map/phases/pallas_call | solution.py:170
  23.1 3.1 %collective-permute-start.4 = (f32[1,16,128]{2,1,0:T(8,128)S(1)}, f32[1,16,128]{2,1,0:T(8,128)S(1)}, u32[]{:S(2)}, u32[]{:S(2)}) collective-permute-start(f32[1,16,128]{2,1,0:T(8,128)S(1)} %slice_add_fusion), channel_id=1, source_target_pairs={{0,32},{8,40},{16,48},{24,56},{32,0},{40,8},{48,16},{56,24},{64,96... | collective-permute-start | bytes 24584 | tf_op jit(solution)/shard_map/ppermute | solution.py:359
  26.2 4.1 %phases.9.own_ref = f32[1,16,128]{2,1,0:T(8,128)S(1)} custom-call(bf16[1,512,48]{2,1,0:T(8,128)(2,1)S(1)} %get-tuple-element.35.refs_0_, f32[1,128,128]{2,1,0:T(8,128)S(1)} %broadcast_in_dim.32.refs_1_, f32[16,128]{1,0:T(8,128)S(1)} %get-tuple-element.23.refs_2_, f32[8,2048]{1,0:T(8,128)S(1)} %join.5.refs_3_), custom_call_target="tpu_custom_call" | custom-call | flops 23068672 | bytes 1048576 | tf_op jit(solution)/shard_map/phases/pallas_call | solution.py:170
  30.6 17.5 %all_to_all.11 = f32[32,1,1408]{2,1,0:T(1,128)S(1)} all-to-all(f32[32,1,1408]{2,1,0:T(1,128)S(1)} %copy.43), channel_id=1, replica_groups={{0,16,32,48,4,20,36,52,1,17,33,49,5,21,37,53,2,18,34,50,6,22,38,54,3,19..., dimensions={0} | all-to-all | bytes 360448 | tf_op jit(solution)/shard_map/all_to_all | solution.py:439
  48.1 0.7 collective-permute-start.7
  48.8 1.4 %collective-permute-start.6 = (f32[32,1408]{1,0:T(8,128)S(1)}, f32[32,1408]{1,0:T(8,128)S(1)}, u32[]{:S(2)}, u32[]{:S(2)}) collective-permute-start(f32[32,1408]{1,0:T(8,128)S(1)} %bitcast.40), channel_id=1, source_target_pairs={{0,128},{8,136},{16,144},{24,152},{32,160},{40,168},{48,176},{56,1... | collective-permute-start | bytes 540680 | tf_op jit(solution)/shard_map/ppermute | solution.py:359
  50.2 1.2 %collective-permute-start.5 = (f32[32,1408]{1,0:T(8,128)S(1)}, f32[32,1408]{1,0:T(8,128)S(1)}, u32[]{:S(2)}, u32[]{:S(2)}) collective-permute-start(f32[32,1408]{1,0:T(8,128)S(1)} %bitcast.41), channel_id=1, source_target_pairs={{0,64},{8,72},{16,80},{24,88},{32,96},{40,104},{48,112},{56,120},{... | collective-permute-start | bytes 540680 | tf_op jit(solution)/shard_map/ppermute | solution.py:359
  51.4 4.5 %collective-permute-start.8 = (f32[32,1408]{1,0:T(8,128)S(1)}, f32[32,1408]{1,0:T(8,128)S(1)}, u32[]{:S(2)}, u32[]{:S(2)}) collective-permute-start(f32[32,1408]{1,0:T(8,128)S(1)} %bitcast.42), channel_id=1, source_target_pairs={{0,8},{8,0},{16,24},{24,16},{32,40},{40,32},{48,56},{56,48},{64,72... | collective-permute-start | bytes 540680 | tf_op jit(solution)/shard_map/ppermute | solution.py:359
  55.9 0.8 %scatter.8.refs_0_ = f32[128,32,128]{2,1,0:T(8,128)S(1)} custom-call(s32[4,128]{1,0:T(4,128)S(1)} %broadcast_in_dim.26.own_ref, f32[32,1408]{1,0:T(8,128)S(1)} %bitcast.43), custom_call_target="tpu_custom_call" | custom-call | flops 536870912 | bytes 1048576 | tf_op jit(solution)/shard_map/scatter/pallas_call | solution.py:259
  56.7 3.8 %collective-permute-start.11 = (f32[32,1408]{1,0:T(8,128)S(1)}, f32[32,1408]{1,0:T(8,128)S(1)}, u32[]{:S(2)}, u32[]{:S(2)}) collective-permute-start(f32[32,1408]{1,0:T(8,128)S(1)} %collective-permute-done.7.p_ref), channel_id=1, source_target_pairs={{0,8},{8,0},{16,24},{24,16},{32,40},{40,32},{48,56},{56,48},{64,72... | collective-permute-start | bytes 540680 | tf_op jit(solution)/shard_map/ppermute | solution.py:359
  60.5 0.8 %collective-permute-start.9 = (f32[32,1408]{1,0:T(8,128)S(1)}, f32[32,1408]{1,0:T(8,128)S(1)}, u32[]{:S(2)}, u32[]{:S(2)}) collective-permute-start(f32[32,1408]{1,0:T(8,128)S(1)} %collective-permute-done.5.p_ref), channel_id=1, source_target_pairs={{0,8},{8,0},{16,24},{24,16},{32,40},{40,32},{48,56},{56,48},{64,72... | collective-permute-start | bytes 540680 | tf_op jit(solution)/shard_map/ppermute | solution.py:359
  61.3 0.7 %scatter.9.refs_1_ = f32[128,32,128]{2,1,0:T(8,128)S(1)} custom-call(s32[4,128]{1,0:T(4,128)S(1)} %broadcast_in_dim.26.own_ref, f32[32,1408]{1,0:T(8,128)S(1)} %collective-permute-done.5.p_ref), custom_call_target="tpu_custom_call" | custom-call | flops 536870912 | bytes 1048576 | tf_op jit(solution)/shard_map/scatter/pallas_call | solution.py:259
  62.1 0.8 %scatter.10.refs_2_ = f32[128,32,128]{2,1,0:T(8,128)S(1)} custom-call(s32[4,128]{1,0:T(4,128)S(1)} %broadcast_in_dim.26.own_ref, f32[32,1408]{1,0:T(8,128)S(1)} %collective-permute-done.6.p_ref), custom_call_target="tpu_custom_call" | custom-call | flops 536870912 | bytes 1048576 | tf_op jit(solution)/shard_map/scatter/pallas_call | solution.py:259
  62.8 0.8 %scatter.11.refs_3_ = f32[128,32,128]{2,1,0:T(8,128)S(1)} custom-call(s32[4,128]{1,0:T(4,128)S(1)} %broadcast_in_dim.26.own_ref, f32[32,1408]{1,0:T(8,128)S(1)} %collective-permute-done.7.p_ref), custom_call_target="tpu_custom_call" | custom-call | flops 536870912 | bytes 1048576 | tf_op jit(solution)/shard_map/scatter/pallas_call | solution.py:259
  63.6 0.7 %scatter.12.refs_4_ = f32[128,32,128]{2,1,0:T(8,128)S(1)} custom-call(s32[4,128]{1,0:T(4,128)S(1)} %broadcast_in_dim.26.own_ref, f32[32,1408]{1,0:T(8,128)S(1)} %collective-permute-done.8.p_ref), custom_call_target="tpu_custom_call" | custom-call | flops 536870912 | bytes 1048576 | tf_op jit(solution)/shard_map/scatter/pallas_call | solution.py:259
  65.1 0.7 scatter.14.refs_6_
  66.6 7.5 %transform.1 = f32[4,32,8,256]{3,2,1,0:T(8,128)} custom-call(s32[4,128]{1,0:T(4,128)S(1)} %broadcast_in_dim.26.own_ref, f32[128,32,128]{2,1,0:T(8,128)S(1)} %scatter.8.refs_0_, f32[128,32,128]{2,1,0:T(8,128)S(1)} %scatter.9.refs_1_, f32[128,32,128]{2,1,0:T(8,128)S(1)} %scatter.10.refs_2_, f32[128,32,128]{2,1,0:T(8,128)S(1)} %scatter.11.refs_3_, ...), custom_call_target="tpu_custom_call" | custom-call | tf_op jit(solution)/shard_map/transform/pallas_call | solution.py:342
  (62 shorter events, 4.8 us)
Async XLA Ops:
  0.9 5.3 %collective-permute-start = (f32[8,256]{1,0:T(8,128)S(1)}, f32[8,256]{1,0:T(8,128)S(1)}, u32[]{:S(2)}, u32[]{:S(2)}) collective-permute-start(f32[8,256]{1,0:T(8,128)S(1)} %maximum_maximum_fusion.a_ref), channel_id=1, source_target_pairs={{0,8},{8,0},{16,24},{24,16},{32,40},{40,32},{48,56},{56,48},{64,72... | collective-permute-start | bytes 24584 | tf_op jit(solution)/shard_map/ppermute | solution.py:359
  5.3 0.7 copy-start.2
  6.2 2.6 %collective-permute-start.1 = (f32[8,512]{1,0:T(8,128)S(1)}, f32[8,512]{1,0:T(8,128)S(1)}, u32[]{:S(2)}, u32[]{:S(2)}) collective-permute-start(f32[8,512]{1,0:T(8,128)S(1)} %join.3.refs_3_.a_ref), channel_id=1, source_target_pairs={{0,16},{8,24},{16,0},{24,8},{32,48},{40,56},{48,32},{56,40},{64,80... | collective-permute-start | bytes 49160 | tf_op jit(solution)/shard_map/ppermute | solution.py:359
  8.9 3.1 %collective-permute-start.2 = (f32[8,1024]{1,0:T(8,128)S(1)}, f32[8,1024]{1,0:T(8,128)S(1)}, u32[]{:S(2)}, u32[]{:S(2)}) collective-permute-start(f32[8,1024]{1,0:T(8,128)S(1)} %join.4.refs_3_.a_ref), channel_id=1, source_target_pairs={{0,64},{8,72},{16,80},{24,88},{32,96},{40,104},{48,112},{56,120},{... | collective-permute-start | bytes 98312 | tf_op jit(solution)/shard_map/ppermute | solution.py:359
  12.0 18.4 %copy-start.1 = (f32[2,1,128]{2,1,0:T(1,128)S(1)}, f32[2,1,128]{2,1,0:T(1,128)}, u32[]{:S(2)}) copy-start(f32[2,1,128]{2,1,0:T(1,128)} %param.12) | copy-start | bytes 3076
  15.7 7.3 %collective-permute-start.3 = (f32[2,16,128]{2,1,0:T(8,128)S(1)}, f32[2,16,128]{2,1,0:T(8,128)S(1)}, u32[]{:S(2)}, u32[]{:S(2)}) collective-permute-start(f32[2,16,128]{2,1,0:T(8,128)S(1)} %phases.7), channel_id=1, source_target_pairs={{0,128},{8,136},{16,144},{24,152},{32,160},{40,168},{48,176},{56,1... | collective-permute-start | bytes 49160 | tf_op jit(solution)/shard_map/ppermute | solution.py:359
  23.1 7.3 %collective-permute-start.4 = (f32[1,16,128]{2,1,0:T(8,128)S(1)}, f32[1,16,128]{2,1,0:T(8,128)S(1)}, u32[]{:S(2)}, u32[]{:S(2)}) collective-permute-start(f32[1,16,128]{2,1,0:T(8,128)S(1)} %slice_add_fusion), channel_id=1, source_target_pairs={{0,32},{8,40},{16,48},{24,56},{32,0},{40,8},{48,16},{56,24},{64,96... | collective-permute-start | bytes 24584 | tf_op jit(solution)/shard_map/ppermute | solution.py:359
  48.1 8.6 %collective-permute-start.7 = (f32[32,1408]{1,0:T(8,128)S(1)}, f32[32,1408]{1,0:T(8,128)S(1)}, u32[]{:S(2)}, u32[]{:S(2)}) collective-permute-start(f32[32,1408]{1,0:T(8,128)S(1)} %bitcast.39), channel_id=1, source_target_pairs={{0,192},{8,200},{16,208},{24,216},{32,224},{40,232},{48,240},{56,2... | collective-permute-start | bytes 540680 | tf_op jit(solution)/shard_map/ppermute | solution.py:359
  48.8 11.7 %collective-permute-start.6 = (f32[32,1408]{1,0:T(8,128)S(1)}, f32[32,1408]{1,0:T(8,128)S(1)}, u32[]{:S(2)}, u32[]{:S(2)}) collective-permute-start(f32[32,1408]{1,0:T(8,128)S(1)} %bitcast.40), channel_id=1, source_target_pairs={{0,128},{8,136},{16,144},{24,152},{32,160},{40,168},{48,176},{56,1... | collective-permute-start | bytes 540680 | tf_op jit(solution)/shard_map/ppermute | solution.py:359
  50.2 10.2 %collective-permute-start.5 = (f32[32,1408]{1,0:T(8,128)S(1)}, f32[32,1408]{1,0:T(8,128)S(1)}, u32[]{:S(2)}, u32[]{:S(2)}) collective-permute-start(f32[32,1408]{1,0:T(8,128)S(1)} %bitcast.41), channel_id=1, source_target_pairs={{0,64},{8,72},{16,80},{24,88},{32,96},{40,104},{48,112},{56,120},{... | collective-permute-start | bytes 540680 | tf_op jit(solution)/shard_map/ppermute | solution.py:359
  51.4 12.2 %collective-permute-start.8 = (f32[32,1408]{1,0:T(8,128)S(1)}, f32[32,1408]{1,0:T(8,128)S(1)}, u32[]{:S(2)}, u32[]{:S(2)}) collective-permute-start(f32[32,1408]{1,0:T(8,128)S(1)} %bitcast.42), channel_id=1, source_target_pairs={{0,8},{8,0},{16,24},{24,16},{32,40},{40,32},{48,56},{56,48},{64,72... | collective-permute-start | bytes 540680 | tf_op jit(solution)/shard_map/ppermute | solution.py:359
  56.7 9.2 %collective-permute-start.11 = (f32[32,1408]{1,0:T(8,128)S(1)}, f32[32,1408]{1,0:T(8,128)S(1)}, u32[]{:S(2)}, u32[]{:S(2)}) collective-permute-start(f32[32,1408]{1,0:T(8,128)S(1)} %collective-permute-done.7.p_ref), channel_id=1, source_target_pairs={{0,8},{8,0},{16,24},{24,16},{32,40},{40,32},{48,56},{56,48},{64,72... | collective-permute-start | bytes 540680 | tf_op jit(solution)/shard_map/ppermute | solution.py:359
  60.5 4.7 %collective-permute-start.10 = (f32[32,1408]{1,0:T(8,128)S(1)}, f32[32,1408]{1,0:T(8,128)S(1)}, u32[]{:S(2)}, u32[]{:S(2)}) collective-permute-start(f32[32,1408]{1,0:T(8,128)S(1)} %collective-permute-done.6.p_ref), channel_id=1, source_target_pairs={{0,8},{8,0},{16,24},{24,16},{32,40},{40,32},{48,56},{56,48},{64,72... | collective-permute-start | bytes 540680 | tf_op jit(solution)/shard_map/ppermute | solution.py:359
  60.5 3.9 %collective-permute-start.9 = (f32[32,1408]{1,0:T(8,128)S(1)}, f32[32,1408]{1,0:T(8,128)S(1)}, u32[]{:S(2)}, u32[]{:S(2)}) collective-permute-start(f32[32,1408]{1,0:T(8,128)S(1)} %collective-permute-done.5.p_ref), channel_id=1, source_target_pairs={{0,8},{8,0},{16,24},{24,16},{32,40},{40,32},{48,56},{56,48},{64,72... | collective-permute-start | bytes 540680 | tf_op jit(solution)/shard_map/ppermute | solution.py:359
  65.1 1.5 %copy-start = (bf16[2,512,256]{2,1,0:T(8,128)(2,1)S(1)}, bf16[2,512,256]{2,1,0:T(8,128)(2,1)}, u32[]{:S(2)}) copy-start(bf16[2,512,256]{2,1,0:T(8,128)(2,1)} %constant.59.clone.refs_8_) | copy-start | bytes 1572868
